TPU v7x, 512 devices: a whole 4x8x8 slice. The times are simulated.
512 devices in a mesh: row: 32 (over x, z), col: 16 (over y, core).
Axes of the slice: x: 4, y: 8, z: 8, core: 2. Of those that a mesh axis runs over, the one named last changes fastest.
Arguments:
- features: bfloat16 [1024, 512, 256], P('row', 'col'), may hold values from -6 to 6
- tower_weight: bfloat16 [2, 3, 3, 256, 256], replicated, may hold values from -0.1875 to 0.1875
- tower_bias: float32 [2, 256], replicated, may hold values from -3 to 3
- boxes: int32 [512, 4], P('row'), may hold values from 0 to 1023, as said below
- owner_slot: int32 [32, 16], P('row'), may hold values from 0 to 15, each once within a row
- mask_weight: bfloat16 [1, 3, 3, 256, 256], replicated, may hold values from -0.1875 to 0.1875
- mask_bias: float32 [1, 256], replicated, may hold values from -3 to 3
- deconv_weight: bfloat16 [2, 2, 256, 256], replicated, may hold values from -0.375 to 0.375
- deconv_bias: float32 [256], replicated, may hold values from -3 to 3
Outputs:
- tower: bfloat16 [1024, 512, 256], P('row', 'col')
- masks: bfloat16 [512, 28, 28, 256], P(('row', 'col'))
Inputs may be any that keep to these rules, and one draw needn't show every extreme that they name: `boxes`: row k is (top, left, height, width) of region k in feature pixels: the box lies inside the image, height 1 to 32, width 1 to 64, and its top row is among rows 32 * g to 32 * g + 31 with g = k // 16. The first region of every group has height 32 and width 64. Region 0 has top 0 and left 0; the last region is the single pixel at the image's bottom right corner.
All inputs are finite; a program needn't handle non-finite values.
Results may differ from a plain program's by a relative error of at most 0.0066.
Values may be sent and summed in bfloat16 or wider, within the bound.
No kernel may reach another device: no remote copies, remote signals or barrier semaphores. Data moves between devices by JAX's collectives and lax.ppermute only.
A program may use at most 64 MiB of HBM per device.

v0:
```python
import jax
import jax.numpy as jnp
from jax import lax
from jax.sharding import PartitionSpec as P

POOL = 14


def padded_2(value, sides, width):
    for axis, dim in sides:
        peers, length = (lax.axis_size(axis), value.shape[dim])
        up = [(i, (i + 1) % peers) for i in range(peers - 1)]
        down = [(j, i) for i, j in up]
        last = lax.slice_in_dim(value, length - width, length, axis=dim)
        leading = lax.slice_in_dim(value, 0, width, axis=dim)
        before = lax.ppermute(last, axis, up)
        after = lax.ppermute(leading, axis, down)
        value = jnp.concatenate([before, value, after], axis=dim)
    return value


def from_behind(block, axis, distance):
    devices = range(lax.axis_size(axis))
    route = [(i - distance, i) for i in devices if i - distance in devices]
    return lax.ppermute(block, axis, route)


def convolve(padded, kernel, bias_row):
    rows_out = padded.shape[-3] - 2
    cols_out = padded.shape[-2] - 2
    leading = padded.shape[:-3]
    channels = kernel.shape[-1]
    running = None
    for row_step in range(3):
        for col_step in range(3):
            window = padded[..., row_step : row_step + rows_out, col_step : col_step + cols_out, :]
            window = window.reshape(-1, padded.shape[-1])
            product = jnp.dot(
                window, kernel[row_step, col_step], preferred_element_type=jnp.float32
            )
            running = product if running is None else running + product
    running = jnp.maximum(running + bias_row, 0.0)
    return running.reshape(leading + (rows_out, cols_out, channels)).astype(jnp.bfloat16)


def bilinear_ramp(lower, extent, coords):
    lower_f = lower.astype(jnp.float32)[:, None, None]
    extent_f = extent.astype(jnp.float32)[:, None, None]
    bins = jnp.arange(POOL).astype(jnp.float32)[None, :, None]
    centre = lower_f + (bins + 0.5) * extent_f / POOL - 0.5
    centre = jnp.clip(centre, lower_f, lower_f + extent_f - 1.0)
    places = coords.astype(jnp.float32)[None, None, :]
    return jnp.maximum(1.0 - jnp.abs(places - centre), 0.0).astype(jnp.bfloat16)


def project(down_f, across, band_part):
    partial_sum = jnp.einsum("rqx,yxc->ryqc", across, band_part, preferred_element_type=jnp.float32)
    return jnp.einsum("rpy,ryqc->rpqc", down_f, partial_sum, precision=lax.Precision.HIGHEST)


def mask_head(pooled, mask_weight, mask_bias, deconv_weight, deconv_bias):
    hidden = pooled
    padded = jnp.pad(hidden, ((0, 0), (1, 1), (1, 1), (0, 0)))
    hidden = convolve(padded, mask_weight[0], mask_bias[0])
    lifted = jnp.einsum(
        "rabc,uvcd->raubvd", hidden, deconv_weight, preferred_element_type=jnp.float32
    )
    lifted = jnp.maximum(lifted + deconv_bias, 0.0)
    return lifted.reshape(hidden.shape[0], 2 * POOL, 2 * POOL, -1).astype(jnp.bfloat16)


def per_device(
    features,
    tower_weight,
    tower_bias,
    boxes,
    owner_slot,
    mask_weight,
    mask_bias,
    deconv_weight,
    deconv_bias,
):
    tile_rows, tile_cols, channels = features.shape
    current = features
    for layer_index in range(tower_weight.shape[0]):
        padded = padded_2(current, (("row", 0), ("col", 1)), 1)
        current = convolve(padded, tower_weight[layer_index], tower_bias[layer_index])
    below_tile = from_behind(current, "row", -1)
    band_tile = jnp.concatenate([current, below_tile], axis=0)
    band_first = lax.axis_index("row") * tile_rows
    band_coords = band_first + jnp.arange(2 * tile_rows, dtype=jnp.int32)
    group_size = boxes.shape[0]
    slot_of = owner_slot[0]
    picked = (slot_of[None, :] == jnp.arange(group_size, dtype=jnp.int32)[:, None]).astype(
        jnp.int32
    )
    ordered = jnp.sum(picked[:, :, None] * boxes[None, :, :], axis=1)
    per_owner = group_size // lax.axis_size("col")
    down_all = bilinear_ramp(ordered[:, 0], ordered[:, 2], band_coords).astype(jnp.float32)
    first_owned = lax.axis_index("col") * per_owner
    owned_boxes = lax.dynamic_slice_in_dim(ordered, first_owned, per_owner, 0)
    owned_down = lax.dynamic_slice_in_dim(down_all, first_owned, per_owner, 0)
    piece = lax.all_gather(band_tile, "col", axis=1, tiled=True)
    columns = jnp.arange(piece.shape[1], dtype=jnp.int32)
    across = bilinear_ramp(owned_boxes[:, 1], owned_boxes[:, 3], columns)
    pooled = project(owned_down, across, piece)
    masks = mask_head(
        pooled.astype(jnp.bfloat16), mask_weight, mask_bias, deconv_weight, deconv_bias
    )
    return (current, masks)


def solution(mesh):
    placed = (P("row", "col", None), P(), P(), P("row", None), P("row", None), P(), P(), P(), P())
    return jax.shard_map(
        per_device,
        mesh=mesh,
        in_specs=placed,
        out_specs=(P("row", "col", None), P(("row", "col"), None, None, None)),
        check_vma=False,
    )
```

profile of v0, /device:TPU:6, one launch (start us, length us, event | category | flops | bytes accessed | tf_op | source)
XLA Modules:
  0.0 195.9 jit_solution(13642533181125782840)
XLA Ops:
  7.2 0.8 fusion.49
  8.0 11.2 %collective-permute-start.1 = (bf16[1,32,256]{2,1,0:T(8,128)(2,1)S(1)}, bf16[1,32,256]{2,1,0:T(8,128)(2,1)S(1)}, u32[]{:S(2)}, u32[]{:S(2)}) collective-permute-start(bf16[1,32,256]{2,1,0:T(8,128)(2,1)S(1)} %get-tuple-element.32), channel_id=1, source_target_pairs={{16,0},{32,16},{48,32},{64,48},{80,64},{96,80},{112,96},{128,112},... | collective-permute-start | bytes 49160 | tf_op jit(solution)/shard_map/ppermute | solution.py:17
  19.2 2.1 %collective-permute-start = (bf16[1,32,256]{2,1,0:T(8,128)(2,1)S(1)}, bf16[1,32,256]{2,1,0:T(8,128)(2,1)S(1)}, u32[]{:S(2)}, u32[]{:S(2)}) collective-permute-start(bf16[1,32,256]{2,1,0:T(8,128)(2,1)S(1)} %get-tuple-element.33), channel_id=1, source_target_pairs={{0,16},{16,32},{32,48},{48,64},{64,80},{80,96},{96,112},{112,128},... | collective-permute-start | bytes 49160 | tf_op jit(solution)/shard_map/ppermute | solution.py:16
  21.3 1.8 slice_bitcast_fusion
  23.1 4.0 %collective-permute-done = bf16[1,32,256]{2,1,0:T(8,128)(2,1)S(1)} collective-permute-done((bf16[1,32,256]{2,1,0:T(8,128)(2,1)S(1)}, bf16[1,32,256]{2,1,0:T(8,128)(2,1)S(1)}, u32[]{:S(2)}, u32[]{:S(2)}) %collective-permute-start) | collective-permute-done | bytes 16416 | tf_op jit(solution)/shard_map/ppermute | solution.py:16
  27.4 1.3 collective-permute-start.2
  28.7 1.3 collective-permute-start.3
  30.3 0.3 fusion.27
  30.6 3.0 %collective-permute-done.3 = bf16[34,1,256]{2,1,0:T(2,128)(2,1)S(1)} collective-permute-done((bf16[34,1,256]{2,1,0:T(2,128)(2,1)S(1)}, bf16[34,1,256]{2,1,0:T(2,128)(2,1)S(1)}, u32[]{:S(2)}, u32[]{:S(2)}) %collective-permute-start.3) | collective-permute-done | bytes 17440 | tf_op jit(solution)/shard_map/ppermute | solution.py:17
  33.6 0.9 pad_maximum_fusion.6
  34.8 0.3 convolution_add_fusion.12
  36.2 0.4 fusion.8
  36.7 1.9 collective-permute-start.4
  38.6 6.0 %collective-permute-start.5 = (bf16[1,32,256]{2,1,0:T(8,128)(2,1)S(1)}, bf16[1,32,256]{2,1,0:T(8,128)(2,1)S(1)}, u32[]{:S(2)}, u32[]{:S(2)}) collective-permute-start(bf16[1,32,256]{2,1,0:T(8,128)(2,1)S(1)} %get-tuple-element.28), channel_id=1, source_target_pairs={{16,0},{32,16},{48,32},{64,48},{80,64},{96,80},{112,96},{128,112},... | collective-permute-start | bytes 49160 | tf_op jit(solution)/shard_map/ppermute | solution.py:17
  44.7 1.4 collective-permute-done.5
  46.1 3.4 %collective-permute-start.6 = (bf16[34,1,256]{2,1,0:T(2,128)(2,1)S(1)}, bf16[34,1,256]{2,1,0:T(2,128)(2,1)S(1)}, u32[]{:S(2)}, u32[]{:S(2)}) collective-permute-start(bf16[34,1,256]{2,1,0:T(2,128)(2,1)S(1)} %get-tuple-element.18), channel_id=1, source_target_pairs={{0,1},{1,2},{2,3},{3,4},{4,5},{5,6},{6,7},{7,8},{8,9},{9,10},{10,1... | collective-permute-start | bytes 52232 | tf_op jit(solution)/shard_map/ppermute | solution.py:16
  49.6 1.3 collective-permute-start.7
  51.2 2.1 %collective-permute-done.7 = bf16[34,1,256]{2,1,0:T(2,128)(2,1)S(1)} collective-permute-done((bf16[34,1,256]{2,1,0:T(2,128)(2,1)S(1)}, bf16[34,1,256]{2,1,0:T(2,128)(2,1)S(1)}, u32[]{:S(2)}, u32[]{:S(2)}) %collective-permute-start.7) | collective-permute-done | bytes 17440 | tf_op jit(solution)/shard_map/ppermute | solution.py:17
  53.3 0.4 maximum_maximum_fusion
  53.7 0.4 fusion.46
  54.2 0.3 convolution_add_fusion.6
  56.3 0.3 fusion.7
  56.6 6.6 %collective-permute-start.8 = (bf16[32,32,256]{2,1,0:T(8,128)(2,1)S(1)}, bf16[32,32,256]{2,1,0:T(8,128)(2,1)S(1)}, u32[]{:S(2)}, u32[]{:S(2)}) collective-permute-start(bf16[32,32,256]{2,1,0:T(8,128)(2,1)S(1)} %bitcast.202), channel_id=1, source_target_pairs={{16,0},{32,16},{48,32},{64,48},{80,64},{96,80},{112,96},{128,112},... | collective-permute-start | bytes 1572872 | tf_op jit(solution)/shard_map/ppermute | solution.py:25
  63.3 10.4 %collective-permute-done.8 = bf16[32,32,256]{2,1,0:T(8,128)(2,1)S(1)} collective-permute-done((bf16[32,32,256]{2,1,0:T(8,128)(2,1)S(1)}, bf16[32,32,256]{2,1,0:T(8,128)(2,1)S(1)}, u32[]{:S(2)}, u32[]{:S(2)}) %collective-permute-start.8) | collective-permute-done | bytes 524320 | tf_op jit(solution)/shard_map/ppermute | solution.py:25
  73.6 1.1 pad_maximum_fusion
  75.0 0.6 fusion.50
  77.0 97.9 %all-gather.2.cloned.1.call-done = bf16[64,512,256]{2,1,0:T(8,128)(2,1)} async-done(((bf16[64,32,256]{2,1,0:T(8,128)(2,1)}), bf16[64,512,256]{2,1,0:T(8,128)(2,1)}) %all-gather.2.cloned.1.call-update) | async-done | bytes 16777232 | tf_op jit(solution)/shard_map/all_gather | solution.py:103
  174.9 8.1 %convolution_bitcast_fusion = f32[64,14,256]{2,1,0:T(8,128)S(1)} fusion(bf16[64,512,256]{2,1,0:T(8,128)(2,1)} %all-gather.2.cloned.1.call-done, f32[14]{0:T(128)S(1)} %maximum_minimum_fusion.1, f32[512]{0:T(512)S(1)} %iota_convert_fusion), kind=kOutput, calls=%fused_computation | convolution fusion | flops 234916864 | bytes 17696824 | tf_op jit(solution)/shard_map/rqx,yxc->ryqc/dot_general | solution.py:57
  183.0 0.9 convolution_convert_fusion
  184.8 0.8 copy-done.3
  187.8 0.3 copy.35
  188.1 0.9 convert_element_type.147
  (85 shorter events, 7.3 us)
Async XLA Ops:
  7.2 180.3 %copy-start = (bf16[2,2,256,256]{3,2,1,0:T(8,128)(2,1)S(1)}, bf16[2,2,256,256]{3,2,1,0:T(8,128)(2,1)}, u32[]{:S(2)}) copy-start(bf16[2,2,256,256]{3,2,1,0:T(8,128)(2,1)} %param.16) | copy-start | bytes 1572868
  7.2 167.8 %all-gather.2.cloned.1.call-start = ((), (), s32[]{:S(2)}) async-start(), calls=%async_computation | async-start | bytes 17825792 | tf_op jit(solution)/shard_map/all_gather | solution.py:103
  8.0 19.1 %collective-permute-start.1 = (bf16[1,32,256]{2,1,0:T(8,128)(2,1)S(1)}, bf16[1,32,256]{2,1,0:T(8,128)(2,1)S(1)}, u32[]{:S(2)}, u32[]{:S(2)}) collective-permute-start(bf16[1,32,256]{2,1,0:T(8,128)(2,1)S(1)} %get-tuple-element.32), channel_id=1, source_target_pairs={{16,0},{32,16},{48,32},{64,48},{80,64},{96,80},{112,96},{128,112},... | collective-permute-start | bytes 49160 | tf_op jit(solution)/shard_map/ppermute | solution.py:17
  19.2 3.9 %copy-start.4 = (f32[2,256]{1,0:T(2,128)S(1)}, f32[2,256]{1,0:T(2,128)}, u32[]{:S(2)}) copy-start(f32[2,256]{1,0:T(2,128)} %param.11) | copy-start | bytes 6148
  19.2 7.9 %copy-start.1 = (bf16[32,32,256]{2,1,0:T(8,128)(2,1)S(1)}, bf16[32,32,256]{2,1,0:T(8,128)(2,1)}, u32[]{:S(2)}) copy-start(bf16[32,32,256]{2,1,0:T(8,128)(2,1)} %param.9) | copy-start | bytes 1572868
  19.2 7.9 %collective-permute-start = (bf16[1,32,256]{2,1,0:T(8,128)(2,1)S(1)}, bf16[1,32,256]{2,1,0:T(8,128)(2,1)S(1)}, u32[]{:S(2)}, u32[]{:S(2)}) collective-permute-start(bf16[1,32,256]{2,1,0:T(8,128)(2,1)S(1)} %get-tuple-element.33), channel_id=1, source_target_pairs={{0,16},{16,32},{32,48},{48,64},{64,80},{80,96},{96,112},{112,128},... | collective-permute-start | bytes 49160 | tf_op jit(solution)/shard_map/ppermute | solution.py:16
  27.4 3.2 %collective-permute-start.2 = (bf16[34,1,256]{2,1,0:T(2,128)(2,1)S(1)}, bf16[34,1,256]{2,1,0:T(2,128)(2,1)S(1)}, u32[]{:S(2)}, u32[]{:S(2)}) collective-permute-start(bf16[34,1,256]{2,1,0:T(2,128)(2,1)S(1)} %get-tuple-element.23), channel_id=1, source_target_pairs={{0,1},{1,2},{2,3},{3,4},{4,5},{5,6},{6,7},{7,8},{8,9},{9,10},{10,1... | collective-permute-start | bytes 52232 | tf_op jit(solution)/shard_map/ppermute | solution.py:16
  28.7 4.9 %collective-permute-start.3 = (bf16[34,1,256]{2,1,0:T(2,128)(2,1)S(1)}, bf16[34,1,256]{2,1,0:T(2,128)(2,1)S(1)}, u32[]{:S(2)}, u32[]{:S(2)}) collective-permute-start(bf16[34,1,256]{2,1,0:T(2,128)(2,1)S(1)} %get-tuple-element.24), channel_id=1, source_target_pairs={{1,0},{2,1},{3,2},{4,3},{5,4},{6,5},{7,6},{8,7},{9,8},{10,9},{11,1... | collective-permute-start | bytes 52232 | tf_op jit(solution)/shard_map/ppermute | solution.py:17
  36.7 8.0 %collective-permute-start.4 = (bf16[1,32,256]{2,1,0:T(8,128)(2,1)S(1)}, bf16[1,32,256]{2,1,0:T(8,128)(2,1)S(1)}, u32[]{:S(2)}, u32[]{:S(2)}) collective-permute-start(bf16[1,32,256]{2,1,0:T(8,128)(2,1)S(1)} %get-tuple-element.27), channel_id=1, source_target_pairs={{0,16},{16,32},{32,48},{48,64},{64,80},{80,96},{96,112},{112,128},... | collective-permute-start | bytes 49160 | tf_op jit(solution)/shard_map/ppermute | solution.py:16
  38.6 7.5 %collective-permute-start.5 = (bf16[1,32,256]{2,1,0:T(8,128)(2,1)S(1)}, bf16[1,32,256]{2,1,0:T(8,128)(2,1)S(1)}, u32[]{:S(2)}, u32[]{:S(2)}) collective-permute-start(bf16[1,32,256]{2,1,0:T(8,128)(2,1)S(1)} %get-tuple-element.28), channel_id=1, source_target_pairs={{16,0},{32,16},{48,32},{64,48},{80,64},{96,80},{112,96},{128,112},... | collective-permute-start | bytes 49160 | tf_op jit(solution)/shard_map/ppermute | solution.py:17
  46.1 5.1 %collective-permute-start.6 = (bf16[34,1,256]{2,1,0:T(2,128)(2,1)S(1)}, bf16[34,1,256]{2,1,0:T(2,128)(2,1)S(1)}, u32[]{:S(2)}, u32[]{:S(2)}) collective-permute-start(bf16[34,1,256]{2,1,0:T(2,128)(2,1)S(1)} %get-tuple-element.18), channel_id=1, source_target_pairs={{0,1},{1,2},{2,3},{3,4},{4,5},{5,6},{6,7},{7,8},{8,9},{9,10},{10,1... | collective-permute-start | bytes 52232 | tf_op jit(solution)/shard_map/ppermute | solution.py:16
  49.6 3.8 %collective-permute-start.7 = (bf16[34,1,256]{2,1,0:T(2,128)(2,1)S(1)}, bf16[34,1,256]{2,1,0:T(2,128)(2,1)S(1)}, u32[]{:S(2)}, u32[]{:S(2)}) collective-permute-start(bf16[34,1,256]{2,1,0:T(2,128)(2,1)S(1)} %get-tuple-element.19), channel_id=1, source_target_pairs={{1,0},{2,1},{3,2},{4,3},{5,4},{6,5},{7,6},{8,7},{9,8},{10,9},{11,1... | collective-permute-start | bytes 52232 | tf_op jit(solution)/shard_map/ppermute | solution.py:17
  56.6 18.1 %copy-start.2 = (bf16[1024,256]{1,0:T(8,128)(2,1)}, bf16[1024,256]{1,0:T(8,128)(2,1)S(1)}, u32[]{:S(2)}) copy-start(bf16[1024,256]{1,0:T(8,128)(2,1)S(1)} %fusion.7) | copy-start | bytes 1572868
  56.6 18.1 %copy-start.8 = (s32[1,16]{1,0:T(1,128)S(1)}, s32[1,16]{1,0:T(1,128)}, u32[]{:S(2)}) copy-start(s32[1,16]{1,0:T(1,128)} %param.13) | copy-start | bytes 196
  56.6 18.1 %copy-start.5 = (s32[16,4]{0,1:T(4,128)S(1)}, s32[16,4]{0,1:T(4,128)}, u32[]{:S(2)}) copy-start(s32[16,4]{0,1:T(4,128)} %param.12) | copy-start | bytes 772
  56.6 17.0 %collective-permute-start.8 = (bf16[32,32,256]{2,1,0:T(8,128)(2,1)S(1)}, bf16[32,32,256]{2,1,0:T(8,128)(2,1)S(1)}, u32[]{:S(2)}, u32[]{:S(2)}) collective-permute-start(bf16[32,32,256]{2,1,0:T(8,128)(2,1)S(1)} %bitcast.202), channel_id=1, source_target_pairs={{16,0},{32,16},{48,32},{64,48},{80,64},{96,80},{112,96},{128,112},... | collective-permute-start | bytes 1572872 | tf_op jit(solution)/shard_map/ppermute | solution.py:25
  184.4 1.3 copy-start.3
  186.4 0.8 copy-start.6
  186.8 0.7 copy-start.7
Sparse Core Ops, SparseCore 0:
  74.8 100.0 all-gather.1
where the time goes:
time: 198 us; the launch traced here: 196 us
  waiting for transfers between devices  119 us (60%)
  starting transfers between devices  35.2 us (18%)
  matrix products  16.4 us (8%)
  between operations  16 us (8%)
  local copies, waits for them, and re-layouts  6.62 us (3%)
  other arithmetic  2.9 us (1%)
    all_gather x1, waiting for transfers between devices, per_device(): piece = lax.all_gather(band_tile, 'col', axis=1, tiled=True)  97.9 us
    ppermute x4, starting transfers between devices, padded_2(): after = lax.ppermute(leading, axis, down)  19.8 us
    ppermute x1, waiting for transfers between devices, from_behind(): return lax.ppermute(block, axis, route)  10.4 us
    ppermute x4, starting transfers between devices, padded_2(): before = lax.ppermute(last, axis, up)  8.69 us
    dot_general x1, matrix products, project(): jnp.einsum('rqx,yxc->ryqc', across, band_part, preferred_element_type=jnp...  8.1 us
    dot_general x27, matrix products, convolve(): jnp.dot(window, kernel[row_step, col_step], preferred_element_type=jnp.fl...  7.1 us
    ppermute x1, starting transfers between devices, from_behind(): return lax.ppermute(block, axis, route)  6.63 us
    ppermute x4, waiting for transfers between devices, padded_2(): after = lax.ppermute(leading, axis, down)  6.49 us
  transfers between devices with their start and end apart: 10, of which 6 were waited for; matrix products, arithmetic and copies ran while one was open for 2% of the time, Pallas kernels for 0%

commit v1 on v0

v1 whole, which is shorter than its diff:
```python
import jax
import jax.numpy as jnp
from jax import lax
from jax.experimental import pallas as pl
from jax.experimental.pallas import tpu as pltpu
from jax.sharding import PartitionSpec as P

POOL = 14
SIDE = 16
LANES = 128
FIRST = 11
SECOND = 8
F32 = jnp.float32
BF16 = jnp.bfloat16


def shift(value, axis, step):
    devices = range(lax.axis_size(axis))
    return lax.ppermute(value, axis, [(i, i + step) for i in devices if i + step in devices])


def conv_valid(padded, kernel, bias):
    out = lax.conv_general_dilated(
        padded[None], kernel, (1, 1), "VALID",
        dimension_numbers=("NHWC", "HWIO", "NHWC"), preferred_element_type=F32,
    )[0]
    return jnp.maximum(out + bias, 0.0).astype(BF16)


def exchange(features, weight, bias):
    rows, cols, channels = features.shape
    row, col = lax.axis_index("row"), lax.axis_index("col")
    last_row, last_col = lax.axis_size("row") - 1, lax.axis_size("col") - 1
    below = shift(features, "row", -1)
    left = shift(features[:, cols - 2 :], "col", 1)
    right = shift(features[:, :2], "col", -1)
    own = jnp.concatenate([left, features, right], axis=1)
    own_sides = jnp.concatenate([left, features[:, :1], features[:, cols - 1 :], right], axis=1)
    sides = shift(own_sides, "row", -1)
    above = shift(own[rows - 2 :], "row", 1)
    after = shift(own[:1], "row", -2)

    def ends(strip):
        return jnp.concatenate([strip[:, :3], strip[:, cols + 1 :]], axis=1)

    columns = jnp.concatenate([ends(above), own_sides, sides, ends(after)], axis=0)
    edge = jnp.pad(columns[:, 1:5:3].astype(F32), ((0, 1), (0, 0), (0, 0)))
    edge = edge.swapaxes(0, 1)[:, :, None]
    batch = columns.reshape(-1, 2, 3, channels).swapaxes(0, 1)
    inner = lax.conv_general_dilated(
        batch, weight[0], (1, 1), "VALID",
        dimension_numbers=("NHWC", "HWIO", "NHWC"), preferred_element_type=F32,
    )
    inner = jnp.maximum(inner + bias[0], 0.0).astype(BF16).astype(F32)
    kept = jnp.stack([col > 0, col < last_col])[:, None, None, None]
    inner = jnp.pad(jnp.where(kept, inner, 0.0), ((0, 0), (0, 1), (0, 0), (0, 0)))
    flags = jnp.stack([row == 0, row == last_row]).astype(jnp.int32)
    return below, above[:, 2 : cols + 2], after[:, 2 : cols + 2], edge, inner, flags


def sample(lower, extent):
    lower_f = lower.astype(F32)[:, None]
    extent_f = extent.astype(F32)[:, None]
    bins = jnp.arange(POOL).astype(F32)[None, :]
    centre = lower_f + (bins + 0.5) * extent_f / POOL - 0.5
    return jnp.clip(centre, lower_f, lower_f + extent_f - 1.0)


def spread(dst, start, value, edges, offset):
    count, width, channels = value.shape
    value = value.astype(F32)
    place = lax.broadcasted_iota(jnp.int32, value.shape, 1)
    here = pl.ds(offset, count)
    before = jnp.where(place == 0, edges[0, here], pltpu.roll(value, 1, 1))
    after = jnp.where(place == width - 1, edges[1, here], pltpu.roll(value, width - 1, 1))
    rows = pl.ds(start, count)
    dst[rows, :, 0:channels] = before.astype(BF16)
    dst[rows, :, channels : 2 * channels] = value.astype(BF16)
    dst[rows, :, 2 * channels : 3 * channels] = after.astype(BF16)


def taps(src, start, count, weight, bias):
    width, depth = src.shape[1:]
    parts = [src[pl.ds(start + d, count)].reshape(count * width, depth) for d in range(3)]
    out = jnp.dot(jnp.concatenate(parts, axis=1), weight, preferred_element_type=F32)
    out = jnp.maximum(out + bias, 0.0)
    return out.reshape(count, width, out.shape[-1])


def main_kernel(
    flags_ref, hit_ref, xa_ref, xb_ref, wa_ref, wb_ref,
    own_ref, below_ref, above_ref, after_ref, edge_ref, inner_ref,
    weight_ref, bias_ref, down_ref,
    tower_ref, mine_ref, other_ref,
    wide_ref, mid_ref, band_ref, pooled_ref, patch_ref,
):
    rows, width, channels = own_ref.shape
    half = mine_ref.shape[0]
    spread(wide_ref, 0, above_ref[...], edge_ref, 0)
    step = 8
    for part, base in ((own_ref, 2), (below_ref, 2 + rows)):
        def fill(i, carry):
            at = i * step
            spread(wide_ref, base + at, part[pl.ds(at, step)], edge_ref, base + at)
            return carry

        lax.fori_loop(0, rows // step, fill, 0)
    spread(wide_ref, 2 + 2 * rows, after_ref[...], edge_ref, 2 + 2 * rows)
    wide_ref[3 + 2 * rows] = jnp.zeros(wide_ref.shape[1:], BF16)

    def first(i, carry):
        at = i * FIRST
        out = taps(wide_ref, at, FIRST, weight_ref[0], bias_ref[0:1])
        spread(mid_ref, at, out.astype(BF16), inner_ref, at)
        return carry

    lax.fori_loop(0, (2 * rows + 2) // FIRST, first, 0)
    blank = jnp.zeros(mid_ref.shape[1:], BF16)

    @pl.when(flags_ref[0] > 0)
    def _():
        mid_ref[0] = blank

    @pl.when(flags_ref[1] > 0)
    def _():
        mid_ref[rows + 1] = blank
    mid_ref[2 * rows + 1] = blank

    def second(i, carry):
        at = i * SECOND
        out = taps(mid_ref, at, SECOND, weight_ref[1], bias_ref[1:2])

        @pl.when(at < rows)
        def _():
            tower_ref[pl.ds(at, SECOND)] = out.astype(BF16)

        for k in range(SECOND):
            line = out[k].astype(BF16).astype(F32)
            for h in range(channels // LANES):
                piece = line[:, h * LANES : (h + 1) * LANES]
                band_ref[h, pl.ds(at + k, width, stride=2 * rows), :] = piece
        return carry

    lax.fori_loop(0, 2 * rows // SECOND, second, 0)
    down = down_ref[...]

    def contract(x, carry):
        here = pl.ds(pl.multiple_of(x * 2 * rows, 2 * rows), 2 * rows)
        rhs = jnp.concatenate([band_ref[h, here, :] for h in range(channels // LANES)], axis=1)
        rhs = rhs.astype(BF16)
        pooled_ref[x] = jnp.dot(down, rhs, preferred_element_type=F32)
        return carry

    lax.fori_loop(0, width, contract, 0, unroll=4)
    for side, out_ref in ((1, other_ref), (0, mine_ref)):
        def region(m, carry):
            n = m + side * half
            base = pl.multiple_of(n * SIDE, SIDE)

            @pl.when(hit_ref[n] > 0)
            def _():
                for q in range(POOL):
                    one = pooled_ref[xa_ref[n, q], pl.ds(base, SIDE), :] * wa_ref[n, q]
                    two = pooled_ref[xb_ref[n, q], pl.ds(base, SIDE), :] * wb_ref[n, q]
                    total = one + two
                    for h in range(channels // LANES):
                        piece = total[:, h * LANES : (h + 1) * LANES]
                        patch_ref[h, pl.ds(q, SIDE, stride=SIDE), :] = piece
                for h in range(channels // LANES):
                    piece = patch_ref[h, pl.ds(0, POOL * SIDE), :]
                    out_ref[m, :, h * LANES : (h + 1) * LANES] = piece.astype(BF16)

            @pl.when(hit_ref[n] == 0)
            def _():
                out_ref[m] = jnp.zeros(out_ref.shape[1:], BF16)

            return carry

        lax.fori_loop(0, half, region, 0)


def weights_of(boxes, rows, cols):
    count = boxes.shape[0]
    row_first = lax.axis_index("row") * rows
    col_first = lax.axis_index("col") * cols
    places = (row_first + jnp.arange(2 * rows)).astype(F32)[None, None, :]
    centre = sample(boxes[:, 0], boxes[:, 2])
    down = jnp.maximum(1.0 - jnp.abs(places - centre[:, :, None]), 0.0).astype(BF16)
    down = jnp.pad(down, ((0, 0), (0, SIDE - POOL), (0, 0))).reshape(count * SIDE, 2 * rows)
    centre = sample(boxes[:, 1], boxes[:, 3])
    low = jnp.floor(centre)

    def tap(place):
        weight = jnp.maximum(1.0 - jnp.abs(place - centre), 0.0).astype(BF16).astype(F32)
        at = place.astype(jnp.int32) - col_first
        inside = (at >= 0) & (at < cols)
        return jnp.clip(at, 0, cols - 1), jnp.where(inside, weight, 0.0)

    xa, wa = tap(low)
    xb, wb = tap(low + 1.0)
    hit = (boxes[:, 1] < col_first + cols) & (boxes[:, 1] + boxes[:, 3] > col_first)
    return hit.astype(jnp.int32), xa, xb, wa, wb, down


def tower_and_pool(features, weight, bias, boxes):
    rows, cols, channels = features.shape
    below, above, after, edge, inner, flags = exchange(features, weight, bias)
    hit, xa, xb, wa, wb, down = weights_of(boxes, rows, cols)
    count = boxes.shape[0]
    smem = pl.BlockSpec(memory_space=pltpu.SMEM)
    vmem = pl.BlockSpec(memory_space=pltpu.VMEM)
    patches = jax.ShapeDtypeStruct((count // 2, POOL * SIDE, channels), BF16)
    return pl.pallas_call(
        main_kernel,
        out_shape=(jax.ShapeDtypeStruct(features.shape, BF16), patches, patches),
        in_specs=[smem] * 6 + [vmem] * 9,
        out_specs=(vmem, vmem, vmem),
        scratch_shapes=[
            pltpu.VMEM((2 * rows + 4, cols, 3 * channels), BF16),
            pltpu.VMEM((2 * rows + 2, cols, 3 * channels), BF16),
            pltpu.VMEM((channels // LANES, 2 * rows * cols, LANES), F32),
            pltpu.VMEM((cols, count * SIDE, channels), F32),
            pltpu.VMEM((channels // LANES, SIDE * SIDE, LANES), F32),
        ],
        compiler_params=pltpu.CompilerParams(vmem_limit_bytes=40 * 2**20),
        cost_estimate=pl.CostEstimate(flops=6 * 10**9, bytes_accessed=8 * 10**6, transcendentals=0),
    )(
        flags, hit, xa, xb, wa, wb, features, below, above, after, edge, inner,
        weight.reshape(2, 9 * channels, channels), bias, down,
    )


def head(pooled, mask_weight, mask_bias, deconv_weight, deconv_bias):
    padded = jnp.pad(pooled, ((1, 1), (1, 1), (0, 0)))
    hidden = conv_valid(padded, mask_weight[0], mask_bias[0])
    lifted = jnp.einsum("abc,uvcd->aubvd", hidden, deconv_weight, preferred_element_type=F32)
    lifted = jnp.maximum(lifted + deconv_bias, 0.0).astype(BF16)
    return lifted.reshape(1, 2 * POOL, 2 * POOL, -1)


def per_device(
    features, tower_weight, tower_bias, boxes, owner_slot,
    mask_weight, mask_bias, deconv_weight, deconv_bias,
):
    peers = lax.axis_size("col")
    chips = peers // 2
    core = lax.axis_index("col") % 2
    slots = jnp.arange(peers, dtype=jnp.int32)
    wanted = 2 * (slots % chips) + jnp.where(slots < chips, core, 1 - core)
    picked = (owner_slot[0][None, :] == wanted[:, None]).astype(jnp.int32)
    ordered = jnp.sum(picked[:, :, None] * boxes[None, :, :], axis=1)
    tower, mine, other = tower_and_pool(features, tower_weight, tower_bias, ordered)
    swapped = lax.ppermute(other, "col", [(i, i ^ 1) for i in range(peers)])
    chip_sum = (mine.astype(F32) + swapped.astype(F32)).astype(BF16)
    groups = [list(range(0, peers, 2)), list(range(1, peers, 2))]
    parts = lax.all_to_all(chip_sum, "col", 0, 0, tiled=True, axis_index_groups=groups)
    pooled = jnp.sum(parts.astype(F32), axis=0).astype(BF16)
    pooled = pooled.reshape(POOL, SIDE, -1)[:, :POOL]
    masks = head(pooled, mask_weight, mask_bias, deconv_weight, deconv_bias)
    return tower, masks


def solution(mesh):
    placed = (P("row", "col", None), P(), P(), P("row", None), P("row", None), P(), P(), P(), P())
    return jax.shard_map(
        per_device,
        mesh=mesh,
        in_specs=placed,
        out_specs=(P("row", "col", None), P(("row", "col"), None, None, None)),
        check_vma=False,
    )
```

time: 198 us -> 97.6 us (0.49)
  waiting for transfers between devices: 119 us -> 4.76 us
  blocking collectives: 0 us -> 35.9 us
  Pallas kernels: 0 us -> 14.9 us
  between operations: 16 us -> 1.11 us
  matrix products: 16.4 us -> 2.9 us
  starting transfers between devices: 35.2 us -> 28 us
    all_gather x1 -> x0, waiting for transfers between devices: 97.9 us -> none  [per_device(): piece = lax.all_gather(band_tile, 'col', axis=1, tiled=True)]
    all_to_all x0 -> x1, blocking collectives: none -> 35.9 us  [per_device(): lax.all_to_all(chip_sum, 'col', 0, 0, tiled=True, axis_index_groups=groups)]
    dot_general x30 -> x1, matrix products: 16.4 us -> 0.29 us  [head(): jnp.einsum('abc,uvcd->aubvd', hidden, deconv_weight, preferred_element_ty...]
    ppermute x9 -> x7, waiting for transfers between devices: 20.8 us -> 4.76 us  [the longest x6 2.69 us: shift(): lax.ppermute(value, axis, [(i, i + step) for i in devices if i + step in...]
    pallas_call x0 -> x1, Pallas kernels: none -> 14.9 us  [tower_and_pool(): pl.pallas_call(main_kernel, out_shape=(jax.ShapeDtypeStruct(features.shap...]
    ppermute x9 -> x7, starting transfers between devices: 35.1 us -> 28 us  [the longest x6 24.5 us: shift(): lax.ppermute(value, axis, [(i, i + step) for i in devices if i + step in...]
    conv_general_dilated x0 -> x2, matrix products: none -> 2.61 us  [the longest x1 2.17 us: exchange(): lax.conv_general_dilated(batch, weight[0], (1, 1), 'VALID', dimension_num...]
  transfers between devices with their start and end apart: 10 -> 7, of which waited for: 6 -> 3; matrix products, arithmetic and copies ran while one was open for 2% -> 10% of each run, Pallas kernels for 0% -> 0%
where the time goes in v1:
time: 97.6 us; the launch traced here: 97.1 us
  blocking collectives  35.9 us (37%)
  starting transfers between devices  28 us (29%)
  Pallas kernels  14.9 us (15%)
  local copies, waits for them, and re-layouts  5.03 us (5%)
  waiting for transfers between devices  4.76 us (5%)
  other arithmetic  4.54 us (5%)
  matrix products  2.9 us (3%)
  between operations  1.11 us (1%)
    all_to_all x1, blocking collectives, per_device(): lax.all_to_all(chip_sum, 'col', 0, 0, tiled=True, axis_index_groups=groups)  35.9 us
    ppermute x6, starting transfers between devices, shift(): lax.ppermute(value, axis, [(i, i + step) for i in devices if i + step in...  24.5 us
    pallas_call x1, Pallas kernels, tower_and_pool(): pl.pallas_call(main_kernel, out_shape=(jax.ShapeDtypeStruct(features.shap...  14.9 us
    ppermute x1, starting transfers between devices, per_device(): swapped = lax.ppermute(other, 'col', [(i, i ^ 1) for i in range(peers)])  3.53 us
    ppermute x6, waiting for transfers between devices, shift(): lax.ppermute(value, axis, [(i, i + step) for i in devices if i + step in...  2.69 us
    conv_general_dilated x1, matrix products, exchange(): lax.conv_general_dilated(batch, weight[0], (1, 1), 'VALID', dimension_num...  2.17 us
    ppermute x1, waiting for transfers between devices, per_device(): swapped = lax.ppermute(other, 'col', [(i, i ^ 1) for i in range(peers)])  2.08 us
  transfers between devices with their start and end apart: 7, of which 3 were waited for; matrix products, arithmetic and copies ran while one was open for 10% of the time, Pallas kernels for 0%

profile of v1, /device:TPU:6, one launch (start us, length us, event | category | flops | bytes accessed | tf_op | source)
XLA Modules:
  0.0 97.1 jit_solution(9819908577570371929)
XLA Ops:
  0.6 11.3 %collective-permute-start = (bf16[32,32,256]{2,1,0:T(8,128)(2,1)}, bf16[32,32,256]{2,1,0:T(8,128)(2,1)S(1)}, u32[]{:S(2)}, u32[]{:S(2)}) collective-permute-start(bf16[32,32,256]{2,1,0:T(8,128)(2,1)} %own_ref.1), channel_id=1, source_target_pairs={{16,0},{32,16},{48,32},{64,48},{80,64},{96,80},{112,96},{128,112},... | collective-permute-start | bytes 1572872 | tf_op jit(solution)/shard_map/ppermute | solution.py:19
  12.0 1.0 %fusion.56 = (bf16[32,2,256]{2,1,0:T(2,128)(2,1)S(1)}, bf16[32,2,256]{2,1,0:T(2,128)(2,1)S(1)}) fusion(bf16[32,32,256]{2,1,0:T(8,128)(2,1)} %own_ref.1), kind=kLoop, calls=%fused_computation.87 | loop fusion | bytes 131072 | tf_op jit(solution)/shard_map/slice | solution.py:35
  13.0 1.5 %collective-permute-start.1 = (bf16[32,2,256]{2,1,0:T(2,128)(2,1)S(1)}, bf16[32,2,256]{2,1,0:T(2,128)(2,1)S(1)}, u32[]{:S(2)}, u32[]{:S(2)}) collective-permute-start(bf16[32,2,256]{2,1,0:T(2,128)(2,1)S(1)} %get-tuple-element.10), channel_id=1, source_target_pairs={{0,1},{1,2},{2,3},{3,4},{4,5},{5,6},{6,7},{7,8},{8,9},{9,10},{10,1... | collective-permute-start | bytes 98312 | tf_op jit(solution)/shard_map/ppermute | solution.py:19
  14.5 1.3 %collective-permute-start.2 = (bf16[32,2,256]{2,1,0:T(2,128)(2,1)S(1)}, bf16[32,2,256]{2,1,0:T(2,128)(2,1)S(1)}, u32[]{:S(2)}, u32[]{:S(2)}) collective-permute-start(bf16[32,2,256]{2,1,0:T(2,128)(2,1)S(1)} %get-tuple-element.11), channel_id=1, source_target_pairs={{1,0},{2,1},{3,2},{4,3},{5,4},{6,5},{7,6},{8,7},{9,8},{10,9},{11,1... | collective-permute-start | bytes 98312 | tf_op jit(solution)/shard_map/ppermute | solution.py:19
  15.8 0.7 compare_convert_fusion
  16.6 0.8 multiply_reduce_fusion
  17.4 1.0 %fusion.55 = (bf16[32,1,256]{2,1,0:T(2,128)(2,1)S(1)}, bf16[32,1,256]{2,1,0:T(2,128)(2,1)S(1)}) fusion(bf16[32,32,256]{2,1,0:T(8,128)(2,1)} %own_ref.1), kind=kLoop, calls=%fused_computation.86 | loop fusion | bytes 65536 | tf_op jit(solution)/shard_map/slice | solution.py:38
  19.0 0.3 collective-permute-done.2
  19.2 0.7 pad_maximum_fusion.2
  20.0 2.5 %collective-permute-start.4 = (bf16[1,36,256]{2,1,0:T(8,128)(2,1)S(1)}, bf16[1,36,256]{2,1,0:T(8,128)(2,1)S(1)}, u32[]{:S(2)}, u32[]{:S(2)}) collective-permute-start(bf16[1,36,256]{2,1,0:T(8,128)(2,1)S(1)} %pad_maximum_fusion.2), channel_id=1, source_target_pairs={{32,0},{48,16},{64,32},{80,48},{96,64},{112,80},{128,96},{144,112}... | collective-permute-start | bytes 55304 | tf_op jit(solution)/shard_map/ppermute | solution.py:19
  22.4 0.8 pad_maximum_fusion.1
  23.2 3.4 %collective-permute-start.3 = (bf16[2,36,256]{2,1,0:T(8,128)(2,1)S(1)}, bf16[2,36,256]{2,1,0:T(8,128)(2,1)S(1)}, u32[]{:S(2)}, u32[]{:S(2)}) collective-permute-start(bf16[2,36,256]{2,1,0:T(8,128)(2,1)S(1)} %pad_maximum_fusion.1), channel_id=1, source_target_pairs={{0,16},{16,32},{32,48},{48,64},{64,80},{80,96},{96,112},{112,128},... | collective-permute-start | bytes 110600 | tf_op jit(solution)/shard_map/ppermute | solution.py:19
  26.6 0.2 pad_maximum_fusion
  26.8 4.6 %collective-permute-start.5 = (bf16[32,6,256]{2,1,0:T(8,128)(2,1)S(1)}, bf16[32,6,256]{2,1,0:T(8,128)(2,1)S(1)}, u32[]{:S(2)}, u32[]{:S(2)}) collective-permute-start(bf16[32,6,256]{2,1,0:T(8,128)(2,1)S(1)} %pad_maximum_fusion), channel_id=1, source_target_pairs={{16,0},{32,16},{48,32},{64,48},{80,64},{96,80},{112,96},{128,112},... | collective-permute-start | bytes 294920 | tf_op jit(solution)/shard_map/ppermute | solution.py:19
  31.4 2.4 %collective-permute-done.5 = bf16[32,6,256]{2,1,0:T(8,128)(2,1)S(1)} collective-permute-done((bf16[32,6,256]{2,1,0:T(8,128)(2,1)S(1)}, bf16[32,6,256]{2,1,0:T(8,128)(2,1)S(1)}, u32[]{:S(2)}, u32[]{:S(2)}) %collective-permute-start.5) | collective-permute-done | bytes 98336 | tf_op jit(solution)/shard_map/ppermute | solution.py:19
  33.8 0.2 maximum_maximum_fusion
  34.0 0.6 slice.77
  34.8 0.1 copy.45.edge_ref
  35.0 2.2 %fusion.5 = f32[2,65,1,256]{3,0,2,1:T(2,128)S(1)} fusion(bf16[2,3,3,256,256]{4,3,2,1,0:T(8,128)(2,1)} %param.10, bf16[67,2,3,256]{3,0,2,1:T(8,128)(2,1)S(1)} %bitcast.68), kind=kOutput, calls=%fused_computation.7 | convolution fusion | flops 153354240 | bytes 1518592 | tf_op jit(solution)/shard_map/conv_general_dilated | solution.py:50
  37.2 0.2 broadcast_select_fusion
  37.5 14.9 %shard_map.104 = (bf16[32,32,256]{2,1,0:T(8,128)(2,1)}, bf16[8,224,256]{2,1,0:T(8,128)(2,1)S(1)}, bf16[8,224,256]{2,1,0:T(8,128)(2,1)S(1)}) custom-call(s32[2]{0:T(128)S(1)} %add_convert_fusion.1.flags_ref, s32[16]{0:T(128)S(1)} %fusion.50.hit_ref, s32[16,14]{1,0:T(8,128)S(1)} %get-tuple-element.25.xa_ref, s32[16,14]{1,0:T(8,128)S(1)} %get-tuple-element.24.xb_ref, ...), custom_call_target="tpu_custom_call" | custom-call | flops 6000000000 | bytes 8000000 | tf_op jit(solution)/shard_map/pallas_call | solution.py:213
  52.4 3.5 %collective-permute-start.6 = (bf16[8,224,256]{2,1,0:T(8,128)(2,1)S(1)}, bf16[8,224,256]{2,1,0:T(8,128)(2,1)S(1)}, u32[]{:S(2)}, u32[]{:S(2)}) collective-permute-start(bf16[8,224,256]{2,1,0:T(8,128)(2,1)S(1)} %get-tuple-element.7), channel_id=1, source_target_pairs={{0,1},{1,0},{2,3},{3,2},{4,5},{5,4},{6,7},{7,6},{8,9},{9,8},{10,11... | collective-permute-start | bytes 2752520 | tf_op jit(solution)/shard_map/ppermute | solution.py:253
  55.9 2.1 %collective-permute-done.6 = bf16[8,224,256]{2,1,0:T(8,128)(2,1)S(1)} collective-permute-done((bf16[8,224,256]{2,1,0:T(8,128)(2,1)S(1)}, bf16[8,224,256]{2,1,0:T(8,128)(2,1)S(1)}, u32[]{:S(2)}, u32[]{:S(2)}) %collective-permute-start.6) | collective-permute-done | bytes 917536 | tf_op jit(solution)/shard_map/ppermute | solution.py:253
  58.0 0.3 add_convert_fusion
  58.3 35.9 %all_to_all.5 = bf16[8,224,256]{2,1,0:T(8,128)(2,1)S(1)} all-to-all(bf16[8,224,256]{2,1,0:T(8,128)(2,1)S(1)} %add_convert_fusion), channel_id=1, replica_groups={{0,2,4,6,8,10,12,14},{1,3,5,7,9,11,13,15},{16,18,20,22,24,26,28,30},{17..., dimensions={0} | all-to-all | bytes 1835008 | tf_op jit(solution)/shard_map/all_to_all | solution.py:256
  94.2 0.1 reduce_sum.22
  94.6 0.4 fusion.8
  95.1 0.2 reshape.187
  95.3 0.3 copy-done.4
  95.6 0.3 fusion.2
  95.9 0.3 copy.50
  96.2 0.9 reshape.180
  (45 shorter events, 1.1 us)
Async XLA Ops:
  0.6 93.9 %copy-start = (bf16[1,3,3,256,256]{4,3,2,1,0:T(8,128)(2,1)S(1)}, bf16[1,3,3,256,256]{4,3,2,1,0:T(8,128)(2,1)}, u32[]{:S(2)}) copy-start(bf16[1,3,3,256,256]{4,3,2,1,0:T(8,128)(2,1)} %param.14) | copy-start | bytes 3538948
  0.6 36.9 %collective-permute-start = (bf16[32,32,256]{2,1,0:T(8,128)(2,1)}, bf16[32,32,256]{2,1,0:T(8,128)(2,1)S(1)}, u32[]{:S(2)}, u32[]{:S(2)}) collective-permute-start(bf16[32,32,256]{2,1,0:T(8,128)(2,1)} %own_ref.1), channel_id=1, source_target_pairs={{16,0},{32,16},{48,32},{64,48},{80,64},{96,80},{112,96},{128,112},... | collective-permute-start | bytes 1572872 | tf_op jit(solution)/shard_map/ppermute | solution.py:19
  13.0 5.9 %collective-permute-start.1 = (bf16[32,2,256]{2,1,0:T(2,128)(2,1)S(1)}, bf16[32,2,256]{2,1,0:T(2,128)(2,1)S(1)}, u32[]{:S(2)}, u32[]{:S(2)}) collective-permute-start(bf16[32,2,256]{2,1,0:T(2,128)(2,1)S(1)} %get-tuple-element.10), channel_id=1, source_target_pairs={{0,1},{1,2},{2,3},{3,4},{4,5},{5,6},{6,7},{7,8},{8,9},{9,10},{10,1... | collective-permute-start | bytes 98312 | tf_op jit(solution)/shard_map/ppermute | solution.py:19
  14.5 4.7 %collective-permute-start.2 = (bf16[32,2,256]{2,1,0:T(2,128)(2,1)S(1)}, bf16[32,2,256]{2,1,0:T(2,128)(2,1)S(1)}, u32[]{:S(2)}, u32[]{:S(2)}) collective-permute-start(bf16[32,2,256]{2,1,0:T(2,128)(2,1)S(1)} %get-tuple-element.11), channel_id=1, source_target_pairs={{1,0},{2,1},{3,2},{4,3},{5,4},{6,5},{7,6},{8,7},{9,8},{10,9},{11,1... | collective-permute-start | bytes 98312 | tf_op jit(solution)/shard_map/ppermute | solution.py:19
  20.0 11.4 %collective-permute-start.4 = (bf16[1,36,256]{2,1,0:T(8,128)(2,1)S(1)}, bf16[1,36,256]{2,1,0:T(8,128)(2,1)S(1)}, u32[]{:S(2)}, u32[]{:S(2)}) collective-permute-start(bf16[1,36,256]{2,1,0:T(8,128)(2,1)S(1)} %pad_maximum_fusion.2), channel_id=1, source_target_pairs={{32,0},{48,16},{64,32},{80,48},{96,64},{112,80},{128,96},{144,112}... | collective-permute-start | bytes 55304 | tf_op jit(solution)/shard_map/ppermute | solution.py:19
  23.2 8.2 %collective-permute-start.3 = (bf16[2,36,256]{2,1,0:T(8,128)(2,1)S(1)}, bf16[2,36,256]{2,1,0:T(8,128)(2,1)S(1)}, u32[]{:S(2)}, u32[]{:S(2)}) collective-permute-start(bf16[2,36,256]{2,1,0:T(8,128)(2,1)S(1)} %pad_maximum_fusion.1), channel_id=1, source_target_pairs={{0,16},{16,32},{32,48},{48,64},{64,80},{80,96},{96,112},{112,128},... | collective-permute-start | bytes 110600 | tf_op jit(solution)/shard_map/ppermute | solution.py:19
  26.8 7.1 %collective-permute-start.5 = (bf16[32,6,256]{2,1,0:T(8,128)(2,1)S(1)}, bf16[32,6,256]{2,1,0:T(8,128)(2,1)S(1)}, u32[]{:S(2)}, u32[]{:S(2)}) collective-permute-start(bf16[32,6,256]{2,1,0:T(8,128)(2,1)S(1)} %pad_maximum_fusion), channel_id=1, source_target_pairs={{16,0},{32,16},{48,32},{64,48},{80,64},{96,80},{112,96},{128,112},... | collective-permute-start | bytes 294920 | tf_op jit(solution)/shard_map/ppermute | solution.py:19
  34.7 2.5 %slice-start = ((f32[2,256]{1,0:T(2,128)}), f32[1,256]{1,0:T(1,128)S(1)}, s32[]{:S(2)}) async-start(f32[2,256]{1,0:T(2,128)} %bias_ref.1), calls=%async_computation.1 | async-start | bytes 2048 | tf_op jit(solution)/shard_map/slice | solution.py:54
  34.8 2.7 %copy-start.1 = (bf16[32,32,256]{2,1,0:T(8,128)(2,1)S(1)}, bf16[32,32,256]{2,1,0:T(8,128)(2,1)}, u32[]{:S(2)}) copy-start(bf16[32,32,256]{2,1,0:T(8,128)(2,1)} %own_ref.1) | copy-start | bytes 1572868
  34.8 2.7 %copy-start.2 = (f32[2,256]{1,0:T(2,128)S(1)}, f32[2,256]{1,0:T(2,128)}, u32[]{:S(2)}) copy-start(f32[2,256]{1,0:T(2,128)} %bias_ref.1) | copy-start | bytes 6148
  34.8 2.7 %copy-start.3 = (bf16[2,3,3,256,256]{4,3,2,1,0:T(8,128)(2,1)S(1)}, bf16[2,3,3,256,256]{4,3,2,1,0:T(8,128)(2,1)}, u32[]{:S(2)}) copy-start(bf16[2,3,3,256,256]{4,3,2,1,0:T(8,128)(2,1)} %param.10) | copy-start | bytes 7077892
  52.4 5.6 %collective-permute-start.6 = (bf16[8,224,256]{2,1,0:T(8,128)(2,1)S(1)}, bf16[8,224,256]{2,1,0:T(8,128)(2,1)S(1)}, u32[]{:S(2)}, u32[]{:S(2)}) collective-permute-start(bf16[8,224,256]{2,1,0:T(8,128)(2,1)S(1)} %get-tuple-element.7), channel_id=1, source_target_pairs={{0,1},{1,0},{2,3},{3,2},{4,5},{5,4},{6,7},{7,6},{8,9},{9,8},{10,11... | collective-permute-start | bytes 2752520 | tf_op jit(solution)/shard_map/ppermute | solution.py:253
  58.3 36.2 %copy-start.7 = (pred[8,2]{0,1:T(4,128)(4,1)S(1)}, pred[8,2]{0,1:T(4,128)(4,1)}, u32[]{:S(2)}) copy-start(pred[8,2]{0,1:T(4,128)(4,1)} %constant.91) | copy-start | bytes 52
  94.5 1.0 %copy-start.4 = (bf16[2,2,256,256]{3,2,1,0:T(8,128)(2,1)S(1)}, bf16[2,2,256,256]{3,2,1,0:T(8,128)(2,1)}, u32[]{:S(2)}) copy-start(bf16[2,2,256,256]{3,2,1,0:T(8,128)(2,1)} %param.16) | copy-start | bytes 1572868
  94.5 1.0 %copy-start.5 = (f32[256]{0:T(256)S(1)}, f32[256]{0:T(256)}, u32[]{:S(2)}) copy-start(f32[256]{0:T(256)} %param.17) | copy-start | bytes 3076
  94.5 1.0 %copy-start.6 = (f32[1,256]{1,0:T(1,128)S(1)}, f32[1,256]{1,0:T(1,128)}, u32[]{:S(2)}) copy-start(f32[1,256]{1,0:T(1,128)} %param.15) | copy-start | bytes 3076

commit v2 on v1

--- a/solution.py
+++ b/solution.py
@@ -8,8 +8,10 @@
 POOL = 14
 SIDE = 16
 LANES = 128
+TILE = 16
 FIRST = 11
 SECOND = 8
+HOPS = (4, 1, -1, 2, -3, 3, -2, 0)
 F32 = jnp.float32
 BF16 = jnp.bfloat16
 
@@ -27,35 +29,65 @@
     return jnp.maximum(out + bias, 0.0).astype(BF16)
 
 
-def exchange(features, weight, bias):
+def call(kernel, out_shape, in_specs, scratch, limit, flops, *args):
+    vmem = pl.BlockSpec(memory_space=pltpu.VMEM)
+    return pl.pallas_call(
+        kernel,
+        out_shape=out_shape,
+        in_specs=in_specs,
+        out_specs=tuple(vmem for _ in out_shape),
+        scratch_shapes=scratch,
+        compiler_params=pltpu.CompilerParams(vmem_limit_bytes=limit * 2**20),
+        cost_estimate=pl.CostEstimate(flops=flops, bytes_accessed=10**6, transcendentals=0),
+    )(*args)
+
+
+def columns_kernel(tile_ref, lead_ref, tail_ref, flat_ref):
+    rows, width, channels = tile_ref.shape
+    for out_ref, first, start in ((lead_ref, 0, 0), (tail_ref, TILE - 2, width - TILE)):
+        block = tile_ref[:, pl.ds(start, TILE), :].astype(F32).reshape(rows * TILE, channels)
+        for h in range(channels // LANES):
+            flat_ref[h] = block[:, h * LANES : (h + 1) * LANES]
+        for x in range(2):
+            here = pl.ds(first + x, rows, stride=TILE)
+            column = [flat_ref[h, here, :] for h in range(channels // LANES)]
+            out_ref[x] = jnp.concatenate(column, axis=1).astype(BF16)
+
+
+def pack_kernel(tile_ref, left_ref, right_ref, lead_ref, tail_ref, sides_ref, down_ref, up_ref):
+    rows, width, channels = tile_ref.shape
+    parts = (left_ref[0], left_ref[1], lead_ref[0], tail_ref[1], right_ref[0], right_ref[1])
+    whole = width // TILE
+    down_ref[0 : 2 * whole] = tile_ref[rows - 2 : rows].reshape(2 * whole, TILE, channels)
+    up_ref[0:whole] = tile_ref[0:1].reshape(whole, TILE, channels)
+    for i, part in enumerate(parts):
+        sides_ref[i] = part
+        down_ref[2 * whole + i] = part[rows - TILE : rows]
+        up_ref[whole + i] = part[0:TILE]
+
+
+def exchange(features, later):
     rows, cols, channels = features.shape
-    row, col = lax.axis_index("row"), lax.axis_index("col")
-    last_row, last_col = lax.axis_size("row") - 1, lax.axis_size("col") - 1
+    vmem = pl.BlockSpec(memory_space=pltpu.VMEM)
     below = shift(features, "row", -1)
-    left = shift(features[:, cols - 2 :], "col", 1)
-    right = shift(features[:, :2], "col", -1)
-    own = jnp.concatenate([left, features, right], axis=1)
-    own_sides = jnp.concatenate([left, features[:, :1], features[:, cols - 1 :], right], axis=1)
+    pair = jax.ShapeDtypeStruct((2, rows, channels), BF16)
+    lead, tail = call(
+        columns_kernel, (pair, pair), [vmem],
+        [pltpu.VMEM((channels // LANES, rows * TILE, LANES), F32)], 4, 10**5, features,
+    )
+    left = shift(tail, "col", 1)
+    right = shift(lead, "col", -1)
+    whole = cols // TILE
+    shapes = [(6, rows), (2 * whole + 6, TILE), (whole + 6, TILE)]
+    own_sides, to_down, to_up = call(
+        pack_kernel,
+        tuple(jax.ShapeDtypeStruct(shape + (channels,), BF16) for shape in shapes),
+        [vmem] * 5, [], 4, 10**5, features, left, right, lead, tail,
+    )
     sides = shift(own_sides, "row", -1)
-    above = shift(own[rows - 2 :], "row", 1)
-    after = shift(own[:1], "row", -2)
-
-    def ends(strip):
-        return jnp.concatenate([strip[:, :3], strip[:, cols + 1 :]], axis=1)
-
-    columns = jnp.concatenate([ends(above), own_sides, sides, ends(after)], axis=0)
-    edge = jnp.pad(columns[:, 1:5:3].astype(F32), ((0, 1), (0, 0), (0, 0)))
-    edge = edge.swapaxes(0, 1)[:, :, None]
-    batch = columns.reshape(-1, 2, 3, channels).swapaxes(0, 1)
-    inner = lax.conv_general_dilated(
-        batch, weight[0], (1, 1), "VALID",
-        dimension_numbers=("NHWC", "HWIO", "NHWC"), preferred_element_type=F32,
-    )
-    inner = jnp.maximum(inner + bias[0], 0.0).astype(BF16).astype(F32)
-    kept = jnp.stack([col > 0, col < last_col])[:, None, None, None]
-    inner = jnp.pad(jnp.where(kept, inner, 0.0), ((0, 0), (0, 1), (0, 0), (0, 0)))
-    flags = jnp.stack([row == 0, row == last_row]).astype(jnp.int32)
-    return below, above[:, 2 : cols + 2], after[:, 2 : cols + 2], edge, inner, flags
+    after, later = lax.optimization_barrier((shift(to_up, "row", -2), later))
+    above = shift(to_down, "row", 1)
+    return below, own_sides, sides, above, after, later
 
 
 def sample(lower, extent):
@@ -66,17 +98,18 @@
     return jnp.clip(centre, lower_f, lower_f + extent_f - 1.0)
 
 
-def spread(dst, start, value, edges, offset):
+def spread(dst, start, value, edge_ref, sides, offset):
     count, width, channels = value.shape
-    value = value.astype(F32)
-    place = lax.broadcasted_iota(jnp.int32, value.shape, 1)
-    here = pl.ds(offset, count)
-    before = jnp.where(place == 0, edges[0, here], pltpu.roll(value, 1, 1))
-    after = jnp.where(place == width - 1, edges[1, here], pltpu.roll(value, width - 1, 1))
-    rows = pl.ds(start, count)
-    dst[rows, :, 0:channels] = before.astype(BF16)
-    dst[rows, :, channels : 2 * channels] = value.astype(BF16)
-    dst[rows, :, 2 * channels : 3 * channels] = after.astype(BF16)
+    place = lax.broadcasted_iota(jnp.int32, (width, channels), 0)
+    for k in range(count):
+        line = value[k].astype(F32)
+        low = edge_ref[sides[0], pl.ds(offset + k, 1), :]
+        high = edge_ref[sides[1], pl.ds(offset + k, 1), :]
+        before = jnp.where(place == 0, low, pltpu.roll(line, 1, 0))
+        after = jnp.where(place == width - 1, high, pltpu.roll(line, width - 1, 0))
+        dst[start + k, :, 0:channels] = before.astype(BF16)
+        dst[start + k, :, channels : 2 * channels] = line.astype(BF16)
+        dst[start + k, :, 2 * channels : 3 * channels] = after.astype(BF16)
 
 
 def taps(src, start, count, weight, bias):
@@ -89,29 +122,50 @@
 
 def main_kernel(
     flags_ref, hit_ref, xa_ref, xb_ref, wa_ref, wb_ref,
-    own_ref, below_ref, above_ref, after_ref, edge_ref, inner_ref,
+    own_ref, below_ref, own_sides_ref, sides_ref, above_ref, after_ref,
     weight_ref, bias_ref, down_ref,
     tower_ref, mine_ref, other_ref,
-    wide_ref, mid_ref, band_ref, pooled_ref, patch_ref,
+    wide_ref, mid_ref, band_ref, pooled_ref, patch_ref, strip_ref, inner_ref,
 ):
     rows, width, channels = own_ref.shape
     half = mine_ref.shape[0]
-    spread(wide_ref, 0, above_ref[...], edge_ref, 0)
+    whole = width // TILE
+    for c in range(6):
+        strip_ref[c, 0:2, :] = above_ref[2 * whole + c].astype(F32)[TILE - 2 : TILE]
+        strip_ref[c, 2 : rows + 2, :] = own_sides_ref[c].astype(F32)
+        strip_ref[c, rows + 2 : 2 * rows + 2, :] = sides_ref[c].astype(F32)
+        strip_ref[c, 2 * rows + 2 : 2 * rows + 3, :] = after_ref[whole + c].astype(F32)[0:1]
+        tail = strip_ref.shape[1] - (2 * rows + 3)
+        strip_ref[c, 2 * rows + 3 :, :] = jnp.zeros((tail, channels), F32)
+    for side in range(2):
+        tall = inner_ref.shape[1]
+        parts = [
+            strip_ref[3 * side + dx, dy : dy + tall, :].astype(BF16)
+            for dy in range(3)
+            for dx in range(3)
+        ]
+        out = jnp.dot(
+            jnp.concatenate(parts, axis=1), weight_ref[0], preferred_element_type=F32
+        )
+        out = jnp.maximum(out + bias_ref[0:1], 0.0).astype(BF16).astype(F32)
+        inner_ref[side] = jnp.where(flags_ref[2 + side] > 0, out, 0.0)
+    spread(wide_ref, 0, above_ref[0 : 2 * whole].reshape(2, width, channels), strip_ref, (1, 4), 0)
     step = 8
     for part, base in ((own_ref, 2), (below_ref, 2 + rows)):
         def fill(i, carry):
             at = i * step
-            spread(wide_ref, base + at, part[pl.ds(at, step)], edge_ref, base + at)
+            spread(wide_ref, base + at, part[pl.ds(at, step)], strip_ref, (1, 4), base + at)
             return carry
 
         lax.fori_loop(0, rows // step, fill, 0)
-    spread(wide_ref, 2 + 2 * rows, after_ref[...], edge_ref, 2 + 2 * rows)
+    last = 2 + 2 * rows
+    spread(wide_ref, last, after_ref[0:whole].reshape(1, width, channels), strip_ref, (1, 4), last)
     wide_ref[3 + 2 * rows] = jnp.zeros(wide_ref.shape[1:], BF16)
 
     def first(i, carry):
         at = i * FIRST
         out = taps(wide_ref, at, FIRST, weight_ref[0], bias_ref[0:1])
-        spread(mid_ref, at, out.astype(BF16), inner_ref, at)
+        spread(mid_ref, at, out.astype(BF16), inner_ref, (0, 1), at)
         return carry
 
     lax.fori_loop(0, (2 * rows + 2) // FIRST, first, 0)
@@ -165,9 +219,9 @@
                     total = one + two
                     for h in range(channels // LANES):
                         piece = total[:, h * LANES : (h + 1) * LANES]
-                        patch_ref[h, pl.ds(q, SIDE, stride=SIDE), :] = piece
+                        patch_ref[h, pl.ds(q, SIDE, stride=POOL), :] = piece
                 for h in range(channels // LANES):
-                    piece = patch_ref[h, pl.ds(0, POOL * SIDE), :]
+                    piece = patch_ref[h, pl.ds(0, POOL * POOL), :]
                     out_ref[m, :, h * LANES : (h + 1) * LANES] = piece.astype(BF16)
 
             @pl.when(hit_ref[n] == 0)
@@ -202,30 +256,36 @@
     return hit.astype(jnp.int32), xa, xb, wa, wb, down
 
 
-def tower_and_pool(features, weight, bias, boxes):
+def tower_and_pool(features, weight, bias, boxes, owner_slot, wanted):
     rows, cols, channels = features.shape
-    below, above, after, edge, inner, flags = exchange(features, weight, bias)
+    below, own_sides, sides, above, after, (boxes, owner_slot, wanted) = exchange(
+        features, (boxes, owner_slot, wanted)
+    )
+    row, col = lax.axis_index("row"), lax.axis_index("col")
+    last_row, last_col = lax.axis_size("row") - 1, lax.axis_size("col") - 1
+    flags = jnp.stack([row == 0, row == last_row, col > 0, col < last_col]).astype(jnp.int32)
+    picked = (owner_slot[0][None, :] == wanted[:, None]).astype(jnp.int32)
+    boxes = jnp.sum(picked[:, :, None] * boxes[None, :, :], axis=1)
     hit, xa, xb, wa, wb, down = weights_of(boxes, rows, cols)
     count = boxes.shape[0]
     smem = pl.BlockSpec(memory_space=pltpu.SMEM)
     vmem = pl.BlockSpec(memory_space=pltpu.VMEM)
-    patches = jax.ShapeDtypeStruct((count // 2, POOL * SIDE, channels), BF16)
-    return pl.pallas_call(
+    patches = jax.ShapeDtypeStruct((count // 2, POOL * POOL, channels), BF16)
+    return call(
         main_kernel,
-        out_shape=(jax.ShapeDtypeStruct(features.shape, BF16), patches, patches),
-        in_specs=[smem] * 6 + [vmem] * 9,
-        out_specs=(vmem, vmem, vmem),
-        scratch_shapes=[
+        (jax.ShapeDtypeStruct(features.shape, BF16), patches, patches),
+        [smem] * 6 + [vmem] * 9,
+        [
             pltpu.VMEM((2 * rows + 4, cols, 3 * channels), BF16),
             pltpu.VMEM((2 * rows + 2, cols, 3 * channels), BF16),
             pltpu.VMEM((channels // LANES, 2 * rows * cols, LANES), F32),
             pltpu.VMEM((cols, count * SIDE, channels), F32),
             pltpu.VMEM((channels // LANES, SIDE * SIDE, LANES), F32),
+            pltpu.VMEM((6, 2 * rows + 24, channels), F32),
+            pltpu.VMEM((2, 2 * rows + 16, channels), F32),
         ],
-        compiler_params=pltpu.CompilerParams(vmem_limit_bytes=40 * 2**20),
-        cost_estimate=pl.CostEstimate(flops=6 * 10**9, bytes_accessed=8 * 10**6, transcendentals=0),
-    )(
-        flags, hit, xa, xb, wa, wb, features, below, above, after, edge, inner,
+        40, 6 * 10**9,
+        flags, hit, xa, xb, wa, wb, features, below, own_sides, sides, above, after,
         weight.reshape(2, 9 * channels, channels), bias, down,
     )
 
@@ -245,17 +305,29 @@
     peers = lax.axis_size("col")
     chips = peers // 2
     core = lax.axis_index("col") % 2
-    slots = jnp.arange(peers, dtype=jnp.int32)
-    wanted = 2 * (slots % chips) + jnp.where(slots < chips, core, 1 - core)
-    picked = (owner_slot[0][None, :] == wanted[:, None]).astype(jnp.int32)
-    ordered = jnp.sum(picked[:, :, None] * boxes[None, :, :], axis=1)
-    tower, mine, other = tower_and_pool(features, tower_weight, tower_bias, ordered)
+    chip = lax.axis_index("col") // 2
+    hops = jnp.array(HOPS * 2, dtype=jnp.int32)
+    sides = jnp.repeat(jnp.stack([core, 1 - core]), chips)
+    wanted = 2 * ((chip + hops * (1 - 2 * sides)) % chips) + sides
+    tower, mine, other = tower_and_pool(
+        features, tower_weight, tower_bias, boxes, owner_slot, wanted
+    )
     swapped = lax.ppermute(other, "col", [(i, i ^ 1) for i in range(peers)])
-    chip_sum = (mine.astype(F32) + swapped.astype(F32)).astype(BF16)
-    groups = [list(range(0, peers, 2)), list(range(1, peers, 2))]
-    parts = lax.all_to_all(chip_sum, "col", 0, 0, tiled=True, axis_index_groups=groups)
-    pooled = jnp.sum(parts.astype(F32), axis=0).astype(BF16)
-    pooled = pooled.reshape(POOL, SIDE, -1)[:, :POOL]
+
+    def send(value, hop):
+        steps = [2 * hop * (1 - 2 * (i % 2)) for i in range(peers)]
+        return lax.ppermute(value, "col", [(i, (i + steps[i]) % peers) for i in range(peers)])
+
+    def total(*parts):
+        parts = [part.astype(F32) for part in parts]
+        return sum(parts[1:], parts[0]).astype(BF16)
+
+    ahead = send(total(mine[0:3], swapped[0:3]), 1)
+    back = send(total(mine[3:5], swapped[3:5]), -1)
+    three = send(total(mine[5], swapped[5], ahead[0], back[0]), 3)
+    two = send(total(mine[6], swapped[6], ahead[2], back[1]), -2)
+    pooled = total(mine[7], swapped[7], ahead[1], three, two)
+    pooled = pooled.reshape(POOL, POOL, -1)
     masks = head(pooled, mask_weight, mask_bias, deconv_weight, deconv_bias)
     return tower, masks
 

time: 97.6 us -> 89.9 us (0.921)
  blocking collectives: 35.9 us -> 0 us
  waiting for transfers between devices: 4.76 us -> 24.7 us
  starting transfers between devices: 28 us -> 38.8 us
  other arithmetic: 4.54 us -> 1.66 us
  matrix products: 2.9 us -> 0.73 us
  local copies, waits for them, and re-layouts: 5.03 us -> 6.96 us
    all_to_all x1 -> x0, blocking collectives: 35.9 us -> none  [per_device(): lax.all_to_all(chip_sum, 'col', 0, 0, tiled=True, axis_index_groups=groups)]
    ppermute x0 -> x4, waiting for transfers between devices: none -> 15.9 us  [send(): lax.ppermute(value, 'col', [(i, (i + steps[i]) % peers) for i in range(pe...]
    ppermute x0 -> x4, starting transfers between devices: none -> 13.2 us  [send(): lax.ppermute(value, 'col', [(i, (i + steps[i]) % peers) for i in range(pe...]
    ppermute x6, waiting for transfers between devices: 2.69 us -> 6.93 us  [shift(): lax.ppermute(value, axis, [(i, i + step) for i in devices if i + step in...]
    unnamed x17 -> x24, local copies, waits for them, and re-layouts: 0.35 us -> 4.06 us
    conv_general_dilated x1 -> x0, matrix products: 2.17 us -> none  [exchange(): lax.conv_general_dilated(batch, weight[0], (1, 1), 'VALID', dimension_num...]
    ppermute x6, starting transfers between devices: 24.5 us -> 22.5 us  [shift(): lax.ppermute(value, axis, [(i, i + step) for i in devices if i + step in...]
    slice x9 -> x3, local copies, waits for them, and re-layouts: 2.72 us -> 0.84 us  [the longest x1 0.52 us: per_device(): pooled = total(mine[7], swapped[7], ahead[1], three, two)]
  transfers between devices with their start and end apart: 7 -> 11, of which waited for: 3 -> 7; matrix products, arithmetic and copies ran while one was open for 10% -> 2% of each run, Pallas kernels for 0% -> 0%
where the time goes in v2:
time: 89.9 us; the launch traced here: 89.3 us
  starting transfers between devices  38.8 us (43%)
  waiting for transfers between devices  24.7 us (27%)
  Pallas kernels  15.4 us (17%)
  local copies, waits for them, and re-layouts  6.96 us (8%)
  other arithmetic  1.66 us (2%)
  between operations  1.06 us (1%)
    ppermute x6, starting transfers between devices, shift(): lax.ppermute(value, axis, [(i, i + step) for i in devices if i + step in...  22.5 us
    ppermute x4, waiting for transfers between devices, send(): lax.ppermute(value, 'col', [(i, (i + steps[i]) % peers) for i in range(pe...  15.9 us
    pallas_call x3, Pallas kernels, call(): pl.pallas_call(kernel, out_shape=out_shape, in_specs=in_specs, out_specs=...  15.4 us
    ppermute x4, starting transfers between devices, send(): lax.ppermute(value, 'col', [(i, (i + steps[i]) % peers) for i in range(pe...  13.2 us
    ppermute x6, waiting for transfers between devices, shift(): lax.ppermute(value, axis, [(i, i + step) for i in devices if i + step in...  6.93 us
    unnamed x24, local copies, waits for them, and re-layouts  4.06 us
    ppermute x1, starting transfers between devices, per_device(): swapped = lax.ppermute(other, 'col', [(i, i ^ 1) for i in range(peers)])  3.13 us
    ppermute x1, waiting for transfers between devices, per_device(): swapped = lax.ppermute(other, 'col', [(i, i ^ 1) for i in range(peers)])  1.91 us
  transfers between devices with their start and end apart: 11, of which 7 were waited for; matrix products, arithmetic and copies ran while one was open for 2% of the time, Pallas kernels for 0%

profile of v2, /device:TPU:6, one launch (start us, length us, event | category | flops | bytes accessed | tf_op | source)
XLA Modules:
  0.0 89.3 jit_solution(1718784412467568549)
XLA Ops:
  0.6 11.3 %collective-permute-start.3 = (bf16[32,32,256]{2,1,0:T(8,128)(2,1)}, bf16[32,32,256]{2,1,0:T(8,128)(2,1)S(1)}, u32[]{:S(2)}, u32[]{:S(2)}) collective-permute-start(bf16[32,32,256]{2,1,0:T(8,128)(2,1)} %own_ref.1), channel_id=1, source_target_pairs={{16,0},{32,16},{48,32},{64,48},{80,64},{96,80},{112,96},{128,112},... | collective-permute-start | bytes 1572872 | tf_op jit(solution)/shard_map/ppermute | solution.py:21
  12.0 1.0 %copy-done.1 = bf16[32,32,256]{2,1,0:T(8,128)(2,1)S(1)} copy-done((bf16[32,32,256]{2,1,0:T(8,128)(2,1)S(1)}, bf16[32,32,256]{2,1,0:T(8,128)(2,1)}, u32[]{:S(2)}) %copy-start.1) | copy-done | bytes 524312
  13.2 1.6 %collective-permute-start = (bf16[2,32,256]{2,1,0:T(8,128)(2,1)S(1)}, bf16[2,32,256]{2,1,0:T(8,128)(2,1)S(1)}, u32[]{:S(2)}, u32[]{:S(2)}) collective-permute-start(bf16[2,32,256]{2,1,0:T(8,128)(2,1)S(1)} %get-tuple-element.14.tail_ref), channel_id=1, source_target_pairs={{0,1},{1,2},{2,3},{3,4},{4,5},{5,6},{6,7},{7,8},{8,9},{9,10},{10,1... | collective-permute-start | bytes 98312 | tf_op jit(solution)/shard_map/ppermute | solution.py:21
  14.8 1.3 %collective-permute-start.1 = (bf16[2,32,256]{2,1,0:T(8,128)(2,1)S(1)}, bf16[2,32,256]{2,1,0:T(8,128)(2,1)S(1)}, u32[]{:S(2)}, u32[]{:S(2)}) collective-permute-start(bf16[2,32,256]{2,1,0:T(8,128)(2,1)S(1)} %get-tuple-element.15.lead_ref), channel_id=1, source_target_pairs={{1,0},{2,1},{3,2},{4,3},{5,4},{6,5},{7,6},{8,7},{9,8},{10,9},{11,1... | collective-permute-start | bytes 98312 | tf_op jit(solution)/shard_map/ppermute | solution.py:21
  16.3 0.7 fusion.46
  17.0 2.5 %collective-permute-done.1.right_ref = bf16[2,32,256]{2,1,0:T(8,128)(2,1)S(1)} collective-permute-done((bf16[2,32,256]{2,1,0:T(8,128)(2,1)S(1)}, bf16[2,32,256]{2,1,0:T(8,128)(2,1)S(1)}, u32[]{:S(2)}, u32[]{:S(2)}) %collective-permute-start.1) | collective-permute-done | bytes 32800 | tf_op jit(solution)/shard_map/ppermute | solution.py:21
  19.5 1.0 %copy-done.2 = bf16[32,32,256]{2,1,0:T(8,128)(2,1)S(1)} copy-done((bf16[32,32,256]{2,1,0:T(8,128)(2,1)S(1)}, bf16[32,32,256]{2,1,0:T(8,128)(2,1)}, u32[]{:S(2)}) %copy-start.2) | copy-done | bytes 524312
  20.6 2.5 %collective-permute-start.2 = (bf16[8,16,256]{2,1,0:T(8,128)(2,1)S(1)}, bf16[8,16,256]{2,1,0:T(8,128)(2,1)S(1)}, u32[]{:S(2)}, u32[]{:S(2)}) collective-permute-start(bf16[8,16,256]{2,1,0:T(8,128)(2,1)S(1)} %get-tuple-element.16), channel_id=1, source_target_pairs={{32,0},{48,16},{64,32},{80,48},{96,64},{112,80},{128,96},{144,112}... | collective-permute-start | bytes 196616 | tf_op jit(solution)/shard_map/ppermute | solution.py:21
  23.1 2.5 %collective-permute-start.4 = (bf16[6,32,256]{2,1,0:T(8,128)(2,1)S(1)}, bf16[6,32,256]{2,1,0:T(8,128)(2,1)S(1)}, u32[]{:S(2)}, u32[]{:S(2)}) collective-permute-start(bf16[6,32,256]{2,1,0:T(8,128)(2,1)S(1)} %get-tuple-element.20.own_sides_ref), channel_id=1, source_target_pairs={{16,0},{32,16},{48,32},{64,48},{80,64},{96,80},{112,96},{128,112},... | collective-permute-start | bytes 294920 | tf_op jit(solution)/shard_map/ppermute | solution.py:21
  25.6 3.4 %collective-permute-start.5 = (bf16[10,16,256]{2,1,0:T(8,128)(2,1)S(1)}, bf16[10,16,256]{2,1,0:T(8,128)(2,1)S(1)}, u32[]{:S(2)}, u32[]{:S(2)}) collective-permute-start(bf16[10,16,256]{2,1,0:T(8,128)(2,1)S(1)} %get-tuple-element.21), channel_id=1, source_target_pairs={{0,16},{16,32},{32,48},{48,64},{64,80},{80,96},{96,112},{112,128},... | collective-permute-start | bytes 245768 | tf_op jit(solution)/shard_map/ppermute | solution.py:21
  29.6 4.4 %collective-permute-done.5.above_ref = bf16[10,16,256]{2,1,0:T(8,128)(2,1)S(1)} collective-permute-done((bf16[10,16,256]{2,1,0:T(8,128)(2,1)S(1)}, bf16[10,16,256]{2,1,0:T(8,128)(2,1)S(1)}, u32[]{:S(2)}, u32[]{:S(2)}) %collective-permute-start.5) | collective-permute-done | bytes 81952 | tf_op jit(solution)/shard_map/ppermute | solution.py:21
  34.0 1.7 %copy-done.4 = bf16[2,3,3,256,256]{4,3,2,1,0:T(8,128)(2,1)S(1)} copy-done((bf16[2,3,3,256,256]{4,3,2,1,0:T(8,128)(2,1)S(1)}, bf16[2,3,3,256,256]{4,3,2,1,0:T(8,128)(2,1)}, u32[]{:S(2)}) %copy-start.4) | copy-done | bytes 2359320
  35.7 15.3 %shard_map.115 = (bf16[32,32,256]{2,1,0:T(8,128)(2,1)}, bf16[8,196,256]{2,1,0:T(8,128)(2,1)S(1)}, bf16[8,196,256]{2,1,0:T(8,128)(2,1)S(1)}) custom-call(s32[4]{0:T(128)S(1)} %add_convert_fusion.4.flags_ref, s32[16]{0:T(128)S(1)} %fusion.48.hit_ref, s32[16,14]{1,0:T(8,128)S(1)} %get-tuple-element.40.xa_ref, s32[16,14]{1,0:T(8,128)S(1)} %get-tuple-element.39.xb_ref, ...), custom_call_target="tpu_custom_call" | custom-call | flops 6000000000 | bytes 1000000 | tf_op jit(solution)/shard_map/pallas_call | solution.py:34
  51.0 0.2 copy.31
  51.1 3.1 %collective-permute-start.6 = (bf16[8,196,256]{2,0,1:T(8,128)(2,1)S(1)}, bf16[8,196,256]{2,0,1:T(8,128)(2,1)S(1)}, u32[]{:S(2)}, u32[]{:S(2)}) collective-permute-start(bf16[8,196,256]{2,0,1:T(8,128)(2,1)S(1)} %copy.31), channel_id=1, source_target_pairs={{0,1},{1,0},{2,3},{3,2},{4,5},{5,4},{6,7},{7,6},{8,9},{9,8},{10,11... | collective-permute-start | bytes 2408456 | tf_op jit(solution)/shard_map/ppermute | solution.py:315
  54.3 1.9 %collective-permute-done.6 = bf16[8,196,256]{2,0,1:T(8,128)(2,1)S(1)} collective-permute-done((bf16[8,196,256]{2,0,1:T(8,128)(2,1)S(1)}, bf16[8,196,256]{2,0,1:T(8,128)(2,1)S(1)}, u32[]{:S(2)}, u32[]{:S(2)}) %collective-permute-start.6) | collective-permute-done | bytes 802848 | tf_op jit(solution)/shard_map/ppermute | solution.py:315
  56.2 0.2 slice.86
  56.4 5.6 %collective-permute-start.8 = (bf16[2,196,256]{2,1,0:T(8,128)(2,1)S(1)}, bf16[2,196,256]{2,1,0:T(8,128)(2,1)S(1)}, u32[]{:S(2)}, u32[]{:S(2)}) collective-permute-start(bf16[2,196,256]{2,1,0:T(8,128)(2,1)S(1)} %add_convert_fusion.1), channel_id=1, source_target_pairs={{0,14},{1,3},{2,0},{3,5},{4,2},{5,7},{6,4},{7,9},{8,6},{9,11},{10,... | collective-permute-start | bytes 602120 | tf_op jit(solution)/shard_map/ppermute | solution.py:319
  62.2 1.9 %collective-permute-start.7 = (bf16[3,196,256]{2,1,0:T(8,128)(2,1)S(1)}, bf16[3,196,256]{2,1,0:T(8,128)(2,1)S(1)}, u32[]{:S(2)}, u32[]{:S(2)}) collective-permute-start(bf16[3,196,256]{2,1,0:T(8,128)(2,1)S(1)} %add_convert_fusion), channel_id=1, source_target_pairs={{0,2},{1,15},{2,4},{3,1},{4,6},{5,3},{6,8},{7,5},{8,10},{9,7},{10,... | collective-permute-start | bytes 903176 | tf_op jit(solution)/shard_map/ppermute | solution.py:319
  64.2 0.5 fusion.53
  64.7 1.5 %collective-permute-done.8 = bf16[2,196,256]{2,1,0:T(8,128)(2,1)S(1)} collective-permute-done((bf16[2,196,256]{2,1,0:T(8,128)(2,1)S(1)}, bf16[2,196,256]{2,1,0:T(8,128)(2,1)S(1)}, u32[]{:S(2)}, u32[]{:S(2)}) %collective-permute-start.8) | collective-permute-done | bytes 200736 | tf_op jit(solution)/shard_map/ppermute | solution.py:319
  66.2 6.0 %collective-permute-done.7 = bf16[3,196,256]{2,1,0:T(8,128)(2,1)S(1)} collective-permute-done((bf16[3,196,256]{2,1,0:T(8,128)(2,1)S(1)}, bf16[3,196,256]{2,1,0:T(8,128)(2,1)S(1)}, u32[]{:S(2)}, u32[]{:S(2)}) %collective-permute-start.7) | collective-permute-done | bytes 301088 | tf_op jit(solution)/shard_map/ppermute | solution.py:319
  72.3 3.3 %collective-permute-start.10 = (bf16[196,256]{1,0:T(8,128)(2,1)S(1)}, bf16[196,256]{1,0:T(8,128)(2,1)S(1)}, u32[]{:S(2)}, u32[]{:S(2)}) collective-permute-start(bf16[196,256]{1,0:T(8,128)(2,1)S(1)} %get-tuple-element.27), channel_id=1, source_target_pairs={{0,12},{1,5},{2,14},{3,7},{4,0},{5,9},{6,2},{7,11},{8,4},{9,13},{1... | collective-permute-start | bytes 301064 | tf_op jit(solution)/shard_map/ppermute | solution.py:319
  75.6 2.4 %collective-permute-start.9 = (bf16[196,256]{1,0:T(8,128)(2,1)S(1)}, bf16[196,256]{1,0:T(8,128)(2,1)S(1)}, u32[]{:S(2)}, u32[]{:S(2)}) collective-permute-start(bf16[196,256]{1,0:T(8,128)(2,1)S(1)} %get-tuple-element.26), channel_id=1, source_target_pairs={{0,6},{1,11},{2,8},{3,13},{4,10},{5,15},{6,12},{7,1},{8,14},{9,3},... | collective-permute-start | bytes 301064 | tf_op jit(solution)/shard_map/ppermute | solution.py:319
  78.0 2.2 %collective-permute-done.10 = bf16[196,256]{1,0:T(8,128)(2,1)S(1)} collective-permute-done((bf16[196,256]{1,0:T(8,128)(2,1)S(1)}, bf16[196,256]{1,0:T(8,128)(2,1)S(1)}, u32[]{:S(2)}, u32[]{:S(2)}) %collective-permute-start.10) | collective-permute-done | bytes 100384 | tf_op jit(solution)/shard_map/ppermute | solution.py:319
  80.2 6.1 %collective-permute-done.9 = bf16[196,256]{1,0:T(8,128)(2,1)S(1)} collective-permute-done((bf16[196,256]{1,0:T(8,128)(2,1)S(1)}, bf16[196,256]{1,0:T(8,128)(2,1)S(1)}, u32[]{:S(2)}, u32[]{:S(2)}) %collective-permute-start.9) | collective-permute-done | bytes 100384 | tf_op jit(solution)/shard_map/ppermute | solution.py:319
  86.7 0.4 fusion.5
  87.3 0.2 reshape.189
  87.5 0.3 copy-done.6
  87.8 0.3 fusion.2
  88.0 0.3 copy.41
  88.4 0.9 %reshape.182 = bf16[1,28,28,256]{3,2,1,0:T(8,128)(2,1)} reshape(bf16[14,2,14,2,256]{4,3,2,1,0:T(2,128)(2,1)S(1)} %copy.41) | data formatting | bytes 802816 | tf_op jit(solution)/shard_map/reshape | solution.py:298
  (52 shorter events, 1.8 us)
Async XLA Ops:
  0.6 86.1 %copy-start = (bf16[1,3,3,256,256]{4,3,2,1,0:T(8,128)(2,1)S(1)}, bf16[1,3,3,256,256]{4,3,2,1,0:T(8,128)(2,1)}, u32[]{:S(2)}) copy-start(bf16[1,3,3,256,256]{4,3,2,1,0:T(8,128)(2,1)} %param.15) | copy-start | bytes 3538948
  0.6 33.4 %collective-permute-start.3 = (bf16[32,32,256]{2,1,0:T(8,128)(2,1)}, bf16[32,32,256]{2,1,0:T(8,128)(2,1)S(1)}, u32[]{:S(2)}, u32[]{:S(2)}) collective-permute-start(bf16[32,32,256]{2,1,0:T(8,128)(2,1)} %own_ref.1), channel_id=1, source_target_pairs={{16,0},{32,16},{48,32},{64,48},{80,64},{96,80},{112,96},{128,112},... | collective-permute-start | bytes 1572872 | tf_op jit(solution)/shard_map/ppermute | solution.py:21
  12.0 1.1 %copy-start.1 = (bf16[32,32,256]{2,1,0:T(8,128)(2,1)S(1)}, bf16[32,32,256]{2,1,0:T(8,128)(2,1)}, u32[]{:S(2)}) copy-start(bf16[32,32,256]{2,1,0:T(8,128)(2,1)} %own_ref.1) | copy-start | bytes 1572868
  13.1 15.9 %copy-start.10 = (s32[1,16]{1,0:T(1,128)S(1)}, s32[1,16]{1,0:T(1,128)}, u32[]{:S(2)}) copy-start(s32[1,16]{1,0:T(1,128)} %param.14) | copy-start | bytes 196
  13.1 16.0 %copy-start.7 = (s32[16,4]{0,1:T(4,128)S(1)}, s32[16,4]{0,1:T(4,128)}, u32[]{:S(2)}) copy-start(s32[16,4]{0,1:T(4,128)} %param.13) | copy-start | bytes 772
  13.1 21.0 %copy-start.3 = (bf16[32,32,256]{2,1,0:T(8,128)(2,1)S(1)}, bf16[32,32,256]{2,1,0:T(8,128)(2,1)}, u32[]{:S(2)}) copy-start(bf16[32,32,256]{2,1,0:T(8,128)(2,1)} %own_ref.1) | copy-start | bytes 1572868
  13.1 21.0 %copy-start.5 = (f32[2,256]{1,0:T(2,128)S(1)}, f32[2,256]{1,0:T(2,128)}, u32[]{:S(2)}) copy-start(f32[2,256]{1,0:T(2,128)} %bias_ref.1) | copy-start | bytes 6148
  13.2 3.9 %collective-permute-start = (bf16[2,32,256]{2,1,0:T(8,128)(2,1)S(1)}, bf16[2,32,256]{2,1,0:T(8,128)(2,1)S(1)}, u32[]{:S(2)}, u32[]{:S(2)}) collective-permute-start(bf16[2,32,256]{2,1,0:T(8,128)(2,1)S(1)} %get-tuple-element.14.tail_ref), channel_id=1, source_target_pairs={{0,1},{1,2},{2,3},{3,4},{4,5},{5,6},{6,7},{7,8},{8,9},{9,10},{10,1... | collective-permute-start | bytes 98312 | tf_op jit(solution)/shard_map/ppermute | solution.py:21
  14.8 4.7 %collective-permute-start.1 = (bf16[2,32,256]{2,1,0:T(8,128)(2,1)S(1)}, bf16[2,32,256]{2,1,0:T(8,128)(2,1)S(1)}, u32[]{:S(2)}, u32[]{:S(2)}) collective-permute-start(bf16[2,32,256]{2,1,0:T(8,128)(2,1)S(1)} %get-tuple-element.15.lead_ref), channel_id=1, source_target_pairs={{1,0},{2,1},{3,2},{4,3},{5,4},{6,5},{7,6},{8,7},{9,8},{10,9},{11,1... | collective-permute-start | bytes 98312 | tf_op jit(solution)/shard_map/ppermute | solution.py:21
  19.5 1.0 %copy-start.2 = (bf16[32,32,256]{2,1,0:T(8,128)(2,1)S(1)}, bf16[32,32,256]{2,1,0:T(8,128)(2,1)}, u32[]{:S(2)}) copy-start(bf16[32,32,256]{2,1,0:T(8,128)(2,1)} %own_ref.1) | copy-start | bytes 1572868
  20.6 8.4 %collective-permute-start.2 = (bf16[8,16,256]{2,1,0:T(8,128)(2,1)S(1)}, bf16[8,16,256]{2,1,0:T(8,128)(2,1)S(1)}, u32[]{:S(2)}, u32[]{:S(2)}) collective-permute-start(bf16[8,16,256]{2,1,0:T(8,128)(2,1)S(1)} %get-tuple-element.16), channel_id=1, source_target_pairs={{32,0},{48,16},{64,32},{80,48},{96,64},{112,80},{128,96},{144,112}... | collective-permute-start | bytes 196616 | tf_op jit(solution)/shard_map/ppermute | solution.py:21
  23.1 10.9 %collective-permute-start.4 = (bf16[6,32,256]{2,1,0:T(8,128)(2,1)S(1)}, bf16[6,32,256]{2,1,0:T(8,128)(2,1)S(1)}, u32[]{:S(2)}, u32[]{:S(2)}) collective-permute-start(bf16[6,32,256]{2,1,0:T(8,128)(2,1)S(1)} %get-tuple-element.20.own_sides_ref), channel_id=1, source_target_pairs={{16,0},{32,16},{48,32},{64,48},{80,64},{96,80},{112,96},{128,112},... | collective-permute-start | bytes 294920 | tf_op jit(solution)/shard_map/ppermute | solution.py:21
  25.6 8.4 %collective-permute-start.5 = (bf16[10,16,256]{2,1,0:T(8,128)(2,1)S(1)}, bf16[10,16,256]{2,1,0:T(8,128)(2,1)S(1)}, u32[]{:S(2)}, u32[]{:S(2)}) collective-permute-start(bf16[10,16,256]{2,1,0:T(8,128)(2,1)S(1)} %get-tuple-element.21), channel_id=1, source_target_pairs={{0,16},{16,32},{32,48},{48,64},{64,80},{80,96},{96,112},{112,128},... | collective-permute-start | bytes 245768 | tf_op jit(solution)/shard_map/ppermute | solution.py:21
  34.0 1.7 %copy-start.4 = (bf16[2,3,3,256,256]{4,3,2,1,0:T(8,128)(2,1)S(1)}, bf16[2,3,3,256,256]{4,3,2,1,0:T(8,128)(2,1)}, u32[]{:S(2)}) copy-start(bf16[2,3,3,256,256]{4,3,2,1,0:T(8,128)(2,1)} %param.11) | copy-start | bytes 7077892
  51.1 5.0 %collective-permute-start.6 = (bf16[8,196,256]{2,0,1:T(8,128)(2,1)S(1)}, bf16[8,196,256]{2,0,1:T(8,128)(2,1)S(1)}, u32[]{:S(2)}, u32[]{:S(2)}) collective-permute-start(bf16[8,196,256]{2,0,1:T(8,128)(2,1)S(1)} %copy.31), channel_id=1, source_target_pairs={{0,1},{1,0},{2,3},{3,2},{4,5},{5,4},{6,7},{7,6},{8,9},{9,8},{10,11... | collective-permute-start | bytes 2408456 | tf_op jit(solution)/shard_map/ppermute | solution.py:315
  56.4 9.7 %collective-permute-start.8 = (bf16[2,196,256]{2,1,0:T(8,128)(2,1)S(1)}, bf16[2,196,256]{2,1,0:T(8,128)(2,1)S(1)}, u32[]{:S(2)}, u32[]{:S(2)}) collective-permute-start(bf16[2,196,256]{2,1,0:T(8,128)(2,1)S(1)} %add_convert_fusion.1), channel_id=1, source_target_pairs={{0,14},{1,3},{2,0},{3,5},{4,2},{5,7},{6,4},{7,9},{8,6},{9,11},{10,... | collective-permute-start | bytes 602120 | tf_op jit(solution)/shard_map/ppermute | solution.py:319
  62.2 10.0 %collective-permute-start.7 = (bf16[3,196,256]{2,1,0:T(8,128)(2,1)S(1)}, bf16[3,196,256]{2,1,0:T(8,128)(2,1)S(1)}, u32[]{:S(2)}, u32[]{:S(2)}) collective-permute-start(bf16[3,196,256]{2,1,0:T(8,128)(2,1)S(1)} %add_convert_fusion), channel_id=1, source_target_pairs={{0,2},{1,15},{2,4},{3,1},{4,6},{5,3},{6,8},{7,5},{8,10},{9,7},{10,... | collective-permute-start | bytes 903176 | tf_op jit(solution)/shard_map/ppermute | solution.py:319
  72.3 14.4 %copy-start.11 = (pred[8,2]{0,1:T(4,128)(4,1)S(1)}, pred[8,2]{0,1:T(4,128)(4,1)}, u32[]{:S(2)}) copy-start(pred[8,2]{0,1:T(4,128)(4,1)} %constant.96) | copy-start | bytes 52
  72.3 7.9 %collective-permute-start.10 = (bf16[196,256]{1,0:T(8,128)(2,1)S(1)}, bf16[196,256]{1,0:T(8,128)(2,1)S(1)}, u32[]{:S(2)}, u32[]{:S(2)}) collective-permute-start(bf16[196,256]{1,0:T(8,128)(2,1)S(1)} %get-tuple-element.27), channel_id=1, source_target_pairs={{0,12},{1,5},{2,14},{3,7},{4,0},{5,9},{6,2},{7,11},{8,4},{9,13},{1... | collective-permute-start | bytes 301064 | tf_op jit(solution)/shard_map/ppermute | solution.py:319
  75.6 10.8 %collective-permute-start.9 = (bf16[196,256]{1,0:T(8,128)(2,1)S(1)}, bf16[196,256]{1,0:T(8,128)(2,1)S(1)}, u32[]{:S(2)}, u32[]{:S(2)}) collective-permute-start(bf16[196,256]{1,0:T(8,128)(2,1)S(1)} %get-tuple-element.26), channel_id=1, source_target_pairs={{0,6},{1,11},{2,8},{3,13},{4,10},{5,15},{6,12},{7,1},{8,14},{9,3},... | collective-permute-start | bytes 301064 | tf_op jit(solution)/shard_map/ppermute | solution.py:319
  86.7 1.0 %copy-start.6 = (bf16[2,2,256,256]{3,2,1,0:T(8,128)(2,1)S(1)}, bf16[2,2,256,256]{3,2,1,0:T(8,128)(2,1)}, u32[]{:S(2)}) copy-start(bf16[2,2,256,256]{3,2,1,0:T(8,128)(2,1)} %param.17) | copy-start | bytes 1572868
  86.7 1.0 %copy-start.8 = (f32[256]{0:T(256)S(1)}, f32[256]{0:T(256)}, u32[]{:S(2)}) copy-start(f32[256]{0:T(256)} %param.18) | copy-start | bytes 3076
  86.7 1.0 %copy-start.9 = (f32[1,256]{1,0:T(1,128)S(1)}, f32[1,256]{1,0:T(1,128)}, u32[]{:S(2)}) copy-start(f32[1,256]{1,0:T(1,128)} %param.16) | copy-start | bytes 3076

commit v3 on v2

v3 whole, which is shorter than its diff:
```python
import jax
import jax.numpy as jnp
from jax import lax
from jax.experimental import pallas as pl
from jax.experimental.pallas import tpu as pltpu
from jax.sharding import PartitionSpec as P

POOL = 14
SIDE = 16
LANES = 128
TILE = 16
FIRST = 33
SECOND = 32
HOPS = (4, 1, -1, 2, -3, 3, -2, 0)
F32 = jnp.float32
BF16 = jnp.bfloat16


def shift(value, axis, step):
    devices = range(lax.axis_size(axis))
    return lax.ppermute(value, axis, [(i, i + step) for i in devices if i + step in devices])


def call(kernel, out_shape, in_specs, scratch, limit, flops, *args):
    vmem = pl.BlockSpec(memory_space=pltpu.VMEM)
    return pl.pallas_call(
        kernel,
        out_shape=out_shape,
        in_specs=in_specs,
        out_specs=tuple(vmem for _ in out_shape),
        scratch_shapes=scratch,
        compiler_params=pltpu.CompilerParams(vmem_limit_bytes=limit * 2**20),
        cost_estimate=pl.CostEstimate(flops=flops, bytes_accessed=10**6, transcendentals=0),
    )(*args)


def columns_kernel(tile_ref, lead_ref, tail_ref, rim_ref, flat_ref):
    rows, width, channels = tile_ref.shape
    for out_ref, first, start in ((lead_ref, 0, 0), (tail_ref, TILE - 2, width - TILE)):
        block = tile_ref[:, pl.ds(start, TILE), :].astype(F32).reshape(rows * TILE, channels)
        for h in range(channels // LANES):
            flat_ref[h] = block[:, h * LANES : (h + 1) * LANES]
        for x in range(2):
            here = pl.ds(first + x, rows, stride=TILE)
            column = [flat_ref[h, here, :] for h in range(channels // LANES)]
            out_ref[x] = jnp.concatenate(column, axis=1).astype(BF16)
    whole = width // TILE
    rim_ref[0 : 2 * whole] = tile_ref[rows - 2 : rows].reshape(2 * whole, TILE, channels)
    rim_ref[2 * whole :] = tile_ref[0:1].reshape(whole, TILE, channels)


def down_kernel(rim_ref, left_ref, right_ref, lead_ref, tail_ref, down_ref):
    rows = left_ref.shape[1]
    parts = (left_ref, left_ref, lead_ref, tail_ref, right_ref, right_ref)
    count = down_ref.shape[0] - len(parts)
    down_ref[0:count] = rim_ref[0:count]
    for i, part in enumerate(parts):
        down_ref[count + i] = part[i % 2, rows - TILE : rows]


def up_kernel(rim_ref, left_ref, right_ref, lead_ref, tail_ref, sides_ref, up_ref):
    parts = (left_ref, left_ref, lead_ref, tail_ref, right_ref, right_ref)
    count = up_ref.shape[0] - len(parts)
    up_ref[0:count] = rim_ref[2 * count : 3 * count]
    for i, part in enumerate(parts):
        sides_ref[i] = part[i % 2]
        up_ref[count + i] = part[i % 2, 0:TILE]


def exchange(features, later):
    rows, cols, channels = features.shape
    vmem = pl.BlockSpec(memory_space=pltpu.VMEM)
    below = shift(features, "row", -1)
    whole = cols // TILE
    pair = jax.ShapeDtypeStruct((2, rows, channels), BF16)
    rim = jax.ShapeDtypeStruct((3 * whole, TILE, channels), BF16)
    lead, tail, rim = call(
        columns_kernel, (pair, pair, rim), [vmem],
        [pltpu.VMEM((channels // LANES, rows * TILE, LANES), F32)], 4, 10**5, features,
    )
    left = shift(tail, "col", 1)
    right = shift(lead, "col", -1)
    strips = (rim, left, right, lead, tail)
    (to_down,) = call(
        down_kernel, (jax.ShapeDtypeStruct((2 * whole + 6, TILE, channels), BF16),),
        [vmem] * 5, [], 4, 10**5, *strips,
    )
    above, later = lax.optimization_barrier((shift(to_down, "row", 1), later))
    sides_shape = jax.ShapeDtypeStruct((6, rows, channels), BF16)
    up_shape = jax.ShapeDtypeStruct((whole + 6, TILE, channels), BF16)
    own_sides, to_up = call(
        up_kernel, (sides_shape, up_shape), [vmem] * 5, [], 4, 10**5, *strips
    )
    sides = shift(own_sides, "row", -1)
    after = shift(to_up, "row", -2)
    return below, own_sides, sides, above, after, later


def sample(lower, extent):
    lower_f = lower.astype(F32)[:, None]
    extent_f = extent.astype(F32)[:, None]
    bins = jnp.arange(POOL).astype(F32)[None, :]
    centre = lower_f + (bins + 0.5) * extent_f / POOL - 0.5
    return jnp.clip(centre, lower_f, lower_f + extent_f - 1.0)


def spread(dst, start, value, edge_ref, sides, offset):
    count, width, channels = value.shape
    place = lax.broadcasted_iota(jnp.int32, (width, channels), 0)
    for k in range(count):
        line = value[k].astype(F32)
        low = edge_ref[sides[0], pl.ds(offset + k, 1), :]
        high = edge_ref[sides[1], pl.ds(offset + k, 1), :]
        before = jnp.where(place == 0, low, pltpu.roll(line, 1, 0))
        after = jnp.where(place == width - 1, high, pltpu.roll(line, width - 1, 0))
        dst[start + k, :, 0:channels] = before.astype(BF16)
        dst[start + k, :, channels : 2 * channels] = line.astype(BF16)
        dst[start + k, :, 2 * channels : 3 * channels] = after.astype(BF16)


def taps(src, start, count, weight, bias):
    width, depth = src.shape[1:]
    parts = [src[pl.ds(start + d, count)].reshape(count * width, depth) for d in range(3)]
    out = jnp.dot(jnp.concatenate(parts, axis=1), weight, preferred_element_type=F32)
    out = jnp.maximum(out + bias, 0.0)
    return out.reshape(count, width, out.shape[-1])


def main_kernel(
    flags_ref, hit_ref, at_ref, by_ref,
    own_ref, below_ref, own_sides_ref, sides_ref, above_ref, after_ref,
    weight_ref, bias_ref,
    tower_ref, mine_ref, other_ref,
    wide_ref, mid_ref, band_ref, comb_ref, patch_ref, strip_ref, inner_ref,
):
    rows, width, channels = own_ref.shape
    half = mine_ref.shape[0]
    whole = width // TILE
    for c in range(6):
        strip_ref[c, 0:2, :] = above_ref[2 * whole + c].astype(F32)[TILE - 2 : TILE]
        strip_ref[c, 2 : rows + 2, :] = own_sides_ref[c].astype(F32)
        strip_ref[c, rows + 2 : 2 * rows + 2, :] = sides_ref[c].astype(F32)
        strip_ref[c, 2 * rows + 2 : 2 * rows + 3, :] = after_ref[whole + c].astype(F32)[0:1]
        tail = strip_ref.shape[1] - (2 * rows + 3)
        strip_ref[c, 2 * rows + 3 :, :] = jnp.zeros((tail, channels), F32)
    spread(wide_ref, 0, above_ref[0 : 2 * whole].reshape(2, width, channels), strip_ref, (1, 4), 0)
    step = 8
    for part, base in ((own_ref, 2), (below_ref, 2 + rows)):
        def fill(i, carry):
            at = i * step
            spread(wide_ref, base + at, part[pl.ds(at, step)], strip_ref, (1, 4), base + at)
            return carry

        lax.fori_loop(0, rows // step, fill, 0)
    last = 2 + 2 * rows
    spread(wide_ref, last, after_ref[0:whole].reshape(1, width, channels), strip_ref, (1, 4), last)
    wide_ref[3 + 2 * rows] = jnp.zeros(wide_ref.shape[1:], BF16)

    tall = inner_ref.shape[1]
    sides = []
    for side in range(2):
        parts = [
            strip_ref[3 * side + dx, dy : dy + tall, :].astype(BF16)
            for dy in range(3)
            for dx in range(3)
        ]
        sides.append(jnp.concatenate(parts, axis=1))
    out = jnp.dot(jnp.concatenate(sides, axis=0), weight_ref[0], preferred_element_type=F32)
    out = jnp.maximum(out + bias_ref[0:1], 0.0).astype(BF16).astype(F32)
    for side in range(2):
        part = out[side * tall : (side + 1) * tall]
        inner_ref[side] = jnp.where(flags_ref[2 + side] > 0, part, 0.0)

    def first(i, carry):
        at = i * FIRST
        out = taps(wide_ref, at, FIRST, weight_ref[0], bias_ref[0:1])
        spread(mid_ref, at, out.astype(BF16), inner_ref, (0, 1), at)
        return carry

    lax.fori_loop(0, (2 * rows + 2) // FIRST, first, 0)
    blank = jnp.zeros(mid_ref.shape[1:], BF16)

    @pl.when(flags_ref[0] > 0)
    def _():
        mid_ref[0] = blank

    @pl.when(flags_ref[1] > 0)
    def _():
        mid_ref[rows + 1] = blank
    mid_ref[2 * rows + 1] = blank

    def second(i, carry):
        at = i * SECOND
        out = taps(mid_ref, at, SECOND, weight_ref[1], bias_ref[1:2])

        @pl.when(at < rows)
        def _():
            tower_ref[pl.ds(at, SECOND)] = out.astype(BF16)

        band_ref[pl.ds(at, SECOND)] = out.astype(BF16).astype(F32)
        return carry

    lax.fori_loop(0, 2 * rows // SECOND, second, 0)
    halves = [(h, slice(h * LANES, (h + 1) * LANES)) for h in range(channels // LANES)]
    for side, out_ref in ((1, other_ref), (0, mine_ref)):
        def region(m, carry):
            n = m + side * half

            @pl.when(hit_ref[n] > 0)
            def _():
                for p in range(POOL):
                    line = band_ref[at_ref[0, n, p]] * by_ref[0, n, p]
                    line = line + band_ref[at_ref[1, n, p]] * by_ref[1, n, p]
                    for h, lanes in halves:
                        comb_ref[h, pl.ds(p, width, stride=SIDE), :] = line[:, lanes]
                for q in range(POOL):
                    low = pl.ds(pl.multiple_of(at_ref[2, n, q] * SIDE, SIDE), SIDE)
                    high = pl.ds(pl.multiple_of(at_ref[3, n, q] * SIDE, SIDE), SIDE)
                    for h, lanes in halves:
                        total = comb_ref[h, low, :] * by_ref[2, n, q]
                        total = total + comb_ref[h, high, :] * by_ref[3, n, q]
                        patch_ref[h, pl.ds(q, SIDE, stride=POOL), :] = total
                for h, lanes in halves:
                    out_ref[m, :, lanes] = patch_ref[h, pl.ds(0, POOL * POOL), :].astype(BF16)

            @pl.when(hit_ref[n] == 0)
            def _():
                out_ref[m] = jnp.zeros(out_ref.shape[1:], BF16)

            return carry

        lax.fori_loop(0, half, region, 0)


def taps_of(boxes, rows, cols):
    row_first = lax.axis_index("row") * rows
    col_first = lax.axis_index("col") * cols
    at, by = [], []
    for dim, start, size in ((0, row_first, 2 * rows), (1, col_first, cols)):
        centre = sample(boxes[:, dim], boxes[:, dim + 2])
        low = jnp.floor(centre)
        for place in (low, low + 1.0):
            weight = jnp.maximum(1.0 - jnp.abs(place - centre), 0.0).astype(BF16).astype(F32)
            index = place.astype(jnp.int32) - start
            at.append(jnp.clip(index, 0, size - 1))
            by.append(jnp.where((index >= 0) & (index < size), weight, 0.0))
    hit = (boxes[:, 1] < col_first + cols) & (boxes[:, 1] + boxes[:, 3] > col_first)
    return hit.astype(jnp.int32), jnp.stack(at), jnp.stack(by)


def stage_kernel(src_ref, dst_ref, sem):
    load = pltpu.make_async_copy(src_ref, dst_ref, sem)
    load.start()
    load.wait()


def tower_and_pool(features, weight, bias, boxes, owner_slot, wanted):
    rows, cols, channels = features.shape
    below, own_sides, sides, above, after, (boxes, owner_slot, wanted, weight) = exchange(
        features, (boxes, owner_slot, wanted, weight.reshape(2, -1, weight.shape[-1]))
    )
    (weight,) = call(
        stage_kernel, (jax.ShapeDtypeStruct(weight.shape, BF16),),
        [pl.BlockSpec(memory_space=pl.ANY)], [pltpu.SemaphoreType.DMA], 4, 10**5, weight,
    )
    row, col = lax.axis_index("row"), lax.axis_index("col")
    last_row, last_col = lax.axis_size("row") - 1, lax.axis_size("col") - 1
    flags = jnp.stack([row == 0, row == last_row, col > 0, col < last_col]).astype(jnp.int32)
    picked = (owner_slot[0][None, :] == wanted[:, None]).astype(jnp.int32)
    boxes = jnp.sum(picked[:, :, None] * boxes[None, :, :], axis=1)
    hit, at, by = taps_of(boxes, rows, cols)
    count = boxes.shape[0]
    smem = pl.BlockSpec(memory_space=pltpu.SMEM)
    vmem = pl.BlockSpec(memory_space=pltpu.VMEM)
    patches = jax.ShapeDtypeStruct((count // 2, POOL * POOL, channels), BF16)
    return call(
        main_kernel,
        (jax.ShapeDtypeStruct(features.shape, BF16), patches, patches),
        [smem] * 4 + [vmem] * 8,
        [
            pltpu.VMEM((2 * rows + 4, cols, 3 * channels), BF16),
            pltpu.VMEM((2 * rows + 2, cols, 3 * channels), BF16),
            pltpu.VMEM((2 * rows, cols, channels), F32),
            pltpu.VMEM((channels // LANES, cols * SIDE, LANES), F32),
            pltpu.VMEM((channels // LANES, SIDE * SIDE, LANES), F32),
            pltpu.VMEM((6, 2 * rows + 24, channels), F32),
            pltpu.VMEM((2, 2 * rows + 16, channels), F32),
        ],
        40, 6 * 10**9,
        flags, hit, at, by, features, below, own_sides, sides, above, after,
        weight, bias,
    )


def head_kernel(
    mine_ref, swapped_ref, ahead_ref, three_ref, two_ref,
    weight_ref, bias_ref, lift_ref, shade_ref,
    out_ref, sum_ref, wide_ref, row_ref,
):
    channels = bias_ref.shape[-1]
    halves = [(h, slice(h * LANES, (h + 1) * LANES)) for h in range(channels // LANES)]
    parts = (mine_ref[7], swapped_ref[7], ahead_ref[1], three_ref[...], two_ref[...])
    pooled = sum(part.astype(F32) for part in parts).astype(BF16).astype(F32)
    for h, lanes in halves:
        sum_ref[h, 8 : 8 + POOL * POOL, :] = pooled[:, lanes]
    blank = jnp.zeros(wide_ref.shape[1:], BF16)
    wide_ref[0] = blank
    wide_ref[POOL + 1] = blank
    place = lax.broadcasted_iota(jnp.int32, (SIDE, LANES), 0)
    for p in range(POOL):
        for d in range(3):
            kept = (place + d - 1 >= 0) & (place + d - 1 < POOL)
            for h in range(channels // LANES):
                value = sum_ref[h, pl.ds(8 + POOL * p + d - 1, SIDE), :]
                first = d * channels + h * LANES
                wide_ref[p + 1, :, first : first + LANES] = jnp.where(kept, value, 0.0).astype(BF16)
    hidden = taps(wide_ref, 0, POOL, weight_ref[...], bias_ref[...]).astype(BF16)
    hidden = hidden.reshape(POOL * SIDE, channels)
    for u in range(2):
        lifted = []
        for v in range(2):
            value = jnp.dot(hidden, lift_ref[2 * u + v], preferred_element_type=F32)
            lifted.append(jnp.maximum(value + shade_ref[...], 0.0))
        for a in range(POOL):
            for v in range(2):
                for h, lanes in halves:
                    row_ref[a, h, pl.ds(v, SIDE, stride=2), :] = lifted[v][
                        a * SIDE : (a + 1) * SIDE, lanes
                    ]
            for h, lanes in halves:
                out_ref[0, 2 * a + u, :, lanes] = row_ref[a, h, 0 : 2 * POOL, :].astype(BF16)


def head(parts, mask_weight, mask_bias, deconv_weight, deconv_bias):
    channels = mask_bias.shape[-1]
    vmem = pl.BlockSpec(memory_space=pltpu.VMEM)
    side = 2 * POOL
    (masks,) = call(
        head_kernel,
        (jax.ShapeDtypeStruct((1, side, side, channels), BF16),),
        [vmem] * 9,
        [
            pltpu.VMEM((channels // LANES, 8 + SIDE * SIDE, LANES), F32),
            pltpu.VMEM((SIDE, SIDE, 3 * channels), BF16),
            pltpu.VMEM((POOL, channels // LANES, 2 * SIDE, LANES), F32),
        ],
        16, 10**9,
        *parts, mask_weight.reshape(9 * channels, channels), mask_bias,
        deconv_weight.reshape(4, channels, channels), deconv_bias.reshape(1, channels),
    )
    return masks


def per_device(
    features, tower_weight, tower_bias, boxes, owner_slot,
    mask_weight, mask_bias, deconv_weight, deconv_bias,
):
    peers = lax.axis_size("col")
    chips = peers // 2
    core = lax.axis_index("col") % 2
    chip = lax.axis_index("col") // 2
    hops = jnp.array(HOPS * 2, dtype=jnp.int32)
    sides = jnp.repeat(jnp.stack([core, 1 - core]), chips)
    wanted = 2 * ((chip + hops * (1 - 2 * sides)) % chips) + sides
    tower, mine, other = tower_and_pool(
        features, tower_weight, tower_bias, boxes, owner_slot, wanted
    )
    swapped = lax.ppermute(other, "col", [(i, i ^ 1) for i in range(peers)])

    def send(value, hop):
        steps = [2 * hop * (1 - 2 * (i % 2)) for i in range(peers)]
        return lax.ppermute(value, "col", [(i, (i + steps[i]) % peers) for i in range(peers)])

    def total(*parts):
        parts = [part.astype(F32) for part in parts]
        return sum(parts[1:], parts[0]).astype(BF16)

    ahead = send(total(mine[0:3], swapped[0:3]), 1)
    back = send(total(mine[3:5], swapped[3:5]), -1)
    three = send(total(mine[5], swapped[5], ahead[0], back[0]), 3)
    two = send(total(mine[6], swapped[6], ahead[2], back[1]), -2)
    parts = (mine, swapped, ahead, three, two)
    masks = head(parts, mask_weight, mask_bias, deconv_weight, deconv_bias)
    return tower, masks


def solution(mesh):
    placed = (P("row", "col", None), P(), P(), P("row", None), P("row", None), P(), P(), P(), P())
    return jax.shard_map(
        per_device,
        mesh=mesh,
        in_specs=placed,
        out_specs=(P("row", "col", None), P(("row", "col"), None, None, None)),
        check_vma=False,
    )
```

time: 89.9 us -> 81.4 us (0.905)
  waiting for transfers between devices: 24.7 us -> 16 us
  starting transfers between devices: 38.8 us -> 45.5 us
  local copies, waits for them, and re-layouts: 6.96 us -> 3.32 us
  Pallas kernels: 15.4 us -> 12.2 us
  other arithmetic: 1.66 us -> 2.86 us
    ppermute x4, waiting for transfers between devices: 15.9 us -> 11.1 us  [send(): lax.ppermute(value, 'col', [(i, (i + steps[i]) % peers) for i in range(pe...]
    ppermute x4, starting transfers between devices: 13.2 us -> 17.3 us  [send(): lax.ppermute(value, 'col', [(i, (i + steps[i]) % peers) for i in range(pe...]
    ppermute x6, waiting for transfers between devices: 6.93 us -> 2.98 us  [shift(): lax.ppermute(value, axis, [(i, i + step) for i in devices if i + step in...]
    pallas_call x3 -> x6, Pallas kernels: 15.4 us -> 12.2 us  [call(): pl.pallas_call(kernel, out_shape=out_shape, in_specs=in_specs, out_specs=...]
    ppermute x6, starting transfers between devices: 22.5 us -> 23.8 us  [shift(): lax.ppermute(value, axis, [(i, i + step) for i in devices if i + step in...]
    ppermute x1, starting transfers between devices: 3.13 us -> 4.41 us  [per_device(): swapped = lax.ppermute(other, 'col', [(i, i ^ 1) for i in range(peers)])]
    unnamed x24 -> x16, local copies, waits for them, and re-layouts: 4.06 us -> 2.85 us
    reshape x3 -> x0, local copies, waits for them, and re-layouts: 0.99 us -> none  [the longest x1 0.92 us: head(): return lifted.reshape(1, 2 * POOL, 2 * POOL, -1)]
  transfers between devices with their start and end apart: 11 -> 11, of which waited for: 7 -> 5; matrix products, arithmetic and copies ran while one was open for 2% -> 3% of each run, Pallas kernels for 0% -> 0%
where the time goes in v3:
time: 81.4 us; the launch traced here: 80.8 us
  starting transfers between devices  45.5 us (56%)
  waiting for transfers between devices  16 us (20%)
  Pallas kernels  12.2 us (15%)
  local copies, waits for them, and re-layouts  3.32 us (4%)
  other arithmetic  2.86 us (4%)
  between operations  0.94 us (1%)
    ppermute x6, starting transfers between devices, shift(): lax.ppermute(value, axis, [(i, i + step) for i in devices if i + step in...  23.8 us
    ppermute x4, starting transfers between devices, send(): lax.ppermute(value, 'col', [(i, (i + steps[i]) % peers) for i in range(pe...  17.3 us
    pallas_call x6, Pallas kernels, call(): pl.pallas_call(kernel, out_shape=out_shape, in_specs=in_specs, out_specs=...  12.2 us
    ppermute x4, waiting for transfers between devices, send(): lax.ppermute(value, 'col', [(i, (i + steps[i]) % peers) for i in range(pe...  11.1 us
    ppermute x1, starting transfers between devices, per_device(): swapped = lax.ppermute(other, 'col', [(i, i ^ 1) for i in range(peers)])  4.41 us
    ppermute x6, waiting for transfers between devices, shift(): lax.ppermute(value, axis, [(i, i + step) for i in devices if i + step in...  2.98 us
    unnamed x16, local copies, waits for them, and re-layouts  2.85 us
    ppermute x1, waiting for transfers between devices, per_device(): swapped = lax.ppermute(other, 'col', [(i, i ^ 1) for i in range(peers)])  1.91 us
  transfers between devices with their start and end apart: 11, of which 5 were waited for; matrix products, arithmetic and copies ran while one was open for 3% of the time, Pallas kernels for 0%

profile of v3, /device:TPU:6, one launch (start us, length us, event | category | flops | bytes accessed | tf_op | source)
XLA Modules:
  0.0 80.8 jit_solution(17033912601837940301)
XLA Ops:
  0.6 11.2 %collective-permute-start.3 = (bf16[32,32,256]{2,1,0:T(8,128)(2,1)}, bf16[32,32,256]{2,1,0:T(8,128)(2,1)S(1)}, u32[]{:S(2)}, u32[]{:S(2)}) collective-permute-start(bf16[32,32,256]{2,1,0:T(8,128)(2,1)} %own_ref.1), channel_id=1, source_target_pairs={{16,0},{32,16},{48,32},{64,48},{80,64},{96,80},{112,96},{128,112},... | collective-permute-start | bytes 1572872 | tf_op jit(solution)/shard_map/ppermute | solution.py:21
  11.9 1.0 %copy-done.3 = bf16[32,32,256]{2,1,0:T(8,128)(2,1)S(1)} copy-done((bf16[32,32,256]{2,1,0:T(8,128)(2,1)S(1)}, bf16[32,32,256]{2,1,0:T(8,128)(2,1)}, u32[]{:S(2)}) %copy-start.3) | copy-done | bytes 524312
  12.9 0.1 shard_map.113
  13.0 1.5 %collective-permute-start = (bf16[2,32,256]{2,1,0:T(8,128)(2,1)S(1)}, bf16[2,32,256]{2,1,0:T(8,128)(2,1)S(1)}, u32[]{:S(2)}, u32[]{:S(2)}) collective-permute-start(bf16[2,32,256]{2,1,0:T(8,128)(2,1)S(1)} %get-tuple-element.16.tail_ref), channel_id=1, source_target_pairs={{0,1},{1,2},{2,3},{3,4},{4,5},{5,6},{6,7},{7,8},{8,9},{9,10},{10,1... | collective-permute-start | bytes 98312 | tf_op jit(solution)/shard_map/ppermute | solution.py:21
  14.5 1.3 %collective-permute-start.1 = (bf16[2,32,256]{2,1,0:T(8,128)(2,1)S(1)}, bf16[2,32,256]{2,1,0:T(8,128)(2,1)S(1)}, u32[]{:S(2)}, u32[]{:S(2)}) collective-permute-start(bf16[2,32,256]{2,1,0:T(8,128)(2,1)S(1)} %get-tuple-element.17.lead_ref), channel_id=1, source_target_pairs={{1,0},{2,1},{3,2},{4,3},{5,4},{6,5},{7,6},{8,7},{9,8},{10,9},{11,1... | collective-permute-start | bytes 98312 | tf_op jit(solution)/shard_map/ppermute | solution.py:21
  15.9 0.1 reshape.1352
  16.0 0.7 fusion.37
  16.7 2.5 %collective-permute-done.1.right_ref = bf16[2,32,256]{2,1,0:T(8,128)(2,1)S(1)} collective-permute-done((bf16[2,32,256]{2,1,0:T(8,128)(2,1)S(1)}, bf16[2,32,256]{2,1,0:T(8,128)(2,1)S(1)}, u32[]{:S(2)}, u32[]{:S(2)}) %collective-permute-start.1) | collective-permute-done | bytes 32800 | tf_op jit(solution)/shard_map/ppermute | solution.py:21
  19.2 1.9 %collective-permute-start.2 = (bf16[10,16,256]{2,1,0:T(8,128)(2,1)S(1)}, bf16[10,16,256]{2,1,0:T(8,128)(2,1)S(1)}, u32[]{:S(2)}, u32[]{:S(2)}) collective-permute-start(bf16[10,16,256]{2,1,0:T(8,128)(2,1)S(1)} %shard_map.114), channel_id=1, source_target_pairs={{0,16},{16,32},{32,48},{48,64},{64,80},{80,96},{96,112},{112,128},... | collective-permute-start | bytes 245768 | tf_op jit(solution)/shard_map/ppermute | solution.py:21
  21.2 3.9 %collective-permute-start.5 = (bf16[8,16,256]{2,1,0:T(8,128)(2,1)S(1)}, bf16[8,16,256]{2,1,0:T(8,128)(2,1)S(1)}, u32[]{:S(2)}, u32[]{:S(2)}) collective-permute-start(bf16[8,16,256]{2,1,0:T(8,128)(2,1)S(1)} %get-tuple-element.23), channel_id=1, source_target_pairs={{32,0},{48,16},{64,32},{80,48},{96,64},{112,80},{128,96},{144,112}... | collective-permute-start | bytes 196616 | tf_op jit(solution)/shard_map/ppermute | solution.py:21
  25.2 4.0 %collective-permute-start.4 = (bf16[6,32,256]{2,1,0:T(8,128)(2,1)S(1)}, bf16[6,32,256]{2,1,0:T(8,128)(2,1)S(1)}, u32[]{:S(2)}, u32[]{:S(2)}) collective-permute-start(bf16[6,32,256]{2,1,0:T(8,128)(2,1)S(1)} %get-tuple-element.21.own_sides_ref), channel_id=1, source_target_pairs={{16,0},{32,16},{48,32},{64,48},{80,64},{96,80},{112,96},{128,112},... | collective-permute-start | bytes 294920 | tf_op jit(solution)/shard_map/ppermute | solution.py:21
  29.2 0.7 compare_convert_fusion
  29.9 0.8 %multiply_reduce_fusion = s32[16,4]{0,1:T(4,128)S(1)} fusion(s32[16,4]{0,1:T(4,128)} %param.13, s32[16,16]{1,0:T(8,128)S(1)} %compare_convert_fusion), kind=kLoop, calls=%fused_computation.8 | loop fusion | flops 1984 | bytes 1536 | tf_op jit(solution)/shard_map/reduce_sum | solution.py:270
  30.8 1.7 %copy-done = bf16[2,3,3,256,256]{4,3,2,1,0:T(8,128)(2,1)S(1)} copy-done((bf16[2,3,3,256,256]{4,3,2,1,0:T(8,128)(2,1)S(1)}, bf16[2,3,3,256,256]{4,3,2,1,0:T(8,128)(2,1)}, u32[]{:S(2)}) %copy-start) | copy-done | bytes 2359320
  32.5 0.2 shard_map.116.weight_ref
  32.6 0.1 convert_select_fusion.3
  32.8 0.1 fusion.31
  32.9 0.5 collective-permute-done.4.sides_ref
  33.4 0.1 copy-done.4
  33.5 10.2 %shard_map.117 = (bf16[32,32,256]{2,1,0:T(8,128)(2,1)}, bf16[8,196,256]{2,1,0:T(8,128)(2,1)S(1)}, bf16[8,196,256]{2,1,0:T(8,128)(2,1)S(1)}) custom-call(s32[4]{0:T(128)S(1)} %add_convert_fusion.4.flags_ref, s32[16]{0:T(128)S(1)} %fusion.39.hit_ref, s32[4,16,14]{2,1,0:T(8,128)S(1)} %pad_add_fusion.at_ref, f32[4,16,14]{2,1,0:T(8,128)S(1)} %pad_maximum_fusion.by_ref, ...), custom_call_target="tpu_custom_call" | custom-call | flops 6000000000 | bytes 1000000 | tf_op jit(solution)/shard_map/pallas_call | solution.py:26
  43.7 0.2 copy.20
  43.9 4.4 %collective-permute-start.6 = (bf16[8,196,256]{2,0,1:T(8,128)(2,1)S(1)}, bf16[8,196,256]{2,0,1:T(8,128)(2,1)S(1)}, u32[]{:S(2)}, u32[]{:S(2)}) collective-permute-start(bf16[8,196,256]{2,0,1:T(8,128)(2,1)S(1)} %copy.20), channel_id=1, source_target_pairs={{0,1},{1,0},{2,3},{3,2},{4,5},{5,4},{6,7},{7,6},{8,9},{9,8},{10,11... | collective-permute-start | bytes 2408456 | tf_op jit(solution)/shard_map/ppermute | solution.py:368
  48.3 1.9 %collective-permute-done.6 = bf16[8,196,256]{2,0,1:T(8,128)(2,1)S(1)} collective-permute-done((bf16[8,196,256]{2,0,1:T(8,128)(2,1)S(1)}, bf16[8,196,256]{2,0,1:T(8,128)(2,1)S(1)}, u32[]{:S(2)}, u32[]{:S(2)}) %collective-permute-start.6) | collective-permute-done | bytes 802848 | tf_op jit(solution)/shard_map/ppermute | solution.py:368
  50.2 0.2 copy.25.swapped_ref
  50.5 3.5 %collective-permute-start.7 = (bf16[3,196,256]{2,1,0:T(8,128)(2,1)S(1)}, bf16[3,196,256]{2,1,0:T(8,128)(2,1)S(1)}, u32[]{:S(2)}, u32[]{:S(2)}) collective-permute-start(bf16[3,196,256]{2,1,0:T(8,128)(2,1)S(1)} %add_convert_fusion), channel_id=1, source_target_pairs={{0,2},{1,15},{2,4},{3,1},{4,6},{5,3},{6,8},{7,5},{8,10},{9,7},{10,... | collective-permute-start | bytes 903176 | tf_op jit(solution)/shard_map/ppermute | solution.py:372
  54.0 3.6 %collective-permute-start.8 = (bf16[2,196,256]{2,1,0:T(8,128)(2,1)S(1)}, bf16[2,196,256]{2,1,0:T(8,128)(2,1)S(1)}, u32[]{:S(2)}, u32[]{:S(2)}) collective-permute-start(bf16[2,196,256]{2,1,0:T(8,128)(2,1)S(1)} %add_convert_fusion.1), channel_id=1, source_target_pairs={{0,14},{1,3},{2,0},{3,5},{4,2},{5,7},{6,4},{7,9},{8,6},{9,11},{10,... | collective-permute-start | bytes 602120 | tf_op jit(solution)/shard_map/ppermute | solution.py:372
  57.6 4.1 %collective-permute-done.8 = bf16[2,196,256]{2,1,0:T(8,128)(2,1)S(1)} collective-permute-done((bf16[2,196,256]{2,1,0:T(8,128)(2,1)S(1)}, bf16[2,196,256]{2,1,0:T(8,128)(2,1)S(1)}, u32[]{:S(2)}, u32[]{:S(2)}) %collective-permute-start.8) | collective-permute-done | bytes 200736 | tf_op jit(solution)/shard_map/ppermute | solution.py:372
  61.7 0.1 fusion.1
  61.8 4.7 %collective-permute-start.10 = (bf16[196,256]{1,0:T(8,128)(2,1)S(1)}, bf16[196,256]{1,0:T(8,128)(2,1)S(1)}, u32[]{:S(2)}, u32[]{:S(2)}) collective-permute-start(bf16[196,256]{1,0:T(8,128)(2,1)S(1)} %get-tuple-element.28), channel_id=1, source_target_pairs={{0,12},{1,5},{2,14},{3,7},{4,0},{5,9},{6,2},{7,11},{8,4},{9,13},{1... | collective-permute-start | bytes 301064 | tf_op jit(solution)/shard_map/ppermute | solution.py:372
  66.5 5.6 %collective-permute-start.9 = (bf16[196,256]{1,0:T(8,128)(2,1)S(1)}, bf16[196,256]{1,0:T(8,128)(2,1)S(1)}, u32[]{:S(2)}, u32[]{:S(2)}) collective-permute-start(bf16[196,256]{1,0:T(8,128)(2,1)S(1)} %get-tuple-element.29), channel_id=1, source_target_pairs={{0,6},{1,11},{2,8},{3,13},{4,10},{5,15},{6,12},{7,1},{8,14},{9,3},... | collective-permute-start | bytes 301064 | tf_op jit(solution)/shard_map/ppermute | solution.py:372
  72.0 7.0 %collective-permute-done.9.three_ref = bf16[196,256]{1,0:T(8,128)(2,1)S(1)} collective-permute-done((bf16[196,256]{1,0:T(8,128)(2,1)S(1)}, bf16[196,256]{1,0:T(8,128)(2,1)S(1)}, u32[]{:S(2)}, u32[]{:S(2)}) %collective-permute-start.9) | collective-permute-done | bytes 100384 | tf_op jit(solution)/shard_map/ppermute | solution.py:372
  79.1 1.7 %shard_map.118 = bf16[1,28,28,256]{3,2,1,0:T(8,128)(2,1)} custom-call(bf16[8,196,256]{2,1,0:T(8,128)(2,1)S(1)} %get-tuple-element.26.mine_ref, bf16[8,196,256]{2,1,0:T(8,128)(2,1)S(1)} %copy.25.swapped_ref, bf16[3,196,256]{2,1,0:T(8,128)(2,1)S(1)} %collective-permute-done.7.ahead_ref, bf16[196,256]{1,0:T(8,128)(2,1)S(1)} %collective-permute-done.9.three_ref, ...), custom_call_target="tpu_custom_call" | custom-call | flops 1000000000 | bytes 1000000 | tf_op jit(solution)/shard_map/pallas_call | solution.py:26
  (32 shorter events, 0.5 us)
Async XLA Ops:
  0.6 32.8 %collective-permute-start.3 = (bf16[32,32,256]{2,1,0:T(8,128)(2,1)}, bf16[32,32,256]{2,1,0:T(8,128)(2,1)S(1)}, u32[]{:S(2)}, u32[]{:S(2)}) collective-permute-start(bf16[32,32,256]{2,1,0:T(8,128)(2,1)} %own_ref.1), channel_id=1, source_target_pairs={{16,0},{32,16},{48,32},{64,48},{80,64},{96,80},{112,96},{128,112},... | collective-permute-start | bytes 1572872 | tf_op jit(solution)/shard_map/ppermute | solution.py:21
  11.9 1.1 %copy-start.3 = (bf16[32,32,256]{2,1,0:T(8,128)(2,1)S(1)}, bf16[32,32,256]{2,1,0:T(8,128)(2,1)}, u32[]{:S(2)}) copy-start(bf16[32,32,256]{2,1,0:T(8,128)(2,1)} %own_ref.1) | copy-start | bytes 1572868
  13.0 3.7 %collective-permute-start = (bf16[2,32,256]{2,1,0:T(8,128)(2,1)S(1)}, bf16[2,32,256]{2,1,0:T(8,128)(2,1)S(1)}, u32[]{:S(2)}, u32[]{:S(2)}) collective-permute-start(bf16[2,32,256]{2,1,0:T(8,128)(2,1)S(1)} %get-tuple-element.16.tail_ref), channel_id=1, source_target_pairs={{0,1},{1,2},{2,3},{3,4},{4,5},{5,6},{6,7},{7,8},{8,9},{9,10},{10,1... | collective-permute-start | bytes 98312 | tf_op jit(solution)/shard_map/ppermute | solution.py:21
  14.5 4.7 %collective-permute-start.1 = (bf16[2,32,256]{2,1,0:T(8,128)(2,1)S(1)}, bf16[2,32,256]{2,1,0:T(8,128)(2,1)S(1)}, u32[]{:S(2)}, u32[]{:S(2)}) collective-permute-start(bf16[2,32,256]{2,1,0:T(8,128)(2,1)S(1)} %get-tuple-element.17.lead_ref), channel_id=1, source_target_pairs={{1,0},{2,1},{3,2},{4,3},{5,4},{6,5},{7,6},{8,7},{9,8},{10,9},{11,1... | collective-permute-start | bytes 98312 | tf_op jit(solution)/shard_map/ppermute | solution.py:21
  19.2 10.0 %collective-permute-start.2 = (bf16[10,16,256]{2,1,0:T(8,128)(2,1)S(1)}, bf16[10,16,256]{2,1,0:T(8,128)(2,1)S(1)}, u32[]{:S(2)}, u32[]{:S(2)}) collective-permute-start(bf16[10,16,256]{2,1,0:T(8,128)(2,1)S(1)} %shard_map.114), channel_id=1, source_target_pairs={{0,16},{16,32},{32,48},{48,64},{64,80},{80,96},{96,112},{112,128},... | collective-permute-start | bytes 245768 | tf_op jit(solution)/shard_map/ppermute | solution.py:21
  21.2 11.7 %collective-permute-start.5 = (bf16[8,16,256]{2,1,0:T(8,128)(2,1)S(1)}, bf16[8,16,256]{2,1,0:T(8,128)(2,1)S(1)}, u32[]{:S(2)}, u32[]{:S(2)}) collective-permute-start(bf16[8,16,256]{2,1,0:T(8,128)(2,1)S(1)} %get-tuple-element.23), channel_id=1, source_target_pairs={{32,0},{48,16},{64,32},{80,48},{96,64},{112,80},{128,96},{144,112}... | collective-permute-start | bytes 196616 | tf_op jit(solution)/shard_map/ppermute | solution.py:21
  25.2 8.2 %collective-permute-start.4 = (bf16[6,32,256]{2,1,0:T(8,128)(2,1)S(1)}, bf16[6,32,256]{2,1,0:T(8,128)(2,1)S(1)}, u32[]{:S(2)}, u32[]{:S(2)}) collective-permute-start(bf16[6,32,256]{2,1,0:T(8,128)(2,1)S(1)} %get-tuple-element.21.own_sides_ref), channel_id=1, source_target_pairs={{16,0},{32,16},{48,32},{64,48},{80,64},{96,80},{112,96},{128,112},... | collective-permute-start | bytes 294920 | tf_op jit(solution)/shard_map/ppermute | solution.py:21
  30.8 1.7 %copy-start = (bf16[2,3,3,256,256]{4,3,2,1,0:T(8,128)(2,1)S(1)}, bf16[2,3,3,256,256]{4,3,2,1,0:T(8,128)(2,1)}, u32[]{:S(2)}) copy-start(bf16[2,3,3,256,256]{4,3,2,1,0:T(8,128)(2,1)} %param.11) | copy-start | bytes 7077892
  32.5 1.0 %copy-start.4 = (bf16[32,32,256]{2,1,0:T(8,128)(2,1)S(1)}, bf16[32,32,256]{2,1,0:T(8,128)(2,1)}, u32[]{:S(2)}) copy-start(bf16[32,32,256]{2,1,0:T(8,128)(2,1)} %own_ref.1) | copy-start | bytes 1572868
  32.5 1.0 %copy-start.7 = (f32[2,256]{1,0:T(2,128)S(1)}, f32[2,256]{1,0:T(2,128)}, u32[]{:S(2)}) copy-start(f32[2,256]{1,0:T(2,128)} %bias_ref.2) | copy-start | bytes 6148
  43.9 35.2 %copy-start.1 = (bf16[1,3,3,256,256]{4,3,2,1,0:T(8,128)(2,1)S(1)}, bf16[1,3,3,256,256]{4,3,2,1,0:T(8,128)(2,1)}, u32[]{:S(2)}) copy-start(bf16[1,3,3,256,256]{4,3,2,1,0:T(8,128)(2,1)} %param.15) | copy-start | bytes 3538948
  43.9 35.2 %copy-start.2 = (bf16[2,2,256,256]{3,2,1,0:T(8,128)(2,1)S(1)}, bf16[2,2,256,256]{3,2,1,0:T(8,128)(2,1)}, u32[]{:S(2)}) copy-start(bf16[2,2,256,256]{3,2,1,0:T(8,128)(2,1)} %param.17) | copy-start | bytes 1572868
  43.9 35.2 %copy-start.5 = (f32[1,256]{1,0:T(1,128)S(1)}, f32[1,256]{1,0:T(1,128)}, u32[]{:S(2)}) copy-start(f32[1,256]{1,0:T(1,128)} %bias_ref.3) | copy-start | bytes 3076
  43.9 35.2 %copy-start.6 = (f32[256]{0:T(256)S(1)}, f32[256]{0:T(256)}, u32[]{:S(2)}) copy-start(f32[256]{0:T(256)} %param.18) | copy-start | bytes 3076
  43.9 6.3 %collective-permute-start.6 = (bf16[8,196,256]{2,0,1:T(8,128)(2,1)S(1)}, bf16[8,196,256]{2,0,1:T(8,128)(2,1)S(1)}, u32[]{:S(2)}, u32[]{:S(2)}) collective-permute-start(bf16[8,196,256]{2,0,1:T(8,128)(2,1)S(1)} %copy.20), channel_id=1, source_target_pairs={{0,1},{1,0},{2,3},{3,2},{4,5},{5,4},{6,7},{7,6},{8,9},{9,8},{10,11... | collective-permute-start | bytes 2408456 | tf_op jit(solution)/shard_map/ppermute | solution.py:368
  50.5 11.2 %collective-permute-start.7 = (bf16[3,196,256]{2,1,0:T(8,128)(2,1)S(1)}, bf16[3,196,256]{2,1,0:T(8,128)(2,1)S(1)}, u32[]{:S(2)}, u32[]{:S(2)}) collective-permute-start(bf16[3,196,256]{2,1,0:T(8,128)(2,1)S(1)} %add_convert_fusion), channel_id=1, source_target_pairs={{0,2},{1,15},{2,4},{3,1},{4,6},{5,3},{6,8},{7,5},{8,10},{9,7},{10,... | collective-permute-start | bytes 903176 | tf_op jit(solution)/shard_map/ppermute | solution.py:372
  54.0 7.7 %collective-permute-start.8 = (bf16[2,196,256]{2,1,0:T(8,128)(2,1)S(1)}, bf16[2,196,256]{2,1,0:T(8,128)(2,1)S(1)}, u32[]{:S(2)}, u32[]{:S(2)}) collective-permute-start(bf16[2,196,256]{2,1,0:T(8,128)(2,1)S(1)} %add_convert_fusion.1), channel_id=1, source_target_pairs={{0,14},{1,3},{2,0},{3,5},{4,2},{5,7},{6,4},{7,9},{8,6},{9,11},{10,... | collective-permute-start | bytes 602120 | tf_op jit(solution)/shard_map/ppermute | solution.py:372
  61.8 10.2 %collective-permute-start.10 = (bf16[196,256]{1,0:T(8,128)(2,1)S(1)}, bf16[196,256]{1,0:T(8,128)(2,1)S(1)}, u32[]{:S(2)}, u32[]{:S(2)}) collective-permute-start(bf16[196,256]{1,0:T(8,128)(2,1)S(1)} %get-tuple-element.28), channel_id=1, source_target_pairs={{0,12},{1,5},{2,14},{3,7},{4,0},{5,9},{6,2},{7,11},{8,4},{9,13},{1... | collective-permute-start | bytes 301064 | tf_op jit(solution)/shard_map/ppermute | solution.py:372
  66.5 12.6 %collective-permute-start.9 = (bf16[196,256]{1,0:T(8,128)(2,1)S(1)}, bf16[196,256]{1,0:T(8,128)(2,1)S(1)}, u32[]{:S(2)}, u32[]{:S(2)}) collective-permute-start(bf16[196,256]{1,0:T(8,128)(2,1)S(1)} %get-tuple-element.29), channel_id=1, source_target_pairs={{0,6},{1,11},{2,8},{3,13},{4,10},{5,15},{6,12},{7,1},{8,14},{9,3},... | collective-permute-start | bytes 301064 | tf_op jit(solution)/shard_map/ppermute | solution.py:372

commit v4 on v3

--- a/solution.py
+++ b/solution.py
@@ -1,3 +1,5 @@
+import functools
+
 import jax
 import jax.numpy as jnp
 from jax import lax
@@ -67,7 +69,7 @@
         up_ref[count + i] = part[i % 2, 0:TILE]
 
 
-def exchange(features, later):
+def exchange(features):
     rows, cols, channels = features.shape
     vmem = pl.BlockSpec(memory_space=pltpu.VMEM)
     below = shift(features, "row", -1)
@@ -85,7 +87,7 @@
         down_kernel, (jax.ShapeDtypeStruct((2 * whole + 6, TILE, channels), BF16),),
         [vmem] * 5, [], 4, 10**5, *strips,
     )
-    above, later = lax.optimization_barrier((shift(to_down, "row", 1), later))
+    above = shift(to_down, "row", 1)
     sides_shape = jax.ShapeDtypeStruct((6, rows, channels), BF16)
     up_shape = jax.ShapeDtypeStruct((whole + 6, TILE, channels), BF16)
     own_sides, to_up = call(
@@ -93,15 +95,42 @@
     )
     sides = shift(own_sides, "row", -1)
     after = shift(to_up, "row", -2)
-    return below, own_sides, sides, above, after, later
-
-
-def sample(lower, extent):
-    lower_f = lower.astype(F32)[:, None]
-    extent_f = extent.astype(F32)[:, None]
-    bins = jnp.arange(POOL).astype(F32)[None, :]
-    centre = lower_f + (bins + 0.5) * extent_f / POOL - 0.5
-    return jnp.clip(centre, lower_f, lower_f + extent_f - 1.0)
+    return below, own_sides, sides, above, after
+
+
+def plan_kernel(boxes_ref, owner_ref, at_ref, by_ref, *, rows, cols, axes):
+    row, col = lax.axis_index("row"), lax.axis_index("col")
+    count = boxes_ref.shape[0]
+    chips = axes[1] // 2
+    slot = lax.broadcasted_iota(jnp.int32, (count, LANES), 0)
+    bins = lax.broadcasted_iota(jnp.int32, (count, LANES), 1).astype(F32)
+    core = jnp.where(slot < chips, col % 2, 1 - col % 2)
+    hop = jnp.zeros_like(slot)
+    for i, step in enumerate(HOPS):
+        hop = jnp.where((slot == i) | (slot == i + chips), step, hop)
+    chip = col // 2 + hop * (1 - 2 * core) + chips
+    chip = jnp.where(chip >= chips, chip - chips, chip)
+    chip = jnp.where(chip >= chips, chip - chips, chip)
+    wanted = 2 * chip + core
+    fields = [jnp.zeros_like(slot) for _ in range(4)]
+    for k in range(count):
+        here = wanted == owner_ref[0, k]
+        fields = [jnp.where(here, boxes_ref[k, f], fields[f]) for f in range(4)]
+    for dim, start, size in ((0, row * rows, 2 * rows), (1, col * cols, cols)):
+        lower, extent = fields[dim].astype(F32), fields[dim + 2].astype(F32)
+        centre = lower + (bins + 0.5) * extent / POOL - 0.5
+        centre = jnp.minimum(jnp.maximum(centre, lower), lower + extent - 1.0)
+        low = jnp.floor(centre)
+        for t, place in enumerate((low, low + 1.0)):
+            weight = jnp.maximum(1.0 - jnp.abs(place - centre), 0.0).astype(BF16).astype(F32)
+            index = place.astype(jnp.int32) - start
+            inside = (index >= 0) & (index < size)
+            at = jnp.minimum(jnp.maximum(index, 0), size - 1)
+            at_ref[2 * dim + t] = at[:, :POOL]
+            by_ref[2 * dim + t] = jnp.where(inside, weight, 0.0)[:, :POOL]
+    left, right = fields[1], fields[1] + fields[3]
+    hit = (left < (col + 1) * cols) & (right > col * cols)
+    at_ref[4] = jnp.where(hit, 1, 0)[:, :POOL]
 
 
 def spread(dst, start, value, edge_ref, sides, offset):
@@ -127,15 +156,21 @@
 
 
 def main_kernel(
-    flags_ref, hit_ref, at_ref, by_ref,
+    at_ref, by_ref,
     own_ref, below_ref, own_sides_ref, sides_ref, above_ref, after_ref,
-    weight_ref, bias_ref,
+    weight_hbm, bias_ref,
     tower_ref, mine_ref, other_ref,
-    wide_ref, mid_ref, band_ref, comb_ref, patch_ref, strip_ref, inner_ref,
+    wide_ref, mid_ref, band_ref, comb_ref, patch_ref, strip_ref, inner_ref, weight_ref, sems, *, last_row, last_col,
 ):
     rows, width, channels = own_ref.shape
     half = mine_ref.shape[0]
     whole = width // TILE
+    loads = [
+        pltpu.make_async_copy(weight_hbm.at[l], weight_ref.at[l], sems.at[l]) for l in range(2)
+    ]
+    for load in loads:
+        load.start()
+    row, col = lax.axis_index("row"), lax.axis_index("col")
     for c in range(6):
         strip_ref[c, 0:2, :] = above_ref[2 * whole + c].astype(F32)[TILE - 2 : TILE]
         strip_ref[c, 2 : rows + 2, :] = own_sides_ref[c].astype(F32)
@@ -156,6 +191,7 @@
     spread(wide_ref, last, after_ref[0:whole].reshape(1, width, channels), strip_ref, (1, 4), last)
     wide_ref[3 + 2 * rows] = jnp.zeros(wide_ref.shape[1:], BF16)
 
+    loads[0].wait()
     tall = inner_ref.shape[1]
     sides = []
     for side in range(2):
@@ -169,7 +205,7 @@
     out = jnp.maximum(out + bias_ref[0:1], 0.0).astype(BF16).astype(F32)
     for side in range(2):
         part = out[side * tall : (side + 1) * tall]
-        inner_ref[side] = jnp.where(flags_ref[2 + side] > 0, part, 0.0)
+        inner_ref[side] = jnp.where((col > 0) if side == 0 else (col < last_col), part, 0.0)
 
     def first(i, carry):
         at = i * FIRST
@@ -180,14 +216,16 @@
     lax.fori_loop(0, (2 * rows + 2) // FIRST, first, 0)
     blank = jnp.zeros(mid_ref.shape[1:], BF16)
 
-    @pl.when(flags_ref[0] > 0)
+    @pl.when(row == 0)
     def _():
         mid_ref[0] = blank
 
-    @pl.when(flags_ref[1] > 0)
+    @pl.when(row == last_row)
     def _():
         mid_ref[rows + 1] = blank
     mid_ref[2 * rows + 1] = blank
+
+    loads[1].wait()
 
     def second(i, carry):
         at = i * SECOND
@@ -206,7 +244,7 @@
         def region(m, carry):
             n = m + side * half
 
-            @pl.when(hit_ref[n] > 0)
+            @pl.when(at_ref[4, n, 0] > 0)
             def _():
                 for p in range(POOL):
                     line = band_ref[at_ref[0, n, p]] * by_ref[0, n, p]
@@ -223,7 +261,7 @@
                 for h, lanes in halves:
                     out_ref[m, :, lanes] = patch_ref[h, pl.ds(0, POOL * POOL), :].astype(BF16)
 
-            @pl.when(hit_ref[n] == 0)
+            @pl.when(at_ref[4, n, 0] == 0)
             def _():
                 out_ref[m] = jnp.zeros(out_ref.shape[1:], BF16)
 
@@ -232,51 +270,31 @@
         lax.fori_loop(0, half, region, 0)
 
 
-def taps_of(boxes, rows, cols):
-    row_first = lax.axis_index("row") * rows
-    col_first = lax.axis_index("col") * cols
-    at, by = [], []
-    for dim, start, size in ((0, row_first, 2 * rows), (1, col_first, cols)):
-        centre = sample(boxes[:, dim], boxes[:, dim + 2])
-        low = jnp.floor(centre)
-        for place in (low, low + 1.0):
-            weight = jnp.maximum(1.0 - jnp.abs(place - centre), 0.0).astype(BF16).astype(F32)
-            index = place.astype(jnp.int32) - start
-            at.append(jnp.clip(index, 0, size - 1))
-            by.append(jnp.where((index >= 0) & (index < size), weight, 0.0))
-    hit = (boxes[:, 1] < col_first + cols) & (boxes[:, 1] + boxes[:, 3] > col_first)
-    return hit.astype(jnp.int32), jnp.stack(at), jnp.stack(by)
-
-
-def stage_kernel(src_ref, dst_ref, sem):
-    load = pltpu.make_async_copy(src_ref, dst_ref, sem)
-    load.start()
-    load.wait()
-
-
-def tower_and_pool(features, weight, bias, boxes, owner_slot, wanted):
+def tower_and_pool(features, weight, bias, boxes, owner_slot):
     rows, cols, channels = features.shape
-    below, own_sides, sides, above, after, (boxes, owner_slot, wanted, weight) = exchange(
-        features, (boxes, owner_slot, wanted, weight.reshape(2, -1, weight.shape[-1]))
-    )
-    (weight,) = call(
-        stage_kernel, (jax.ShapeDtypeStruct(weight.shape, BF16),),
-        [pl.BlockSpec(memory_space=pl.ANY)], [pltpu.SemaphoreType.DMA], 4, 10**5, weight,
-    )
-    row, col = lax.axis_index("row"), lax.axis_index("col")
-    last_row, last_col = lax.axis_size("row") - 1, lax.axis_size("col") - 1
-    flags = jnp.stack([row == 0, row == last_row, col > 0, col < last_col]).astype(jnp.int32)
-    picked = (owner_slot[0][None, :] == wanted[:, None]).astype(jnp.int32)
-    boxes = jnp.sum(picked[:, :, None] * boxes[None, :, :], axis=1)
-    hit, at, by = taps_of(boxes, rows, cols)
+    below, own_sides, sides, above, after = exchange(features)
+    above, boxes = lax.optimization_barrier((above, boxes))
     count = boxes.shape[0]
     smem = pl.BlockSpec(memory_space=pltpu.SMEM)
     vmem = pl.BlockSpec(memory_space=pltpu.VMEM)
+    at, by = call(
+        functools.partial(
+            plan_kernel, rows=rows, cols=cols, axes=(lax.axis_size("row"), lax.axis_size("col"))
+        ),
+        (
+            jax.ShapeDtypeStruct((5, count, POOL), jnp.int32),
+            jax.ShapeDtypeStruct((4, count, POOL), F32),
+        ),
+        [smem, smem], [], 4, 10**5, boxes, owner_slot,
+    )
     patches = jax.ShapeDtypeStruct((count // 2, POOL * POOL, channels), BF16)
+    kernel = functools.partial(
+        main_kernel, last_row=lax.axis_size("row") - 1, last_col=lax.axis_size("col") - 1
+    )
     return call(
-        main_kernel,
+        kernel,
         (jax.ShapeDtypeStruct(features.shape, BF16), patches, patches),
-        [smem] * 4 + [vmem] * 8,
+        [smem] * 2 + [vmem] * 6 + [pl.BlockSpec(memory_space=pl.ANY), vmem],
         [
             pltpu.VMEM((2 * rows + 4, cols, 3 * channels), BF16),
             pltpu.VMEM((2 * rows + 2, cols, 3 * channels), BF16),
@@ -285,10 +303,12 @@
             pltpu.VMEM((channels // LANES, SIDE * SIDE, LANES), F32),
             pltpu.VMEM((6, 2 * rows + 24, channels), F32),
             pltpu.VMEM((2, 2 * rows + 16, channels), F32),
+            pltpu.VMEM((2, 9 * channels, channels), BF16),
+            pltpu.SemaphoreType.DMA((2,)),
         ],
-        40, 6 * 10**9,
-        flags, hit, at, by, features, below, own_sides, sides, above, after,
-        weight, bias,
+        51, 6 * 10**9,
+        at, by, features, below, own_sides, sides, above, after,
+        weight.reshape(2, 9 * channels, channels), bias,
     )
 
 
@@ -357,14 +377,7 @@
 ):
     peers = lax.axis_size("col")
     chips = peers // 2
-    core = lax.axis_index("col") % 2
-    chip = lax.axis_index("col") // 2
-    hops = jnp.array(HOPS * 2, dtype=jnp.int32)
-    sides = jnp.repeat(jnp.stack([core, 1 - core]), chips)
-    wanted = 2 * ((chip + hops * (1 - 2 * sides)) % chips) + sides
-    tower, mine, other = tower_and_pool(
-        features, tower_weight, tower_bias, boxes, owner_slot, wanted
-    )
+    tower, mine, other = tower_and_pool(features, tower_weight, tower_bias, boxes, owner_slot)
     swapped = lax.ppermute(other, "col", [(i, i ^ 1) for i in range(peers)])
 
     def send(value, hop):

time: 81.4 us -> 84.8 us (1.042)
  waiting for transfers between devices: 16 us -> 22.2 us
  starting transfers between devices: 45.5 us -> 41.6 us
  other arithmetic: 2.86 us -> 0.25 us
  local copies, waits for them, and re-layouts: 3.32 us -> 5.67 us
  Pallas kernels: 12.2 us -> 13.6 us
    ppermute x6, waiting for transfers between devices: 2.98 us -> 7.54 us  [shift(): lax.ppermute(value, axis, [(i, i + step) for i in devices if i + step in...]
    ppermute x1, starting transfers between devices: 4.41 us -> 2.19 us  [per_device(): swapped = lax.ppermute(other, 'col', [(i, i ^ 1) for i in range(peers)])]
    ppermute x6, starting transfers between devices: 23.8 us -> 22.3 us  [shift(): lax.ppermute(value, axis, [(i, i + step) for i in devices if i + step in...]
    pallas_call x6, Pallas kernels: 12.2 us -> 13.6 us  [call(): pl.pallas_call(kernel, out_shape=out_shape, in_specs=in_specs, out_specs=...]
    ppermute x4, waiting for transfers between devices: 11.1 us -> 12.5 us  [send(): lax.ppermute(value, 'col', [(i, (i + steps[i]) % peers) for i in range(pe...]
    pallas_call x1, local copies, waits for them, and re-layouts: 0.16 us -> 1.3 us  [call(): pl.pallas_call(kernel, out_shape=out_shape, in_specs=in_specs, out_specs=...]
  transfers between devices with their start and end apart: 11 -> 11, of which waited for: 5 -> 6; matrix products, arithmetic and copies ran while one was open for 3% -> 1% of each run, Pallas kernels for 0% -> 1%
where the time goes in v4:
time: 84.8 us; the launch traced here: 84.2 us
  starting transfers between devices  41.6 us (49%)
  waiting for transfers between devices  22.2 us (26%)
  Pallas kernels  13.6 us (16%)
  local copies, waits for them, and re-layouts  5.67 us (7%)
  between operations  0.85 us (1%)
    ppermute x6, starting transfers between devices, shift(): lax.ppermute(value, axis, [(i, i + step) for i in devices if i + step in...  22.3 us
    ppermute x4, starting transfers between devices, send(): lax.ppermute(value, 'col', [(i, (i + steps[i]) % peers) for i in range(pe...  17.2 us
    pallas_call x6, Pallas kernels, call(): pl.pallas_call(kernel, out_shape=out_shape, in_specs=in_specs, out_specs=...  13.6 us
    ppermute x4, waiting for transfers between devices, send(): lax.ppermute(value, 'col', [(i, (i + steps[i]) % peers) for i in range(pe...  12.5 us
    ppermute x6, waiting for transfers between devices, shift(): lax.ppermute(value, axis, [(i, i + step) for i in devices if i + step in...  7.54 us
    unnamed x16, local copies, waits for them, and re-layouts  3.45 us
    ppermute x1, starting transfers between devices, per_device(): swapped = lax.ppermute(other, 'col', [(i, i ^ 1) for i in range(peers)])  2.19 us
    ppermute x1, waiting for transfers between devices, per_device(): swapped = lax.ppermute(other, 'col', [(i, i ^ 1) for i in range(peers)])  2.14 us
  transfers between devices with their start and end apart: 11, of which 6 were waited for; matrix products, arithmetic and copies ran while one was open for 1% of the time, Pallas kernels for 1%

profile of v4, /device:TPU:6, one launch (start us, length us, event | category | flops | bytes accessed | tf_op | source)
XLA Modules:
  0.0 84.2 jit_solution(15386599541755454675)
XLA Ops:
  0.6 11.2 %collective-permute-start.3 = (bf16[32,32,256]{2,1,0:T(8,128)(2,1)}, bf16[32,32,256]{2,1,0:T(8,128)(2,1)S(1)}, u32[]{:S(2)}, u32[]{:S(2)}) collective-permute-start(bf16[32,32,256]{2,1,0:T(8,128)(2,1)} %own_ref.1), channel_id=1, source_target_pairs={{16,0},{32,16},{48,32},{64,48},{80,64},{96,80},{112,96},{128,112},... | collective-permute-start | bytes 1572872 | tf_op jit(solution)/shard_map/ppermute | solution.py:23
  11.9 0.0 copy-start.2
  11.9 1.0 %copy-done.2 = bf16[32,32,256]{2,1,0:T(8,128)(2,1)S(1)} copy-done((bf16[32,32,256]{2,1,0:T(8,128)(2,1)S(1)}, bf16[32,32,256]{2,1,0:T(8,128)(2,1)}, u32[]{:S(2)}) %copy-start.2) | copy-done | bytes 524312
  12.9 0.1 shard_map.104
  13.0 1.5 %collective-permute-start = (bf16[2,32,256]{2,1,0:T(8,128)(2,1)S(1)}, bf16[2,32,256]{2,1,0:T(8,128)(2,1)S(1)}, u32[]{:S(2)}, u32[]{:S(2)}) collective-permute-start(bf16[2,32,256]{2,1,0:T(8,128)(2,1)S(1)} %get-tuple-element.15.tail_ref), channel_id=1, source_target_pairs={{0,1},{1,2},{2,3},{3,4},{4,5},{5,6},{6,7},{7,8},{8,9},{9,10},{10,1... | collective-permute-start | bytes 98312 | tf_op jit(solution)/shard_map/ppermute | solution.py:23
  14.5 1.3 %collective-permute-start.1 = (bf16[2,32,256]{2,1,0:T(8,128)(2,1)S(1)}, bf16[2,32,256]{2,1,0:T(8,128)(2,1)S(1)}, u32[]{:S(2)}, u32[]{:S(2)}) collective-permute-start(bf16[2,32,256]{2,1,0:T(8,128)(2,1)S(1)} %get-tuple-element.16.lead_ref), channel_id=1, source_target_pairs={{1,0},{2,1},{3,2},{4,3},{5,4},{6,5},{7,6},{8,7},{9,8},{10,9},{11,1... | collective-permute-start | bytes 98312 | tf_op jit(solution)/shard_map/ppermute | solution.py:23
  15.8 3.4 %collective-permute-done.1.right_ref = bf16[2,32,256]{2,1,0:T(8,128)(2,1)S(1)} collective-permute-done((bf16[2,32,256]{2,1,0:T(8,128)(2,1)S(1)}, bf16[2,32,256]{2,1,0:T(8,128)(2,1)S(1)}, u32[]{:S(2)}, u32[]{:S(2)}) %collective-permute-start.1) | collective-permute-done | bytes 32800 | tf_op jit(solution)/shard_map/ppermute | solution.py:23
  19.2 2.5 %collective-permute-start.4 = (bf16[6,32,256]{2,1,0:T(8,128)(2,1)S(1)}, bf16[6,32,256]{2,1,0:T(8,128)(2,1)S(1)}, u32[]{:S(2)}, u32[]{:S(2)}) collective-permute-start(bf16[6,32,256]{2,1,0:T(8,128)(2,1)S(1)} %get-tuple-element.20.own_sides_ref), channel_id=1, source_target_pairs={{16,0},{32,16},{48,32},{64,48},{80,64},{96,80},{112,96},{128,112},... | collective-permute-start | bytes 294920 | tf_op jit(solution)/shard_map/ppermute | solution.py:23
  21.7 3.4 %collective-permute-start.2 = (bf16[10,16,256]{2,1,0:T(8,128)(2,1)S(1)}, bf16[10,16,256]{2,1,0:T(8,128)(2,1)S(1)}, u32[]{:S(2)}, u32[]{:S(2)}) collective-permute-start(bf16[10,16,256]{2,1,0:T(8,128)(2,1)S(1)} %shard_map.105), channel_id=1, source_target_pairs={{0,16},{16,32},{32,48},{48,64},{64,80},{80,96},{96,112},{112,128},... | collective-permute-start | bytes 245768 | tf_op jit(solution)/shard_map/ppermute | solution.py:23
  25.1 2.5 %collective-permute-start.5 = (bf16[8,16,256]{2,1,0:T(8,128)(2,1)S(1)}, bf16[8,16,256]{2,1,0:T(8,128)(2,1)S(1)}, u32[]{:S(2)}, u32[]{:S(2)}) collective-permute-start(bf16[8,16,256]{2,1,0:T(8,128)(2,1)S(1)} %get-tuple-element.22), channel_id=1, source_target_pairs={{32,0},{48,16},{64,32},{80,48},{96,64},{112,80},{128,96},{144,112}... | collective-permute-start | bytes 196616 | tf_op jit(solution)/shard_map/ppermute | solution.py:23
  27.6 2.6 %collective-permute-done.2.above_ref = bf16[10,16,256]{2,1,0:T(8,128)(2,1)S(1)} collective-permute-done((bf16[10,16,256]{2,1,0:T(8,128)(2,1)S(1)}, bf16[10,16,256]{2,1,0:T(8,128)(2,1)S(1)}, u32[]{:S(2)}, u32[]{:S(2)}) %collective-permute-start.2) | collective-permute-done | bytes 81952 | tf_op jit(solution)/shard_map/ppermute | solution.py:23
  30.2 0.8 copy.12.boxes_ref
  30.9 0.7 copy-done.6
  31.6 0.8 shard_map.106
  32.3 1.5 %collective-permute-done.5.after_ref = bf16[8,16,256]{2,1,0:T(8,128)(2,1)S(1)} collective-permute-done((bf16[8,16,256]{2,1,0:T(8,128)(2,1)S(1)}, bf16[8,16,256]{2,1,0:T(8,128)(2,1)S(1)}, u32[]{:S(2)}, u32[]{:S(2)}) %collective-permute-start.5) | collective-permute-done | bytes 65568 | tf_op jit(solution)/shard_map/ppermute | solution.py:23
  33.9 1.0 %copy-done.3 = bf16[32,32,256]{2,1,0:T(8,128)(2,1)S(1)} copy-done((bf16[32,32,256]{2,1,0:T(8,128)(2,1)S(1)}, bf16[32,32,256]{2,1,0:T(8,128)(2,1)}, u32[]{:S(2)}) %copy-start.3) | copy-done | bytes 524312
  34.9 0.7 copy-done.7
  35.6 11.0 %shard_map.108 = (bf16[32,32,256]{2,1,0:T(8,128)(2,1)}, bf16[8,196,256]{2,1,0:T(8,128)(2,1)S(1)}, bf16[8,196,256]{2,1,0:T(8,128)(2,1)}) custom-call(s32[5,16,14]{2,1,0:T(8,128)S(1)} %get-tuple-element.18.at_ref, f32[4,16,14]{2,1,0:T(8,128)S(1)} %get-tuple-element.19.by_ref, bf16[32,32,256]{2,1,0:T(8,128)(2,1)S(1)} %copy-done.3, ...), custom_call_target="tpu_custom_call" | custom-call | flops 6000000000 | bytes 1000000 | tf_op jit(solution)/shard_map/pallas_call | solution.py:28
  46.6 1.3 %copy.13 = bf16[8,196,256]{2,0,1:T(8,128)(2,1)S(1)} copy(bf16[8,196,256]{2,1,0:T(8,128)(2,1)} %get-tuple-element.25) | data formatting | bytes 1605632 | tf_op jit(solution)/shard_map/pallas_call | solution.py:28
  48.0 2.2 %collective-permute-start.6 = (bf16[8,196,256]{2,0,1:T(8,128)(2,1)S(1)}, bf16[8,196,256]{2,0,1:T(8,128)(2,1)S(1)}, u32[]{:S(2)}, u32[]{:S(2)}) collective-permute-start(bf16[8,196,256]{2,0,1:T(8,128)(2,1)S(1)} %copy.13), channel_id=1, source_target_pairs={{0,1},{1,0},{2,3},{3,2},{4,5},{5,4},{6,7},{7,6},{8,9},{9,8},{10,11... | collective-permute-start | bytes 2408456 | tf_op jit(solution)/shard_map/ppermute | solution.py:381
  50.2 2.1 %collective-permute-done.6 = bf16[8,196,256]{2,0,1:T(8,128)(2,1)S(1)} collective-permute-done((bf16[8,196,256]{2,0,1:T(8,128)(2,1)S(1)}, bf16[8,196,256]{2,0,1:T(8,128)(2,1)S(1)}, u32[]{:S(2)}, u32[]{:S(2)}) %collective-permute-start.6) | collective-permute-done | bytes 802848 | tf_op jit(solution)/shard_map/ppermute | solution.py:381
  52.3 0.2 copy.18.swapped_ref
  52.5 0.1 add_convert_fusion
  52.5 4.4 %collective-permute-start.7 = (bf16[3,196,256]{2,1,0:T(8,128)(2,1)S(1)}, bf16[3,196,256]{2,1,0:T(8,128)(2,1)S(1)}, u32[]{:S(2)}, u32[]{:S(2)}) collective-permute-start(bf16[3,196,256]{2,1,0:T(8,128)(2,1)S(1)} %add_convert_fusion), channel_id=1, source_target_pairs={{0,2},{1,15},{2,4},{3,1},{4,6},{5,3},{6,8},{7,5},{8,10},{9,7},{10,... | collective-permute-start | bytes 903176 | tf_op jit(solution)/shard_map/ppermute | solution.py:385
  56.9 0.1 add_convert_fusion.1
  57.0 3.0 %collective-permute-start.8 = (bf16[2,196,256]{2,1,0:T(8,128)(2,1)S(1)}, bf16[2,196,256]{2,1,0:T(8,128)(2,1)S(1)}, u32[]{:S(2)}, u32[]{:S(2)}) collective-permute-start(bf16[2,196,256]{2,1,0:T(8,128)(2,1)S(1)} %add_convert_fusion.1), channel_id=1, source_target_pairs={{0,14},{1,3},{2,0},{3,5},{4,2},{5,7},{6,4},{7,9},{8,6},{9,11},{10,... | collective-permute-start | bytes 602120 | tf_op jit(solution)/shard_map/ppermute | solution.py:385
  60.0 5.1 %collective-permute-done.8 = bf16[2,196,256]{2,1,0:T(8,128)(2,1)S(1)} collective-permute-done((bf16[2,196,256]{2,1,0:T(8,128)(2,1)S(1)}, bf16[2,196,256]{2,1,0:T(8,128)(2,1)S(1)}, u32[]{:S(2)}, u32[]{:S(2)}) %collective-permute-start.8) | collective-permute-done | bytes 200736 | tf_op jit(solution)/shard_map/ppermute | solution.py:385
  65.1 0.1 fusion.1
  65.3 6.4 %collective-permute-start.10 = (bf16[196,256]{1,0:T(8,128)(2,1)S(1)}, bf16[196,256]{1,0:T(8,128)(2,1)S(1)}, u32[]{:S(2)}, u32[]{:S(2)}) collective-permute-start(bf16[196,256]{1,0:T(8,128)(2,1)S(1)} %get-tuple-element.26), channel_id=1, source_target_pairs={{0,12},{1,5},{2,14},{3,7},{4,0},{5,9},{6,2},{7,11},{8,4},{9,13},{1... | collective-permute-start | bytes 301064 | tf_op jit(solution)/shard_map/ppermute | solution.py:385
  71.7 3.4 %collective-permute-start.9 = (bf16[196,256]{1,0:T(8,128)(2,1)S(1)}, bf16[196,256]{1,0:T(8,128)(2,1)S(1)}, u32[]{:S(2)}, u32[]{:S(2)}) collective-permute-start(bf16[196,256]{1,0:T(8,128)(2,1)S(1)} %get-tuple-element.27), channel_id=1, source_target_pairs={{0,6},{1,11},{2,8},{3,13},{4,10},{5,15},{6,12},{7,1},{8,14},{9,3},... | collective-permute-start | bytes 301064 | tf_op jit(solution)/shard_map/ppermute | solution.py:385
  75.1 7.4 %collective-permute-done.9.three_ref = bf16[196,256]{1,0:T(8,128)(2,1)S(1)} collective-permute-done((bf16[196,256]{1,0:T(8,128)(2,1)S(1)}, bf16[196,256]{1,0:T(8,128)(2,1)S(1)}, u32[]{:S(2)}, u32[]{:S(2)}) %collective-permute-start.9) | collective-permute-done | bytes 100384 | tf_op jit(solution)/shard_map/ppermute | solution.py:385
  82.5 1.7 %shard_map.109 = bf16[1,28,28,256]{3,2,1,0:T(8,128)(2,1)} custom-call(bf16[8,196,256]{2,1,0:T(8,128)(2,1)S(1)} %get-tuple-element.24.mine_ref, bf16[8,196,256]{2,1,0:T(8,128)(2,1)S(1)} %copy.18.swapped_ref, bf16[3,196,256]{2,1,0:T(8,128)(2,1)S(1)} %collective-permute-done.7.ahead_ref, bf16[196,256]{1,0:T(8,128)(2,1)S(1)} %collective-permute-done.9.three_ref, ...), custom_call_target="tpu_custom_call" | custom-call | flops 1000000000 | bytes 1000000 | tf_op jit(solution)/shard_map/pallas_call | solution.py:28
  (18 shorter events, 0.1 us)
Async XLA Ops:
  0.6 33.2 %collective-permute-start.3 = (bf16[32,32,256]{2,1,0:T(8,128)(2,1)}, bf16[32,32,256]{2,1,0:T(8,128)(2,1)S(1)}, u32[]{:S(2)}, u32[]{:S(2)}) collective-permute-start(bf16[32,32,256]{2,1,0:T(8,128)(2,1)} %own_ref.1), channel_id=1, source_target_pairs={{16,0},{32,16},{48,32},{64,48},{80,64},{96,80},{112,96},{128,112},... | collective-permute-start | bytes 1572872 | tf_op jit(solution)/shard_map/ppermute | solution.py:23
  11.9 1.1 %copy-start.2 = (bf16[32,32,256]{2,1,0:T(8,128)(2,1)S(1)}, bf16[32,32,256]{2,1,0:T(8,128)(2,1)}, u32[]{:S(2)}) copy-start(bf16[32,32,256]{2,1,0:T(8,128)(2,1)} %own_ref.1) | copy-start | bytes 1572868
  13.0 2.8 %collective-permute-start = (bf16[2,32,256]{2,1,0:T(8,128)(2,1)S(1)}, bf16[2,32,256]{2,1,0:T(8,128)(2,1)S(1)}, u32[]{:S(2)}, u32[]{:S(2)}) collective-permute-start(bf16[2,32,256]{2,1,0:T(8,128)(2,1)S(1)} %get-tuple-element.15.tail_ref), channel_id=1, source_target_pairs={{0,1},{1,2},{2,3},{3,4},{4,5},{5,6},{6,7},{7,8},{8,9},{9,10},{10,1... | collective-permute-start | bytes 98312 | tf_op jit(solution)/shard_map/ppermute | solution.py:23
  14.5 4.7 %collective-permute-start.1 = (bf16[2,32,256]{2,1,0:T(8,128)(2,1)S(1)}, bf16[2,32,256]{2,1,0:T(8,128)(2,1)S(1)}, u32[]{:S(2)}, u32[]{:S(2)}) collective-permute-start(bf16[2,32,256]{2,1,0:T(8,128)(2,1)S(1)} %get-tuple-element.16.lead_ref), channel_id=1, source_target_pairs={{1,0},{2,1},{3,2},{4,3},{5,4},{6,5},{7,6},{8,7},{9,8},{10,9},{11,1... | collective-permute-start | bytes 98312 | tf_op jit(solution)/shard_map/ppermute | solution.py:23
  19.2 14.6 %collective-permute-start.4 = (bf16[6,32,256]{2,1,0:T(8,128)(2,1)S(1)}, bf16[6,32,256]{2,1,0:T(8,128)(2,1)S(1)}, u32[]{:S(2)}, u32[]{:S(2)}) collective-permute-start(bf16[6,32,256]{2,1,0:T(8,128)(2,1)S(1)} %get-tuple-element.20.own_sides_ref), channel_id=1, source_target_pairs={{16,0},{32,16},{48,32},{64,48},{80,64},{96,80},{112,96},{128,112},... | collective-permute-start | bytes 294920 | tf_op jit(solution)/shard_map/ppermute | solution.py:23
  21.7 8.4 %collective-permute-start.2 = (bf16[10,16,256]{2,1,0:T(8,128)(2,1)S(1)}, bf16[10,16,256]{2,1,0:T(8,128)(2,1)S(1)}, u32[]{:S(2)}, u32[]{:S(2)}) collective-permute-start(bf16[10,16,256]{2,1,0:T(8,128)(2,1)S(1)} %shard_map.105), channel_id=1, source_target_pairs={{0,16},{16,32},{32,48},{48,64},{64,80},{80,96},{96,112},{112,128},... | collective-permute-start | bytes 245768 | tf_op jit(solution)/shard_map/ppermute | solution.py:23
  25.1 8.7 %collective-permute-start.5 = (bf16[8,16,256]{2,1,0:T(8,128)(2,1)S(1)}, bf16[8,16,256]{2,1,0:T(8,128)(2,1)S(1)}, u32[]{:S(2)}, u32[]{:S(2)}) collective-permute-start(bf16[8,16,256]{2,1,0:T(8,128)(2,1)S(1)} %get-tuple-element.22), channel_id=1, source_target_pairs={{32,0},{48,16},{64,32},{80,48},{96,64},{112,80},{128,96},{144,112}... | collective-permute-start | bytes 196616 | tf_op jit(solution)/shard_map/ppermute | solution.py:23
  30.9 0.7 copy-start.6
  33.9 1.0 %copy-start.3 = (bf16[32,32,256]{2,1,0:T(8,128)(2,1)S(1)}, bf16[32,32,256]{2,1,0:T(8,128)(2,1)}, u32[]{:S(2)}) copy-start(bf16[32,32,256]{2,1,0:T(8,128)(2,1)} %own_ref.1) | copy-start | bytes 1572868
  34.9 0.7 copy-start.7
  47.9 34.5 %copy-start = (bf16[1,3,3,256,256]{4,3,2,1,0:T(8,128)(2,1)S(1)}, bf16[1,3,3,256,256]{4,3,2,1,0:T(8,128)(2,1)}, u32[]{:S(2)}) copy-start(bf16[1,3,3,256,256]{4,3,2,1,0:T(8,128)(2,1)} %param.14) | copy-start | bytes 3538948
  47.9 34.5 %copy-start.1 = (bf16[2,2,256,256]{3,2,1,0:T(8,128)(2,1)S(1)}, bf16[2,2,256,256]{3,2,1,0:T(8,128)(2,1)}, u32[]{:S(2)}) copy-start(bf16[2,2,256,256]{3,2,1,0:T(8,128)(2,1)} %param.16) | copy-start | bytes 1572868
  47.9 34.5 %copy-start.4 = (f32[1,256]{1,0:T(1,128)S(1)}, f32[1,256]{1,0:T(1,128)}, u32[]{:S(2)}) copy-start(f32[1,256]{1,0:T(1,128)} %bias_ref.3) | copy-start | bytes 3076
  48.0 34.5 %copy-start.5 = (f32[256]{0:T(256)S(1)}, f32[256]{0:T(256)}, u32[]{:S(2)}) copy-start(f32[256]{0:T(256)} %param.17) | copy-start | bytes 3076
  48.0 4.3 %collective-permute-start.6 = (bf16[8,196,256]{2,0,1:T(8,128)(2,1)S(1)}, bf16[8,196,256]{2,0,1:T(8,128)(2,1)S(1)}, u32[]{:S(2)}, u32[]{:S(2)}) collective-permute-start(bf16[8,196,256]{2,0,1:T(8,128)(2,1)S(1)} %copy.13), channel_id=1, source_target_pairs={{0,1},{1,0},{2,3},{3,2},{4,5},{5,4},{6,7},{7,6},{8,9},{9,8},{10,11... | collective-permute-start | bytes 2408456 | tf_op jit(solution)/shard_map/ppermute | solution.py:381
  52.5 12.6 %collective-permute-start.7 = (bf16[3,196,256]{2,1,0:T(8,128)(2,1)S(1)}, bf16[3,196,256]{2,1,0:T(8,128)(2,1)S(1)}, u32[]{:S(2)}, u32[]{:S(2)}) collective-permute-start(bf16[3,196,256]{2,1,0:T(8,128)(2,1)S(1)} %add_convert_fusion), channel_id=1, source_target_pairs={{0,2},{1,15},{2,4},{3,1},{4,6},{5,3},{6,8},{7,5},{8,10},{9,7},{10,... | collective-permute-start | bytes 903176 | tf_op jit(solution)/shard_map/ppermute | solution.py:385
  57.0 8.1 %collective-permute-start.8 = (bf16[2,196,256]{2,1,0:T(8,128)(2,1)S(1)}, bf16[2,196,256]{2,1,0:T(8,128)(2,1)S(1)}, u32[]{:S(2)}, u32[]{:S(2)}) collective-permute-start(bf16[2,196,256]{2,1,0:T(8,128)(2,1)S(1)} %add_convert_fusion.1), channel_id=1, source_target_pairs={{0,14},{1,3},{2,0},{3,5},{4,2},{5,7},{6,4},{7,9},{8,6},{9,11},{10,... | collective-permute-start | bytes 602120 | tf_op jit(solution)/shard_map/ppermute | solution.py:385
  65.3 9.8 %collective-permute-start.10 = (bf16[196,256]{1,0:T(8,128)(2,1)S(1)}, bf16[196,256]{1,0:T(8,128)(2,1)S(1)}, u32[]{:S(2)}, u32[]{:S(2)}) collective-permute-start(bf16[196,256]{1,0:T(8,128)(2,1)S(1)} %get-tuple-element.26), channel_id=1, source_target_pairs={{0,12},{1,5},{2,14},{3,7},{4,0},{5,9},{6,2},{7,11},{8,4},{9,13},{1... | collective-permute-start | bytes 301064 | tf_op jit(solution)/shard_map/ppermute | solution.py:385
  71.7 10.8 %collective-permute-start.9 = (bf16[196,256]{1,0:T(8,128)(2,1)S(1)}, bf16[196,256]{1,0:T(8,128)(2,1)S(1)}, u32[]{:S(2)}, u32[]{:S(2)}) collective-permute-start(bf16[196,256]{1,0:T(8,128)(2,1)S(1)} %get-tuple-element.27), channel_id=1, source_target_pairs={{0,6},{1,11},{2,8},{3,13},{4,10},{5,15},{6,12},{7,1},{8,14},{9,3},... | collective-permute-start | bytes 301064 | tf_op jit(solution)/shard_map/ppermute | solution.py:385

commit v5 on v4

--- a/solution.py
+++ b/solution.py
@@ -10,6 +10,7 @@
 POOL = 14
 SIDE = 16
 LANES = 128
+PATCH = 200
 TILE = 16
 FIRST = 33
 SECOND = 32
@@ -36,8 +37,16 @@
     )(*args)
 
 
-def columns_kernel(tile_ref, lead_ref, tail_ref, rim_ref, flat_ref):
+def columns_kernel(
+    tile_ref, bias_ref, boxes_ref, owner_ref,
+    lead_ref, tail_ref, rim_ref, held_ref, held_bias_ref, held_boxes_ref, held_owner_ref,
+    flat_ref,
+):
     rows, width, channels = tile_ref.shape
+    held_ref[...] = tile_ref[...]
+    held_bias_ref[...] = bias_ref[...]
+    held_boxes_ref[...] = boxes_ref[...]
+    held_owner_ref[...] = owner_ref[...]
     for out_ref, first, start in ((lead_ref, 0, 0), (tail_ref, TILE - 2, width - TILE)):
         block = tile_ref[:, pl.ds(start, TILE), :].astype(F32).reshape(rows * TILE, channels)
         for h in range(channels // LANES):
@@ -69,16 +78,17 @@
         up_ref[count + i] = part[i % 2, 0:TILE]
 
 
-def exchange(features):
+def exchange(features, *small):
     rows, cols, channels = features.shape
     vmem = pl.BlockSpec(memory_space=pltpu.VMEM)
     below = shift(features, "row", -1)
     whole = cols // TILE
     pair = jax.ShapeDtypeStruct((2, rows, channels), BF16)
     rim = jax.ShapeDtypeStruct((3 * whole, TILE, channels), BF16)
-    lead, tail, rim = call(
-        columns_kernel, (pair, pair, rim), [vmem],
-        [pltpu.VMEM((channels // LANES, rows * TILE, LANES), F32)], 4, 10**5, features,
+    held = tuple(jax.ShapeDtypeStruct(value.shape, value.dtype) for value in (features,) + small)
+    lead, tail, rim, *held = call(
+        columns_kernel, (pair, pair, rim) + held, [vmem] * 4,
+        [pltpu.VMEM((channels // LANES, rows * TILE, LANES), F32)], 8, 10**5, features, *small,
     )
     left = shift(tail, "col", 1)
     right = shift(lead, "col", -1)
@@ -95,13 +105,12 @@
     )
     sides = shift(own_sides, "row", -1)
     after = shift(to_up, "row", -2)
-    return below, own_sides, sides, above, after
-
-
-def plan_kernel(boxes_ref, owner_ref, at_ref, by_ref, *, rows, cols, axes):
+    return below, own_sides, sides, above, after, held
+
+
+def plan(boxes_ref, owner_ref, at_ref, by_ref, rows, cols, chips):
     row, col = lax.axis_index("row"), lax.axis_index("col")
-    count = boxes_ref.shape[0]
-    chips = axes[1] // 2
+    count = boxes_ref.shape[1]
     slot = lax.broadcasted_iota(jnp.int32, (count, LANES), 0)
     bins = lax.broadcasted_iota(jnp.int32, (count, LANES), 1).astype(F32)
     core = jnp.where(slot < chips, col % 2, 1 - col % 2)
@@ -115,7 +124,7 @@
     fields = [jnp.zeros_like(slot) for _ in range(4)]
     for k in range(count):
         here = wanted == owner_ref[0, k]
-        fields = [jnp.where(here, boxes_ref[k, f], fields[f]) for f in range(4)]
+        fields = [jnp.where(here, boxes_ref[f, k], fields[f]) for f in range(4)]
     for dim, start, size in ((0, row * rows, 2 * rows), (1, col * cols, cols)):
         lower, extent = fields[dim].astype(F32), fields[dim + 2].astype(F32)
         centre = lower + (bins + 0.5) * extent / POOL - 0.5
@@ -126,11 +135,11 @@
             index = place.astype(jnp.int32) - start
             inside = (index >= 0) & (index < size)
             at = jnp.minimum(jnp.maximum(index, 0), size - 1)
-            at_ref[2 * dim + t] = at[:, :POOL]
-            by_ref[2 * dim + t] = jnp.where(inside, weight, 0.0)[:, :POOL]
+            at_ref[2 * dim + t] = at
+            by_ref[2 * dim + t] = jnp.where(inside, weight, 0.0)
     left, right = fields[1], fields[1] + fields[3]
     hit = (left < (col + 1) * cols) & (right > col * cols)
-    at_ref[4] = jnp.where(hit, 1, 0)[:, :POOL]
+    at_ref[4] = jnp.where(hit, 1, 0)
 
 
 def spread(dst, start, value, edge_ref, sides, offset):
@@ -156,11 +165,12 @@
 
 
 def main_kernel(
-    at_ref, by_ref,
+    boxes_ref, owner_ref,
     own_ref, below_ref, own_sides_ref, sides_ref, above_ref, after_ref,
     weight_hbm, bias_ref,
     tower_ref, mine_ref, other_ref,
-    wide_ref, mid_ref, band_ref, comb_ref, patch_ref, strip_ref, inner_ref, weight_ref, sems, *, last_row, last_col,
+    wide_ref, mid_ref, band_ref, comb_ref, patch_ref, strip_ref, inner_ref, weight_ref,
+    at_tile, by_tile, at_ref, by_ref, sems, *, last_row, last_col,
 ):
     rows, width, channels = own_ref.shape
     half = mine_ref.shape[0]
@@ -168,8 +178,14 @@
     loads = [
         pltpu.make_async_copy(weight_hbm.at[l], weight_ref.at[l], sems.at[l]) for l in range(2)
     ]
-    for load in loads:
-        load.start()
+    loads[0].start()
+    plan(boxes_ref, owner_ref, at_tile, by_tile, rows, width, (last_col + 1) // 2)
+    moves = [
+        pltpu.make_async_copy(at_tile, at_ref, sems.at[2]),
+        pltpu.make_async_copy(by_tile, by_ref, sems.at[3]),
+    ]
+    for move in moves:
+        move.start()
     row, col = lax.axis_index("row"), lax.axis_index("col")
     for c in range(6):
         strip_ref[c, 0:2, :] = above_ref[2 * whole + c].astype(F32)[TILE - 2 : TILE]
@@ -192,6 +208,7 @@
     wide_ref[3 + 2 * rows] = jnp.zeros(wide_ref.shape[1:], BF16)
 
     loads[0].wait()
+    loads[1].start()
     tall = inner_ref.shape[1]
     sides = []
     for side in range(2):
@@ -239,6 +256,8 @@
         return carry
 
     lax.fori_loop(0, 2 * rows // SECOND, second, 0)
+    for move in moves:
+        move.wait()
     halves = [(h, slice(h * LANES, (h + 1) * LANES)) for h in range(channels // LANES)]
     for side, out_ref in ((1, other_ref), (0, mine_ref)):
         def region(m, carry):
@@ -259,7 +278,7 @@
                         total = total + comb_ref[h, high, :] * by_ref[3, n, q]
                         patch_ref[h, pl.ds(q, SIDE, stride=POOL), :] = total
                 for h, lanes in halves:
-                    out_ref[m, :, lanes] = patch_ref[h, pl.ds(0, POOL * POOL), :].astype(BF16)
+                    out_ref[m, :, lanes] = patch_ref[h, pl.ds(0, PATCH), :].astype(BF16)
 
             @pl.when(at_ref[4, n, 0] == 0)
             def _():
@@ -272,22 +291,12 @@
 
 def tower_and_pool(features, weight, bias, boxes, owner_slot):
     rows, cols, channels = features.shape
-    below, own_sides, sides, above, after = exchange(features)
-    above, boxes = lax.optimization_barrier((above, boxes))
-    count = boxes.shape[0]
+    below, own_sides, sides, above, after, held = exchange(features, bias, boxes.T, owner_slot)
+    features, bias, boxes, owner_slot = held
+    count = boxes.shape[1]
     smem = pl.BlockSpec(memory_space=pltpu.SMEM)
     vmem = pl.BlockSpec(memory_space=pltpu.VMEM)
-    at, by = call(
-        functools.partial(
-            plan_kernel, rows=rows, cols=cols, axes=(lax.axis_size("row"), lax.axis_size("col"))
-        ),
-        (
-            jax.ShapeDtypeStruct((5, count, POOL), jnp.int32),
-            jax.ShapeDtypeStruct((4, count, POOL), F32),
-        ),
-        [smem, smem], [], 4, 10**5, boxes, owner_slot,
-    )
-    patches = jax.ShapeDtypeStruct((count // 2, POOL * POOL, channels), BF16)
+    patches = jax.ShapeDtypeStruct((count // 2, PATCH, channels), BF16)
     kernel = functools.partial(
         main_kernel, last_row=lax.axis_size("row") - 1, last_col=lax.axis_size("col") - 1
     )
@@ -304,10 +313,14 @@
             pltpu.VMEM((6, 2 * rows + 24, channels), F32),
             pltpu.VMEM((2, 2 * rows + 16, channels), F32),
             pltpu.VMEM((2, 9 * channels, channels), BF16),
-            pltpu.SemaphoreType.DMA((2,)),
+            pltpu.VMEM((5, count, LANES), jnp.int32),
+            pltpu.VMEM((4, count, LANES), F32),
+            pltpu.SMEM((5, count, LANES), jnp.int32),
+            pltpu.SMEM((4, count, LANES), F32),
+            pltpu.SemaphoreType.DMA((4,)),
         ],
         51, 6 * 10**9,
-        at, by, features, below, own_sides, sides, above, after,
+        boxes, owner_slot, features, below, own_sides, sides, above, after,
         weight.reshape(2, 9 * channels, channels), bias,
     )
 
@@ -322,7 +335,7 @@
     parts = (mine_ref[7], swapped_ref[7], ahead_ref[1], three_ref[...], two_ref[...])
     pooled = sum(part.astype(F32) for part in parts).astype(BF16).astype(F32)
     for h, lanes in halves:
-        sum_ref[h, 8 : 8 + POOL * POOL, :] = pooled[:, lanes]
+        sum_ref[h, 8 : 8 + PATCH, :] = pooled[:, lanes]
     blank = jnp.zeros(wide_ref.shape[1:], BF16)
     wide_ref[0] = blank
     wide_ref[POOL + 1] = blank

time: 84.8 us -> 81.9 us (0.966)
  local copies, waits for them, and re-layouts: 5.67 us -> 3.09 us
  waiting for transfers between devices: 22.2 us -> 24.2 us
  Pallas kernels: 13.6 us -> 11.8 us
  starting transfers between devices: 41.6 us -> 40.6 us
    ppermute x6, waiting for transfers between devices: 7.54 us -> 9.72 us  [shift(): lax.ppermute(value, axis, [(i, i + step) for i in devices if i + step in...]
    pallas_call x6 -> x5, Pallas kernels: 13.6 us -> 11.8 us  [call(): pl.pallas_call(kernel, out_shape=out_shape, in_specs=in_specs, out_specs=...]
    ppermute x4, starting transfers between devices: 17.2 us -> 15.6 us  [send(): lax.ppermute(value, 'col', [(i, (i + steps[i]) % peers) for i in range(pe...]
    pallas_call x1 -> x0, local copies, waits for them, and re-layouts: 1.3 us -> none  [call(): pl.pallas_call(kernel, out_shape=out_shape, in_specs=in_specs, out_specs=...]
  transfers between devices with their start and end apart: 11 -> 11, of which waited for: 6 -> 5; matrix products, arithmetic and copies ran while one was open for 1% -> 0% of each run, Pallas kernels for 1% -> 0%
where the time goes in v5:
time: 81.9 us; the launch traced here: 80.8 us
  starting transfers between devices  40.6 us (50%)
  waiting for transfers between devices  24.2 us (30%)
  Pallas kernels  11.8 us (14%)
  local copies, waits for them, and re-layouts  3.09 us (4%)
  between operations  0.83 us (1%)
    ppermute x6, starting transfers between devices, shift(): lax.ppermute(value, axis, [(i, i + step) for i in devices if i + step in...  22.3 us
    ppermute x4, starting transfers between devices, send(): lax.ppermute(value, 'col', [(i, (i + steps[i]) % peers) for i in range(pe...  15.6 us
    ppermute x4, waiting for transfers between devices, send(): lax.ppermute(value, 'col', [(i, (i + steps[i]) % peers) for i in range(pe...  12.5 us
    pallas_call x5, Pallas kernels, call(): pl.pallas_call(kernel, out_shape=out_shape, in_specs=in_specs, out_specs=...  11.8 us
    ppermute x6, waiting for transfers between devices, shift(): lax.ppermute(value, axis, [(i, i + step) for i in devices if i + step in...  9.72 us
    unnamed x16, local copies, waits for them, and re-layouts  3.09 us
    ppermute x1, starting transfers between devices, per_device(): swapped = lax.ppermute(other, 'col', [(i, i ^ 1) for i in range(peers)])  2.79 us
    ppermute x1, waiting for transfers between devices, per_device(): swapped = lax.ppermute(other, 'col', [(i, i ^ 1) for i in range(peers)])  1.94 us
  transfers between devices with their start and end apart: 11, of which 5 were waited for; matrix products, arithmetic and copies ran while one was open for 0% of the time, Pallas kernels for 0%

profile of v5, /device:TPU:6, one launch (start us, length us, event | category | flops | bytes accessed | tf_op | source)
XLA Modules:
  0.0 80.8 jit_solution(14047557149867417465)
XLA Ops:
  0.6 11.2 %collective-permute-start = (bf16[32,32,256]{2,1,0:T(8,128)(2,1)}, bf16[32,32,256]{2,1,0:T(8,128)(2,1)S(1)}, u32[]{:S(2)}, u32[]{:S(2)}) collective-permute-start(bf16[32,32,256]{2,1,0:T(8,128)(2,1)} %tile_ref.1), channel_id=1, source_target_pairs={{16,0},{32,16},{48,32},{64,48},{80,64},{96,80},{112,96},{128,112},... | collective-permute-start | bytes 1572872 | tf_op jit(solution)/shard_map/ppermute | solution.py:24
  11.9 1.0 %copy-done.2 = bf16[32,32,256]{2,1,0:T(8,128)(2,1)S(1)} copy-done((bf16[32,32,256]{2,1,0:T(8,128)(2,1)S(1)}, bf16[32,32,256]{2,1,0:T(8,128)(2,1)}, u32[]{:S(2)}) %copy-start.2) | copy-done | bytes 524312
  12.9 0.7 copy-done.3
  13.6 0.7 copy-done.4
  14.3 0.7 copy-done.7
  14.9 0.1 shard_map.104
  15.1 1.5 %collective-permute-start.1 = (bf16[2,32,256]{2,1,0:T(8,128)(2,1)S(1)}, bf16[2,32,256]{2,1,0:T(8,128)(2,1)S(1)}, u32[]{:S(2)}, u32[]{:S(2)}) collective-permute-start(bf16[2,32,256]{2,1,0:T(8,128)(2,1)S(1)} %get-tuple-element.18.tail_ref), channel_id=1, source_target_pairs={{0,1},{1,2},{2,3},{3,4},{4,5},{5,6},{6,7},{7,8},{8,9},{9,10},{10,1... | collective-permute-start | bytes 98312 | tf_op jit(solution)/shard_map/ppermute | solution.py:24
  16.5 1.3 %collective-permute-start.2 = (bf16[2,32,256]{2,1,0:T(8,128)(2,1)S(1)}, bf16[2,32,256]{2,1,0:T(8,128)(2,1)S(1)}, u32[]{:S(2)}, u32[]{:S(2)}) collective-permute-start(bf16[2,32,256]{2,1,0:T(8,128)(2,1)S(1)} %get-tuple-element.19.lead_ref), channel_id=1, source_target_pairs={{1,0},{2,1},{3,2},{4,3},{5,4},{6,5},{7,6},{8,7},{9,8},{10,9},{11,1... | collective-permute-start | bytes 98312 | tf_op jit(solution)/shard_map/ppermute | solution.py:24
  17.8 0.0 collective-permute-done.1.left_ref
  17.8 3.4 %collective-permute-done.2.right_ref = bf16[2,32,256]{2,1,0:T(8,128)(2,1)S(1)} collective-permute-done((bf16[2,32,256]{2,1,0:T(8,128)(2,1)S(1)}, bf16[2,32,256]{2,1,0:T(8,128)(2,1)S(1)}, u32[]{:S(2)}, u32[]{:S(2)}) %collective-permute-start.2) | collective-permute-done | bytes 32800 | tf_op jit(solution)/shard_map/ppermute | solution.py:24
  21.3 2.5 %collective-permute-start.3 = (bf16[6,32,256]{2,1,0:T(8,128)(2,1)S(1)}, bf16[6,32,256]{2,1,0:T(8,128)(2,1)S(1)}, u32[]{:S(2)}, u32[]{:S(2)}) collective-permute-start(bf16[6,32,256]{2,1,0:T(8,128)(2,1)S(1)} %get-tuple-element.20.own_sides_ref), channel_id=1, source_target_pairs={{16,0},{32,16},{48,32},{64,48},{80,64},{96,80},{112,96},{128,112},... | collective-permute-start | bytes 294920 | tf_op jit(solution)/shard_map/ppermute | solution.py:24
  23.8 3.4 %collective-permute-start.4 = (bf16[10,16,256]{2,1,0:T(8,128)(2,1)S(1)}, bf16[10,16,256]{2,1,0:T(8,128)(2,1)S(1)}, u32[]{:S(2)}, u32[]{:S(2)}) collective-permute-start(bf16[10,16,256]{2,1,0:T(8,128)(2,1)S(1)} %shard_map.106), channel_id=1, source_target_pairs={{0,16},{16,32},{32,48},{48,64},{64,80},{80,96},{96,112},{112,128},... | collective-permute-start | bytes 245768 | tf_op jit(solution)/shard_map/ppermute | solution.py:24
  27.2 2.5 %collective-permute-start.5 = (bf16[8,16,256]{2,1,0:T(8,128)(2,1)S(1)}, bf16[8,16,256]{2,1,0:T(8,128)(2,1)S(1)}, u32[]{:S(2)}, u32[]{:S(2)}) collective-permute-start(bf16[8,16,256]{2,1,0:T(8,128)(2,1)S(1)} %get-tuple-element.21), channel_id=1, source_target_pairs={{32,0},{48,16},{64,32},{80,48},{96,64},{112,80},{128,96},{144,112}... | collective-permute-start | bytes 196616 | tf_op jit(solution)/shard_map/ppermute | solution.py:24
  29.6 6.3 %collective-permute-done.5.after_ref = bf16[8,16,256]{2,1,0:T(8,128)(2,1)S(1)} collective-permute-done((bf16[8,16,256]{2,1,0:T(8,128)(2,1)S(1)}, bf16[8,16,256]{2,1,0:T(8,128)(2,1)S(1)}, u32[]{:S(2)}, u32[]{:S(2)}) %collective-permute-start.5) | collective-permute-done | bytes 65568 | tf_op jit(solution)/shard_map/ppermute | solution.py:24
  35.9 0.0 collective-permute-done.4.above_ref
  35.9 10.0 %shard_map.107 = (bf16[32,32,256]{2,1,0:T(8,128)(2,1)}, bf16[8,200,256]{2,1,0:T(8,128)(2,1)S(1)}, bf16[8,200,256]{2,1,0:T(8,128)(2,1)S(1)}) custom-call(s32[4,16]{1,0:T(4,128)S(1)} %get-tuple-element.14.boxes_ref, s32[1,16]{1,0:T(1,128)S(1)} %get-tuple-element.15.owner_ref, bf16[32,32,256]{2,1,0:T(8,128)(2,1)S(1)} %get-tuple-element.16.own_ref, ...), custom_call_target="tpu_custom_call" | custom-call | flops 6000000000 | bytes 1000000 | tf_op jit(solution)/shard_map/pallas_call | solution.py:29
  45.9 0.0 copy-start
  45.9 0.0 copy-start.1
  45.9 0.0 copy-start.5
  45.9 0.0 copy-start.6
  45.9 2.8 %collective-permute-start.6 = (bf16[8,200,256]{2,1,0:T(8,128)(2,1)S(1)}, bf16[8,200,256]{2,1,0:T(8,128)(2,1)S(1)}, u32[]{:S(2)}, u32[]{:S(2)}) collective-permute-start(bf16[8,200,256]{2,1,0:T(8,128)(2,1)S(1)} %get-tuple-element.25), channel_id=1, source_target_pairs={{0,1},{1,0},{2,3},{3,2},{4,5},{5,4},{6,7},{7,6},{8,9},{9,8},{10,11... | collective-permute-start | bytes 2457608 | tf_op jit(solution)/shard_map/ppermute | solution.py:394
  48.7 1.9 %collective-permute-done.6.swapped_ref = bf16[8,200,256]{2,1,0:T(8,128)(2,1)S(1)} collective-permute-done((bf16[8,200,256]{2,1,0:T(8,128)(2,1)S(1)}, bf16[8,200,256]{2,1,0:T(8,128)(2,1)S(1)}, u32[]{:S(2)}, u32[]{:S(2)}) %collective-permute-start.6) | collective-permute-done | bytes 819232 | tf_op jit(solution)/shard_map/ppermute | solution.py:394
  50.7 0.1 add_convert_fusion
  50.7 5.2 %collective-permute-start.7 = (bf16[3,200,256]{2,1,0:T(8,128)(2,1)S(1)}, bf16[3,200,256]{2,1,0:T(8,128)(2,1)S(1)}, u32[]{:S(2)}, u32[]{:S(2)}) collective-permute-start(bf16[3,200,256]{2,1,0:T(8,128)(2,1)S(1)} %add_convert_fusion), channel_id=1, source_target_pairs={{0,2},{1,15},{2,4},{3,1},{4,6},{5,3},{6,8},{7,5},{8,10},{9,7},{10,... | collective-permute-start | bytes 921608 | tf_op jit(solution)/shard_map/ppermute | solution.py:398
  56.0 0.1 add_convert_fusion.1
  56.0 1.9 %collective-permute-start.8 = (bf16[2,200,256]{2,1,0:T(8,128)(2,1)S(1)}, bf16[2,200,256]{2,1,0:T(8,128)(2,1)S(1)}, u32[]{:S(2)}, u32[]{:S(2)}) collective-permute-start(bf16[2,200,256]{2,1,0:T(8,128)(2,1)S(1)} %add_convert_fusion.1), channel_id=1, source_target_pairs={{0,14},{1,3},{2,0},{3,5},{4,2},{5,7},{6,4},{7,9},{8,6},{9,11},{10,... | collective-permute-start | bytes 614408 | tf_op jit(solution)/shard_map/ppermute | solution.py:398
  58.0 5.7 %collective-permute-done.8 = bf16[2,200,256]{2,1,0:T(8,128)(2,1)S(1)} collective-permute-done((bf16[2,200,256]{2,1,0:T(8,128)(2,1)S(1)}, bf16[2,200,256]{2,1,0:T(8,128)(2,1)S(1)}, u32[]{:S(2)}, u32[]{:S(2)}) %collective-permute-start.8) | collective-permute-done | bytes 204832 | tf_op jit(solution)/shard_map/ppermute | solution.py:398
  63.7 0.1 fusion.1
  63.8 3.7 %collective-permute-start.10 = (bf16[200,256]{1,0:T(8,128)(2,1)S(1)}, bf16[200,256]{1,0:T(8,128)(2,1)S(1)}, u32[]{:S(2)}, u32[]{:S(2)}) collective-permute-start(bf16[200,256]{1,0:T(8,128)(2,1)S(1)} %get-tuple-element.26), channel_id=1, source_target_pairs={{0,12},{1,5},{2,14},{3,7},{4,0},{5,9},{6,2},{7,11},{8,4},{9,13},{1... | collective-permute-start | bytes 307208 | tf_op jit(solution)/shard_map/ppermute | solution.py:398
  67.5 4.7 %collective-permute-start.9 = (bf16[200,256]{1,0:T(8,128)(2,1)S(1)}, bf16[200,256]{1,0:T(8,128)(2,1)S(1)}, u32[]{:S(2)}, u32[]{:S(2)}) collective-permute-start(bf16[200,256]{1,0:T(8,128)(2,1)S(1)} %get-tuple-element.27), channel_id=1, source_target_pairs={{0,6},{1,11},{2,8},{3,13},{4,10},{5,15},{6,12},{7,1},{8,14},{9,3},... | collective-permute-start | bytes 307208 | tf_op jit(solution)/shard_map/ppermute | solution.py:398
  72.3 6.8 %collective-permute-done.9.three_ref = bf16[200,256]{1,0:T(8,128)(2,1)S(1)} collective-permute-done((bf16[200,256]{1,0:T(8,128)(2,1)S(1)}, bf16[200,256]{1,0:T(8,128)(2,1)S(1)}, u32[]{:S(2)}, u32[]{:S(2)}) %collective-permute-start.9) | collective-permute-done | bytes 102432 | tf_op jit(solution)/shard_map/ppermute | solution.py:398
  79.1 1.7 %shard_map.108 = bf16[1,28,28,256]{3,2,1,0:T(8,128)(2,1)} custom-call(bf16[8,200,256]{2,1,0:T(8,128)(2,1)S(1)} %get-tuple-element.24.mine_ref, bf16[8,200,256]{2,1,0:T(8,128)(2,1)S(1)} %collective-permute-done.6.swapped_ref, bf16[3,200,256]{2,1,0:T(8,128)(2,1)S(1)} %collective-permute-done.7.ahead_ref, ...), custom_call_target="tpu_custom_call" | custom-call | flops 1000000000 | bytes 1000000 | tf_op jit(solution)/shard_map/pallas_call | solution.py:29
  (14 shorter events, 0.0 us)
Async XLA Ops:
  0.6 35.3 %collective-permute-start = (bf16[32,32,256]{2,1,0:T(8,128)(2,1)}, bf16[32,32,256]{2,1,0:T(8,128)(2,1)S(1)}, u32[]{:S(2)}, u32[]{:S(2)}) collective-permute-start(bf16[32,32,256]{2,1,0:T(8,128)(2,1)} %tile_ref.1), channel_id=1, source_target_pairs={{16,0},{32,16},{48,32},{64,48},{80,64},{96,80},{112,96},{128,112},... | collective-permute-start | bytes 1572872 | tf_op jit(solution)/shard_map/ppermute | solution.py:24
  11.9 1.1 %copy-start.2 = (bf16[32,32,256]{2,1,0:T(8,128)(2,1)S(1)}, bf16[32,32,256]{2,1,0:T(8,128)(2,1)}, u32[]{:S(2)}) copy-start(bf16[32,32,256]{2,1,0:T(8,128)(2,1)} %tile_ref.1) | copy-start | bytes 1572868
  12.9 0.7 copy-start.3
  13.6 0.7 copy-start.4
  14.3 0.7 copy-start.7
  15.1 2.8 %collective-permute-start.1 = (bf16[2,32,256]{2,1,0:T(8,128)(2,1)S(1)}, bf16[2,32,256]{2,1,0:T(8,128)(2,1)S(1)}, u32[]{:S(2)}, u32[]{:S(2)}) collective-permute-start(bf16[2,32,256]{2,1,0:T(8,128)(2,1)S(1)} %get-tuple-element.18.tail_ref), channel_id=1, source_target_pairs={{0,1},{1,2},{2,3},{3,4},{4,5},{5,6},{6,7},{7,8},{8,9},{9,10},{10,1... | collective-permute-start | bytes 98312 | tf_op jit(solution)/shard_map/ppermute | solution.py:24
  16.5 4.7 %collective-permute-start.2 = (bf16[2,32,256]{2,1,0:T(8,128)(2,1)S(1)}, bf16[2,32,256]{2,1,0:T(8,128)(2,1)S(1)}, u32[]{:S(2)}, u32[]{:S(2)}) collective-permute-start(bf16[2,32,256]{2,1,0:T(8,128)(2,1)S(1)} %get-tuple-element.19.lead_ref), channel_id=1, source_target_pairs={{1,0},{2,1},{3,2},{4,3},{5,4},{6,5},{7,6},{8,7},{9,8},{10,9},{11,1... | collective-permute-start | bytes 98312 | tf_op jit(solution)/shard_map/ppermute | solution.py:24
  21.3 14.6 %collective-permute-start.3 = (bf16[6,32,256]{2,1,0:T(8,128)(2,1)S(1)}, bf16[6,32,256]{2,1,0:T(8,128)(2,1)S(1)}, u32[]{:S(2)}, u32[]{:S(2)}) collective-permute-start(bf16[6,32,256]{2,1,0:T(8,128)(2,1)S(1)} %get-tuple-element.20.own_sides_ref), channel_id=1, source_target_pairs={{16,0},{32,16},{48,32},{64,48},{80,64},{96,80},{112,96},{128,112},... | collective-permute-start | bytes 294920 | tf_op jit(solution)/shard_map/ppermute | solution.py:24
  23.8 12.1 %collective-permute-start.4 = (bf16[10,16,256]{2,1,0:T(8,128)(2,1)S(1)}, bf16[10,16,256]{2,1,0:T(8,128)(2,1)S(1)}, u32[]{:S(2)}, u32[]{:S(2)}) collective-permute-start(bf16[10,16,256]{2,1,0:T(8,128)(2,1)S(1)} %shard_map.106), channel_id=1, source_target_pairs={{0,16},{16,32},{32,48},{48,64},{64,80},{80,96},{96,112},{112,128},... | collective-permute-start | bytes 245768 | tf_op jit(solution)/shard_map/ppermute | solution.py:24
  27.2 8.7 %collective-permute-start.5 = (bf16[8,16,256]{2,1,0:T(8,128)(2,1)S(1)}, bf16[8,16,256]{2,1,0:T(8,128)(2,1)S(1)}, u32[]{:S(2)}, u32[]{:S(2)}) collective-permute-start(bf16[8,16,256]{2,1,0:T(8,128)(2,1)S(1)} %get-tuple-element.21), channel_id=1, source_target_pairs={{32,0},{48,16},{64,32},{80,48},{96,64},{112,80},{128,96},{144,112}... | collective-permute-start | bytes 196616 | tf_op jit(solution)/shard_map/ppermute | solution.py:24
  45.9 33.2 %copy-start = (bf16[1,3,3,256,256]{4,3,2,1,0:T(8,128)(2,1)S(1)}, bf16[1,3,3,256,256]{4,3,2,1,0:T(8,128)(2,1)}, u32[]{:S(2)}) copy-start(bf16[1,3,3,256,256]{4,3,2,1,0:T(8,128)(2,1)} %param.14) | copy-start | bytes 3538948
  45.9 33.2 %copy-start.1 = (bf16[2,2,256,256]{3,2,1,0:T(8,128)(2,1)S(1)}, bf16[2,2,256,256]{3,2,1,0:T(8,128)(2,1)}, u32[]{:S(2)}) copy-start(bf16[2,2,256,256]{3,2,1,0:T(8,128)(2,1)} %param.16) | copy-start | bytes 1572868
  45.9 33.2 %copy-start.5 = (f32[1,256]{1,0:T(1,128)S(1)}, f32[1,256]{1,0:T(1,128)}, u32[]{:S(2)}) copy-start(f32[1,256]{1,0:T(1,128)} %bias_ref.3) | copy-start | bytes 3076
  45.9 33.2 %copy-start.6 = (f32[256]{0:T(256)S(1)}, f32[256]{0:T(256)}, u32[]{:S(2)}) copy-start(f32[256]{0:T(256)} %param.17) | copy-start | bytes 3076
  45.9 4.7 %collective-permute-start.6 = (bf16[8,200,256]{2,1,0:T(8,128)(2,1)S(1)}, bf16[8,200,256]{2,1,0:T(8,128)(2,1)S(1)}, u32[]{:S(2)}, u32[]{:S(2)}) collective-permute-start(bf16[8,200,256]{2,1,0:T(8,128)(2,1)S(1)} %get-tuple-element.25), channel_id=1, source_target_pairs={{0,1},{1,0},{2,3},{3,2},{4,5},{5,4},{6,7},{7,6},{8,9},{9,8},{10,11... | collective-permute-start | bytes 2457608 | tf_op jit(solution)/shard_map/ppermute | solution.py:394
  50.7 12.9 %collective-permute-start.7 = (bf16[3,200,256]{2,1,0:T(8,128)(2,1)S(1)}, bf16[3,200,256]{2,1,0:T(8,128)(2,1)S(1)}, u32[]{:S(2)}, u32[]{:S(2)}) collective-permute-start(bf16[3,200,256]{2,1,0:T(8,128)(2,1)S(1)} %add_convert_fusion), channel_id=1, source_target_pairs={{0,2},{1,15},{2,4},{3,1},{4,6},{5,3},{6,8},{7,5},{8,10},{9,7},{10,... | collective-permute-start | bytes 921608 | tf_op jit(solution)/shard_map/ppermute | solution.py:398
  56.0 7.7 %collective-permute-start.8 = (bf16[2,200,256]{2,1,0:T(8,128)(2,1)S(1)}, bf16[2,200,256]{2,1,0:T(8,128)(2,1)S(1)}, u32[]{:S(2)}, u32[]{:S(2)}) collective-permute-start(bf16[2,200,256]{2,1,0:T(8,128)(2,1)S(1)} %add_convert_fusion.1), channel_id=1, source_target_pairs={{0,14},{1,3},{2,0},{3,5},{4,2},{5,7},{6,4},{7,9},{8,6},{9,11},{10,... | collective-permute-start | bytes 614408 | tf_op jit(solution)/shard_map/ppermute | solution.py:398
  63.8 8.5 %collective-permute-start.10 = (bf16[200,256]{1,0:T(8,128)(2,1)S(1)}, bf16[200,256]{1,0:T(8,128)(2,1)S(1)}, u32[]{:S(2)}, u32[]{:S(2)}) collective-permute-start(bf16[200,256]{1,0:T(8,128)(2,1)S(1)} %get-tuple-element.26), channel_id=1, source_target_pairs={{0,12},{1,5},{2,14},{3,7},{4,0},{5,9},{6,2},{7,11},{8,4},{9,13},{1... | collective-permute-start | bytes 307208 | tf_op jit(solution)/shard_map/ppermute | solution.py:398
  67.5 11.6 %collective-permute-start.9 = (bf16[200,256]{1,0:T(8,128)(2,1)S(1)}, bf16[200,256]{1,0:T(8,128)(2,1)S(1)}, u32[]{:S(2)}, u32[]{:S(2)}) collective-permute-start(bf16[200,256]{1,0:T(8,128)(2,1)S(1)} %get-tuple-element.27), channel_id=1, source_target_pairs={{0,6},{1,11},{2,8},{3,13},{4,10},{5,15},{6,12},{7,1},{8,14},{9,3},... | collective-permute-start | bytes 307208 | tf_op jit(solution)/shard_map/ppermute | solution.py:398

commit v6 on v5

--- a/solution.py
+++ b/solution.py
@@ -38,15 +38,10 @@
 
 
 def columns_kernel(
-    tile_ref, bias_ref, boxes_ref, owner_ref,
-    lead_ref, tail_ref, rim_ref, held_ref, held_bias_ref, held_boxes_ref, held_owner_ref,
-    flat_ref,
+    tile_ref, lead_ref, tail_ref, rim_ref, held_ref, flat_ref
 ):
     rows, width, channels = tile_ref.shape
     held_ref[...] = tile_ref[...]
-    held_bias_ref[...] = bias_ref[...]
-    held_boxes_ref[...] = boxes_ref[...]
-    held_owner_ref[...] = owner_ref[...]
     for out_ref, first, start in ((lead_ref, 0, 0), (tail_ref, TILE - 2, width - TILE)):
         block = tile_ref[:, pl.ds(start, TILE), :].astype(F32).reshape(rows * TILE, channels)
         for h in range(channels // LANES):
@@ -60,6 +55,12 @@
     rim_ref[2 * whole :] = tile_ref[0:1].reshape(whole, TILE, channels)
 
 
+def hold_kernel(*refs):
+    count = len(refs) // 2
+    for src_ref, dst_ref in zip(refs[:count], refs[count:]):
+        dst_ref[...] = src_ref[...]
+
+
 def down_kernel(rim_ref, left_ref, right_ref, lead_ref, tail_ref, down_ref):
     rows = left_ref.shape[1]
     parts = (left_ref, left_ref, lead_ref, tail_ref, right_ref, right_ref)
@@ -81,15 +82,16 @@
 def exchange(features, *small):
     rows, cols, channels = features.shape
     vmem = pl.BlockSpec(memory_space=pltpu.VMEM)
-    below = shift(features, "row", -1)
     whole = cols // TILE
     pair = jax.ShapeDtypeStruct((2, rows, channels), BF16)
     rim = jax.ShapeDtypeStruct((3 * whole, TILE, channels), BF16)
-    held = tuple(jax.ShapeDtypeStruct(value.shape, value.dtype) for value in (features,) + small)
-    lead, tail, rim, *held = call(
-        columns_kernel, (pair, pair, rim) + held, [vmem] * 4,
-        [pltpu.VMEM((channels // LANES, rows * TILE, LANES), F32)], 8, 10**5, features, *small,
-    )
+    held = jax.ShapeDtypeStruct(features.shape, BF16)
+    lead, tail, rim, held = call(
+        columns_kernel, (pair, pair, rim, held), [vmem],
+        [pltpu.VMEM((channels // LANES, rows * TILE, LANES), F32)], 8, 10**5, features,
+    )
+    late, lead, tail = lax.optimization_barrier((features, lead, tail))
+    below = shift(late, "row", -1)
     left = shift(tail, "col", 1)
     right = shift(lead, "col", -1)
     strips = (rim, left, right, lead, tail)
@@ -97,7 +99,9 @@
         down_kernel, (jax.ShapeDtypeStruct((2 * whole + 6, TILE, channels), BF16),),
         [vmem] * 5, [], 4, 10**5, *strips,
     )
-    above = shift(to_down, "row", 1)
+    above, small = lax.optimization_barrier((shift(to_down, "row", 1), small))
+    shapes = tuple(jax.ShapeDtypeStruct(value.shape, value.dtype) for value in small)
+    small = call(hold_kernel, shapes, [vmem] * len(small), [], 4, 10**5, *small)
     sides_shape = jax.ShapeDtypeStruct((6, rows, channels), BF16)
     up_shape = jax.ShapeDtypeStruct((whole + 6, TILE, channels), BF16)
     own_sides, to_up = call(
@@ -105,7 +109,7 @@
     )
     sides = shift(own_sides, "row", -1)
     after = shift(to_up, "row", -2)
-    return below, own_sides, sides, above, after, held
+    return below, own_sides, sides, above, after, held, small
 
 
 def plan(boxes_ref, owner_ref, at_ref, by_ref, rows, cols, chips):
@@ -291,8 +295,10 @@
 
 def tower_and_pool(features, weight, bias, boxes, owner_slot):
     rows, cols, channels = features.shape
-    below, own_sides, sides, above, after, held = exchange(features, bias, boxes.T, owner_slot)
-    features, bias, boxes, owner_slot = held
+    below, own_sides, sides, above, after, features, small = exchange(
+        features, bias, boxes.T, owner_slot
+    )
+    bias, boxes, owner_slot = small
     count = boxes.shape[1]
     smem = pl.BlockSpec(memory_space=pltpu.SMEM)
     vmem = pl.BlockSpec(memory_space=pltpu.VMEM)
@@ -403,8 +409,8 @@
 
     ahead = send(total(mine[0:3], swapped[0:3]), 1)
     back = send(total(mine[3:5], swapped[3:5]), -1)
+    two = send(total(mine[6], swapped[6], ahead[2], back[1]), -2)
     three = send(total(mine[5], swapped[5], ahead[0], back[0]), 3)
-    two = send(total(mine[6], swapped[6], ahead[2], back[1]), -2)
     parts = (mine, swapped, ahead, three, two)
     masks = head(parts, mask_weight, mask_bias, deconv_weight, deconv_bias)
     return tower, masks

time: 81.9 us -> 79.7 us (0.973)
  the two profiles are of different devices: /device:TPU:6 before, /device:TPU:42 now
where the time goes in v6:
time: 79.7 us; the launch traced here: 79.4 us
  starting transfers between devices  42.9 us (54%)
  waiting for transfers between devices  20.9 us (26%)
  Pallas kernels  11.5 us (14%)
  local copies, waits for them, and re-layouts  3.08 us (4%)
  between operations  0.82 us (1%)
    ppermute x6, starting transfers between devices, shift(): lax.ppermute(value, axis, [(i, i + step) for i in devices if i + step in...  24.8 us
    ppermute x4, starting transfers between devices, send(): lax.ppermute(value, 'col', [(i, (i + steps[i]) % peers) for i in range(pe...  14.9 us
    ppermute x4, waiting for transfers between devices, send(): lax.ppermute(value, 'col', [(i, (i + steps[i]) % peers) for i in range(pe...  13.6 us
    pallas_call x6, Pallas kernels, call(): pl.pallas_call(kernel, out_shape=out_shape, in_specs=in_specs, out_specs=...  11.5 us
    ppermute x6, waiting for transfers between devices, shift(): lax.ppermute(value, axis, [(i, i + step) for i in devices if i + step in...  5.34 us
    ppermute x1, starting transfers between devices, per_device(): swapped = lax.ppermute(other, 'col', [(i, i ^ 1) for i in range(peers)])  3.2 us
    unnamed x16, local copies, waits for them, and re-layouts  3.08 us
    ppermute x1, waiting for transfers between devices, per_device(): swapped = lax.ppermute(other, 'col', [(i, i ^ 1) for i in range(peers)])  1.94 us
  transfers between devices with their start and end apart: 11, of which 7 were waited for; matrix products, arithmetic and copies ran while one was open for 0% of the time, Pallas kernels for 0%

profile of v6, /device:TPU:42, one launch (start us, length us, event | category | flops | bytes accessed | tf_op | source)
XLA Modules:
  0.0 79.4 jit_solution(5779644083986245254)
XLA Ops:
  0.6 1.0 %copy-done.2 = bf16[32,32,256]{2,1,0:T(8,128)(2,1)S(1)} copy-done((bf16[32,32,256]{2,1,0:T(8,128)(2,1)S(1)}, bf16[32,32,256]{2,1,0:T(8,128)(2,1)}, u32[]{:S(2)}) %copy-start.2) | copy-done | bytes 524312
  1.7 0.1 shard_map.104
  1.8 10.9 %collective-permute-start.3 = (bf16[32,32,256]{2,1,0:T(8,128)(2,1)S(1)}, bf16[32,32,256]{2,1,0:T(8,128)(2,1)S(1)}, u32[]{:S(2)}, u32[]{:S(2)}) collective-permute-start(bf16[32,32,256]{2,1,0:T(8,128)(2,1)S(1)} %copy-done.2), channel_id=1, source_target_pairs={{16,0},{32,16},{48,32},{64,48},{80,64},{96,80},{112,96},{128,112},... | collective-permute-start | bytes 1572872 | tf_op jit(solution)/shard_map/ppermute | solution.py:24
  12.7 1.9 %collective-permute-start = (bf16[2,32,256]{2,1,0:T(8,128)(2,1)S(1)}, bf16[2,32,256]{2,1,0:T(8,128)(2,1)S(1)}, u32[]{:S(2)}, u32[]{:S(2)}) collective-permute-start(bf16[2,32,256]{2,1,0:T(8,128)(2,1)S(1)} %get-tuple-element.24.tail_ref), channel_id=1, source_target_pairs={{0,1},{1,2},{2,3},{3,4},{4,5},{5,6},{6,7},{7,8},{8,9},{9,10},{10,1... | collective-permute-start | bytes 98312 | tf_op jit(solution)/shard_map/ppermute | solution.py:24
  14.7 3.6 %collective-permute-start.1 = (bf16[2,32,256]{2,1,0:T(8,128)(2,1)S(1)}, bf16[2,32,256]{2,1,0:T(8,128)(2,1)S(1)}, u32[]{:S(2)}, u32[]{:S(2)}) collective-permute-start(bf16[2,32,256]{2,1,0:T(8,128)(2,1)S(1)} %get-tuple-element.25.lead_ref), channel_id=1, source_target_pairs={{1,0},{2,1},{3,2},{4,3},{5,4},{6,5},{7,6},{8,7},{9,8},{10,9},{11,1... | collective-permute-start | bytes 98312 | tf_op jit(solution)/shard_map/ppermute | solution.py:24
  18.3 1.6 %collective-permute-done.1.right_ref = bf16[2,32,256]{2,1,0:T(8,128)(2,1)S(1)} collective-permute-done((bf16[2,32,256]{2,1,0:T(8,128)(2,1)S(1)}, bf16[2,32,256]{2,1,0:T(8,128)(2,1)S(1)}, u32[]{:S(2)}, u32[]{:S(2)}) %collective-permute-start.1) | collective-permute-done | bytes 32800 | tf_op jit(solution)/shard_map/ppermute | solution.py:24
  19.9 2.5 %collective-permute-start.4 = (bf16[6,32,256]{2,1,0:T(8,128)(2,1)S(1)}, bf16[6,32,256]{2,1,0:T(8,128)(2,1)S(1)}, u32[]{:S(2)}, u32[]{:S(2)}) collective-permute-start(bf16[6,32,256]{2,1,0:T(8,128)(2,1)S(1)} %get-tuple-element.33.own_sides_ref), channel_id=1, source_target_pairs={{16,0},{32,16},{48,32},{64,48},{80,64},{96,80},{112,96},{128,112},... | collective-permute-start | bytes 294920 | tf_op jit(solution)/shard_map/ppermute | solution.py:24
  22.4 3.4 %collective-permute-start.2 = (bf16[10,16,256]{2,1,0:T(8,128)(2,1)S(1)}, bf16[10,16,256]{2,1,0:T(8,128)(2,1)S(1)}, u32[]{:S(2)}, u32[]{:S(2)}) collective-permute-start(bf16[10,16,256]{2,1,0:T(8,128)(2,1)S(1)} %shard_map.105), channel_id=1, source_target_pairs={{0,16},{16,32},{32,48},{48,64},{64,80},{80,96},{96,112},{112,128},... | collective-permute-start | bytes 245768 | tf_op jit(solution)/shard_map/ppermute | solution.py:24
  25.8 2.5 %collective-permute-start.5 = (bf16[8,16,256]{2,1,0:T(8,128)(2,1)S(1)}, bf16[8,16,256]{2,1,0:T(8,128)(2,1)S(1)}, u32[]{:S(2)}, u32[]{:S(2)}) collective-permute-start(bf16[8,16,256]{2,1,0:T(8,128)(2,1)S(1)} %get-tuple-element.35), channel_id=1, source_target_pairs={{32,0},{48,16},{64,32},{80,48},{96,64},{112,80},{128,96},{144,112}... | collective-permute-start | bytes 196616 | tf_op jit(solution)/shard_map/ppermute | solution.py:24
  28.2 3.3 %collective-permute-done.2.above_ref = bf16[10,16,256]{2,1,0:T(8,128)(2,1)S(1)} collective-permute-done((bf16[10,16,256]{2,1,0:T(8,128)(2,1)S(1)}, bf16[10,16,256]{2,1,0:T(8,128)(2,1)S(1)}, u32[]{:S(2)}, u32[]{:S(2)}) %collective-permute-start.2) | collective-permute-done | bytes 81952 | tf_op jit(solution)/shard_map/ppermute | solution.py:24
  31.5 0.7 copy-done.3
  32.2 0.7 copy-done.4
  32.9 0.7 copy-done.7
  33.6 0.5 collective-permute-done.5.after_ref
  34.0 9.6 %shard_map.108 = (bf16[32,32,256]{2,1,0:T(8,128)(2,1)}, bf16[8,200,256]{2,1,0:T(8,128)(2,1)S(1)}, bf16[8,200,256]{2,1,0:T(8,128)(2,1)S(1)}) custom-call(s32[4,16]{1,0:T(4,128)S(1)} %get-tuple-element.29.boxes_ref, s32[1,16]{1,0:T(1,128)S(1)} %get-tuple-element.30.owner_ref, bf16[32,32,256]{2,1,0:T(8,128)(2,1)S(1)} %get-tuple-element.31.own_ref, ...), custom_call_target="tpu_custom_call" | custom-call | flops 6000000000 | bytes 1000000 | tf_op jit(solution)/shard_map/pallas_call | solution.py:29
  43.7 0.0 copy-start
  43.7 0.0 copy-start.1
  43.7 0.0 copy-start.5
  43.7 0.0 copy-start.6
  43.7 3.2 %collective-permute-start.6 = (bf16[8,200,256]{2,1,0:T(8,128)(2,1)S(1)}, bf16[8,200,256]{2,1,0:T(8,128)(2,1)S(1)}, u32[]{:S(2)}, u32[]{:S(2)}) collective-permute-start(bf16[8,200,256]{2,1,0:T(8,128)(2,1)S(1)} %get-tuple-element.39), channel_id=1, source_target_pairs={{0,1},{1,0},{2,3},{3,2},{4,5},{5,4},{6,7},{7,6},{8,9},{9,8},{10,11... | collective-permute-start | bytes 2457608 | tf_op jit(solution)/shard_map/ppermute | solution.py:400
  46.9 1.9 %collective-permute-done.6.swapped_ref = bf16[8,200,256]{2,1,0:T(8,128)(2,1)S(1)} collective-permute-done((bf16[8,200,256]{2,1,0:T(8,128)(2,1)S(1)}, bf16[8,200,256]{2,1,0:T(8,128)(2,1)S(1)}, u32[]{:S(2)}, u32[]{:S(2)}) %collective-permute-start.6) | collective-permute-done | bytes 819232 | tf_op jit(solution)/shard_map/ppermute | solution.py:400
  48.9 0.1 add_convert_fusion
  49.0 2.4 %collective-permute-start.7 = (bf16[3,200,256]{2,1,0:T(8,128)(2,1)S(1)}, bf16[3,200,256]{2,1,0:T(8,128)(2,1)S(1)}, u32[]{:S(2)}, u32[]{:S(2)}) collective-permute-start(bf16[3,200,256]{2,1,0:T(8,128)(2,1)S(1)} %add_convert_fusion), channel_id=1, source_target_pairs={{0,2},{1,15},{2,4},{3,1},{4,6},{5,3},{6,8},{7,5},{8,10},{9,7},{10,... | collective-permute-start | bytes 921608 | tf_op jit(solution)/shard_map/ppermute | solution.py:404
  51.4 0.1 add_convert_fusion.1
  51.4 3.5 %collective-permute-start.8 = (bf16[2,200,256]{2,1,0:T(8,128)(2,1)S(1)}, bf16[2,200,256]{2,1,0:T(8,128)(2,1)S(1)}, u32[]{:S(2)}, u32[]{:S(2)}) collective-permute-start(bf16[2,200,256]{2,1,0:T(8,128)(2,1)S(1)} %add_convert_fusion.1), channel_id=1, source_target_pairs={{0,14},{1,3},{2,0},{3,5},{4,2},{5,7},{6,4},{7,9},{8,6},{9,11},{10,... | collective-permute-start | bytes 614408 | tf_op jit(solution)/shard_map/ppermute | solution.py:404
  54.9 4.4 %collective-permute-done.8 = bf16[2,200,256]{2,1,0:T(8,128)(2,1)S(1)} collective-permute-done((bf16[2,200,256]{2,1,0:T(8,128)(2,1)S(1)}, bf16[2,200,256]{2,1,0:T(8,128)(2,1)S(1)}, u32[]{:S(2)}, u32[]{:S(2)}) %collective-permute-start.8) | collective-permute-done | bytes 204832 | tf_op jit(solution)/shard_map/ppermute | solution.py:404
  59.3 0.1 fusion.1
  59.4 7.1 %collective-permute-start.10 = (bf16[200,256]{1,0:T(8,128)(2,1)S(1)}, bf16[200,256]{1,0:T(8,128)(2,1)S(1)}, u32[]{:S(2)}, u32[]{:S(2)}) collective-permute-start(bf16[200,256]{1,0:T(8,128)(2,1)S(1)} %get-tuple-element.40), channel_id=1, source_target_pairs={{0,12},{1,5},{2,14},{3,7},{4,0},{5,9},{6,2},{7,11},{8,4},{9,13},{1... | collective-permute-start | bytes 307208 | tf_op jit(solution)/shard_map/ppermute | solution.py:404
  66.5 1.9 %collective-permute-start.9 = (bf16[200,256]{1,0:T(8,128)(2,1)S(1)}, bf16[200,256]{1,0:T(8,128)(2,1)S(1)}, u32[]{:S(2)}, u32[]{:S(2)}) collective-permute-start(bf16[200,256]{1,0:T(8,128)(2,1)S(1)} %get-tuple-element.41), channel_id=1, source_target_pairs={{0,6},{1,11},{2,8},{3,13},{4,10},{5,15},{6,12},{7,1},{8,14},{9,3},... | collective-permute-start | bytes 307208 | tf_op jit(solution)/shard_map/ppermute | solution.py:404
  68.5 0.3 collective-permute-done.10.two_ref
  68.8 8.9 %collective-permute-done.9.three_ref = bf16[200,256]{1,0:T(8,128)(2,1)S(1)} collective-permute-done((bf16[200,256]{1,0:T(8,128)(2,1)S(1)}, bf16[200,256]{1,0:T(8,128)(2,1)S(1)}, u32[]{:S(2)}, u32[]{:S(2)}) %collective-permute-start.9) | collective-permute-done | bytes 102432 | tf_op jit(solution)/shard_map/ppermute | solution.py:404
  77.7 1.7 %shard_map.109 = bf16[1,28,28,256]{3,2,1,0:T(8,128)(2,1)} custom-call(bf16[8,200,256]{2,1,0:T(8,128)(2,1)S(1)} %get-tuple-element.38.mine_ref, bf16[8,200,256]{2,1,0:T(8,128)(2,1)S(1)} %collective-permute-done.6.swapped_ref, bf16[3,200,256]{2,1,0:T(8,128)(2,1)S(1)} %collective-permute-done.7.ahead_ref, ...), custom_call_target="tpu_custom_call" | custom-call | flops 1000000000 | bytes 1000000 | tf_op jit(solution)/shard_map/pallas_call | solution.py:29
  (15 shorter events, 0.0 us)
Async XLA Ops:
  0.6 1.0 %copy-start.2 = (bf16[32,32,256]{2,1,0:T(8,128)(2,1)S(1)}, bf16[32,32,256]{2,1,0:T(8,128)(2,1)}, u32[]{:S(2)}) copy-start(bf16[32,32,256]{2,1,0:T(8,128)(2,1)} %tile_ref.1) | copy-start | bytes 1572868
  1.8 32.2 %collective-permute-start.3 = (bf16[32,32,256]{2,1,0:T(8,128)(2,1)S(1)}, bf16[32,32,256]{2,1,0:T(8,128)(2,1)S(1)}, u32[]{:S(2)}, u32[]{:S(2)}) collective-permute-start(bf16[32,32,256]{2,1,0:T(8,128)(2,1)S(1)} %copy-done.2), channel_id=1, source_target_pairs={{16,0},{32,16},{48,32},{64,48},{80,64},{96,80},{112,96},{128,112},... | collective-permute-start | bytes 1572872 | tf_op jit(solution)/shard_map/ppermute | solution.py:24
  12.7 5.6 %collective-permute-start = (bf16[2,32,256]{2,1,0:T(8,128)(2,1)S(1)}, bf16[2,32,256]{2,1,0:T(8,128)(2,1)S(1)}, u32[]{:S(2)}, u32[]{:S(2)}) collective-permute-start(bf16[2,32,256]{2,1,0:T(8,128)(2,1)S(1)} %get-tuple-element.24.tail_ref), channel_id=1, source_target_pairs={{0,1},{1,2},{2,3},{3,4},{4,5},{5,6},{6,7},{7,8},{8,9},{9,10},{10,1... | collective-permute-start | bytes 98312 | tf_op jit(solution)/shard_map/ppermute | solution.py:24
  14.7 5.2 %collective-permute-start.1 = (bf16[2,32,256]{2,1,0:T(8,128)(2,1)S(1)}, bf16[2,32,256]{2,1,0:T(8,128)(2,1)S(1)}, u32[]{:S(2)}, u32[]{:S(2)}) collective-permute-start(bf16[2,32,256]{2,1,0:T(8,128)(2,1)S(1)} %get-tuple-element.25.lead_ref), channel_id=1, source_target_pairs={{1,0},{2,1},{3,2},{4,3},{5,4},{6,5},{7,6},{8,7},{9,8},{10,9},{11,1... | collective-permute-start | bytes 98312 | tf_op jit(solution)/shard_map/ppermute | solution.py:24
  19.9 14.1 %collective-permute-start.4 = (bf16[6,32,256]{2,1,0:T(8,128)(2,1)S(1)}, bf16[6,32,256]{2,1,0:T(8,128)(2,1)S(1)}, u32[]{:S(2)}, u32[]{:S(2)}) collective-permute-start(bf16[6,32,256]{2,1,0:T(8,128)(2,1)S(1)} %get-tuple-element.33.own_sides_ref), channel_id=1, source_target_pairs={{16,0},{32,16},{48,32},{64,48},{80,64},{96,80},{112,96},{128,112},... | collective-permute-start | bytes 294920 | tf_op jit(solution)/shard_map/ppermute | solution.py:24
  22.4 9.2 %collective-permute-start.2 = (bf16[10,16,256]{2,1,0:T(8,128)(2,1)S(1)}, bf16[10,16,256]{2,1,0:T(8,128)(2,1)S(1)}, u32[]{:S(2)}, u32[]{:S(2)}) collective-permute-start(bf16[10,16,256]{2,1,0:T(8,128)(2,1)S(1)} %shard_map.105), channel_id=1, source_target_pairs={{0,16},{16,32},{32,48},{48,64},{64,80},{80,96},{96,112},{112,128},... | collective-permute-start | bytes 245768 | tf_op jit(solution)/shard_map/ppermute | solution.py:24
  25.8 8.3 %collective-permute-start.5 = (bf16[8,16,256]{2,1,0:T(8,128)(2,1)S(1)}, bf16[8,16,256]{2,1,0:T(8,128)(2,1)S(1)}, u32[]{:S(2)}, u32[]{:S(2)}) collective-permute-start(bf16[8,16,256]{2,1,0:T(8,128)(2,1)S(1)} %get-tuple-element.35), channel_id=1, source_target_pairs={{32,0},{48,16},{64,32},{80,48},{96,64},{112,80},{128,96},{144,112}... | collective-permute-start | bytes 196616 | tf_op jit(solution)/shard_map/ppermute | solution.py:24
  31.5 0.7 copy-start.3
  32.2 0.7 copy-start.4
  32.9 0.7 copy-start.7
  43.7 34.0 %copy-start = (bf16[1,3,3,256,256]{4,3,2,1,0:T(8,128)(2,1)S(1)}, bf16[1,3,3,256,256]{4,3,2,1,0:T(8,128)(2,1)}, u32[]{:S(2)}) copy-start(bf16[1,3,3,256,256]{4,3,2,1,0:T(8,128)(2,1)} %param.14) | copy-start | bytes 3538948
  43.7 34.0 %copy-start.1 = (bf16[2,2,256,256]{3,2,1,0:T(8,128)(2,1)S(1)}, bf16[2,2,256,256]{3,2,1,0:T(8,128)(2,1)}, u32[]{:S(2)}) copy-start(bf16[2,2,256,256]{3,2,1,0:T(8,128)(2,1)} %param.16) | copy-start | bytes 1572868
  43.7 34.0 %copy-start.5 = (f32[1,256]{1,0:T(1,128)S(1)}, f32[1,256]{1,0:T(1,128)}, u32[]{:S(2)}) copy-start(f32[1,256]{1,0:T(1,128)} %bias_ref.1) | copy-start | bytes 3076
  43.7 34.0 %copy-start.6 = (f32[256]{0:T(256)S(1)}, f32[256]{0:T(256)}, u32[]{:S(2)}) copy-start(f32[256]{0:T(256)} %param.17) | copy-start | bytes 3076
  43.7 5.1 %collective-permute-start.6 = (bf16[8,200,256]{2,1,0:T(8,128)(2,1)S(1)}, bf16[8,200,256]{2,1,0:T(8,128)(2,1)S(1)}, u32[]{:S(2)}, u32[]{:S(2)}) collective-permute-start(bf16[8,200,256]{2,1,0:T(8,128)(2,1)S(1)} %get-tuple-element.39), channel_id=1, source_target_pairs={{0,1},{1,0},{2,3},{3,2},{4,5},{5,4},{6,7},{7,6},{8,9},{9,8},{10,11... | collective-permute-start | bytes 2457608 | tf_op jit(solution)/shard_map/ppermute | solution.py:400
  49.0 10.3 %collective-permute-start.7 = (bf16[3,200,256]{2,1,0:T(8,128)(2,1)S(1)}, bf16[3,200,256]{2,1,0:T(8,128)(2,1)S(1)}, u32[]{:S(2)}, u32[]{:S(2)}) collective-permute-start(bf16[3,200,256]{2,1,0:T(8,128)(2,1)S(1)} %add_convert_fusion), channel_id=1, source_target_pairs={{0,2},{1,15},{2,4},{3,1},{4,6},{5,3},{6,8},{7,5},{8,10},{9,7},{10,... | collective-permute-start | bytes 921608 | tf_op jit(solution)/shard_map/ppermute | solution.py:404
  51.4 7.9 %collective-permute-start.8 = (bf16[2,200,256]{2,1,0:T(8,128)(2,1)S(1)}, bf16[2,200,256]{2,1,0:T(8,128)(2,1)S(1)}, u32[]{:S(2)}, u32[]{:S(2)}) collective-permute-start(bf16[2,200,256]{2,1,0:T(8,128)(2,1)S(1)} %add_convert_fusion.1), channel_id=1, source_target_pairs={{0,14},{1,3},{2,0},{3,5},{4,2},{5,7},{6,4},{7,9},{8,6},{9,11},{10,... | collective-permute-start | bytes 614408 | tf_op jit(solution)/shard_map/ppermute | solution.py:404
  59.4 9.4 %collective-permute-start.10 = (bf16[200,256]{1,0:T(8,128)(2,1)S(1)}, bf16[200,256]{1,0:T(8,128)(2,1)S(1)}, u32[]{:S(2)}, u32[]{:S(2)}) collective-permute-start(bf16[200,256]{1,0:T(8,128)(2,1)S(1)} %get-tuple-element.40), channel_id=1, source_target_pairs={{0,12},{1,5},{2,14},{3,7},{4,0},{5,9},{6,2},{7,11},{8,4},{9,13},{1... | collective-permute-start | bytes 307208 | tf_op jit(solution)/shard_map/ppermute | solution.py:404
  66.5 11.1 %collective-permute-start.9 = (bf16[200,256]{1,0:T(8,128)(2,1)S(1)}, bf16[200,256]{1,0:T(8,128)(2,1)S(1)}, u32[]{:S(2)}, u32[]{:S(2)}) collective-permute-start(bf16[200,256]{1,0:T(8,128)(2,1)S(1)} %get-tuple-element.41), channel_id=1, source_target_pairs={{0,6},{1,11},{2,8},{3,13},{4,10},{5,15},{6,12},{7,1},{8,14},{9,3},... | collective-permute-start | bytes 307208 | tf_op jit(solution)/shard_map/ppermute | solution.py:404

commit v7 on v6

--- a/solution.py
+++ b/solution.py
@@ -332,7 +332,7 @@
 
 
 def head_kernel(
-    mine_ref, swapped_ref, ahead_ref, three_ref, two_ref,
+    mine_ref, swapped_ref, ahead_ref, two_ref, three_ref,
     weight_ref, bias_ref, lift_ref, shade_ref,
     out_ref, sum_ref, wide_ref, row_ref,
 ):
@@ -411,7 +411,7 @@
     back = send(total(mine[3:5], swapped[3:5]), -1)
     two = send(total(mine[6], swapped[6], ahead[2], back[1]), -2)
     three = send(total(mine[5], swapped[5], ahead[0], back[0]), 3)
-    parts = (mine, swapped, ahead, three, two)
+    parts = (mine, swapped, ahead, two, three)
     masks = head(parts, mask_weight, mask_bias, deconv_weight, deconv_bias)
     return tower, masks
 

time: 79.7 us -> 79.3 us (level)
  the two profiles are of different devices: /device:TPU:42 before, /device:TPU:6 now
where the time goes in v7:
time: 79.3 us; the launch traced here: 79.2 us
  starting transfers between devices  42 us (53%)
  waiting for transfers between devices  21.2 us (27%)
  Pallas kernels  11.8 us (15%)
  local copies, waits for them, and re-layouts  3.08 us (4%)
  between operations  0.82 us (1%)
    ppermute x6, starting transfers between devices, shift(): lax.ppermute(value, axis, [(i, i + step) for i in devices if i + step in...  22.3 us
    ppermute x4, starting transfers between devices, send(): lax.ppermute(value, 'col', [(i, (i + steps[i]) % peers) for i in range(pe...  17.6 us
    pallas_call x6, Pallas kernels, call(): pl.pallas_call(kernel, out_shape=out_shape, in_specs=in_specs, out_specs=...  11.8 us
    ppermute x4, waiting for transfers between devices, send(): lax.ppermute(value, 'col', [(i, (i + steps[i]) % peers) for i in range(pe...  11.3 us
    ppermute x6, waiting for transfers between devices, shift(): lax.ppermute(value, axis, [(i, i + step) for i in devices if i + step in...  7.69 us
    unnamed x16, local copies, waits for them, and re-layouts  3.08 us
    ppermute x1, starting transfers between devices, per_device(): swapped = lax.ppermute(other, 'col', [(i, i ^ 1) for i in range(peers)])  2.19 us
    ppermute x1, waiting for transfers between devices, per_device(): swapped = lax.ppermute(other, 'col', [(i, i ^ 1) for i in range(peers)])  2.16 us
  transfers between devices with their start and end apart: 11, of which 7 were waited for; matrix products, arithmetic and copies ran while one was open for 0% of the time, Pallas kernels for 0%

profile of v7, /device:TPU:6, one launch (start us, length us, event | category | flops | bytes accessed | tf_op | source)
XLA Modules:
  0.0 79.2 jit_solution(12624794204840173701)
XLA Ops:
  0.6 1.0 %copy-done.2 = bf16[32,32,256]{2,1,0:T(8,128)(2,1)S(1)} copy-done((bf16[32,32,256]{2,1,0:T(8,128)(2,1)S(1)}, bf16[32,32,256]{2,1,0:T(8,128)(2,1)}, u32[]{:S(2)}) %copy-start.2) | copy-done | bytes 524312
  1.7 0.1 shard_map.104
  1.8 11.2 %collective-permute-start.3 = (bf16[32,32,256]{2,1,0:T(8,128)(2,1)S(1)}, bf16[32,32,256]{2,1,0:T(8,128)(2,1)S(1)}, u32[]{:S(2)}, u32[]{:S(2)}) collective-permute-start(bf16[32,32,256]{2,1,0:T(8,128)(2,1)S(1)} %copy-done.2), channel_id=1, source_target_pairs={{16,0},{32,16},{48,32},{64,48},{80,64},{96,80},{112,96},{128,112},... | collective-permute-start | bytes 1572872 | tf_op jit(solution)/shard_map/ppermute | solution.py:24
  13.0 1.5 %collective-permute-start = (bf16[2,32,256]{2,1,0:T(8,128)(2,1)S(1)}, bf16[2,32,256]{2,1,0:T(8,128)(2,1)S(1)}, u32[]{:S(2)}, u32[]{:S(2)}) collective-permute-start(bf16[2,32,256]{2,1,0:T(8,128)(2,1)S(1)} %get-tuple-element.24.tail_ref), channel_id=1, source_target_pairs={{0,1},{1,2},{2,3},{3,4},{4,5},{5,6},{6,7},{7,8},{8,9},{9,10},{10,1... | collective-permute-start | bytes 98312 | tf_op jit(solution)/shard_map/ppermute | solution.py:24
  14.5 1.3 %collective-permute-start.1 = (bf16[2,32,256]{2,1,0:T(8,128)(2,1)S(1)}, bf16[2,32,256]{2,1,0:T(8,128)(2,1)S(1)}, u32[]{:S(2)}, u32[]{:S(2)}) collective-permute-start(bf16[2,32,256]{2,1,0:T(8,128)(2,1)S(1)} %get-tuple-element.25.lead_ref), channel_id=1, source_target_pairs={{1,0},{2,1},{3,2},{4,3},{5,4},{6,5},{7,6},{8,7},{9,8},{10,9},{11,1... | collective-permute-start | bytes 98312 | tf_op jit(solution)/shard_map/ppermute | solution.py:24
  15.8 3.4 %collective-permute-done.1.right_ref = bf16[2,32,256]{2,1,0:T(8,128)(2,1)S(1)} collective-permute-done((bf16[2,32,256]{2,1,0:T(8,128)(2,1)S(1)}, bf16[2,32,256]{2,1,0:T(8,128)(2,1)S(1)}, u32[]{:S(2)}, u32[]{:S(2)}) %collective-permute-start.1) | collective-permute-done | bytes 32800 | tf_op jit(solution)/shard_map/ppermute | solution.py:24
  19.3 2.5 %collective-permute-start.4 = (bf16[6,32,256]{2,1,0:T(8,128)(2,1)S(1)}, bf16[6,32,256]{2,1,0:T(8,128)(2,1)S(1)}, u32[]{:S(2)}, u32[]{:S(2)}) collective-permute-start(bf16[6,32,256]{2,1,0:T(8,128)(2,1)S(1)} %get-tuple-element.33.own_sides_ref), channel_id=1, source_target_pairs={{16,0},{32,16},{48,32},{64,48},{80,64},{96,80},{112,96},{128,112},... | collective-permute-start | bytes 294920 | tf_op jit(solution)/shard_map/ppermute | solution.py:24
  21.7 3.4 %collective-permute-start.2 = (bf16[10,16,256]{2,1,0:T(8,128)(2,1)S(1)}, bf16[10,16,256]{2,1,0:T(8,128)(2,1)S(1)}, u32[]{:S(2)}, u32[]{:S(2)}) collective-permute-start(bf16[10,16,256]{2,1,0:T(8,128)(2,1)S(1)} %shard_map.105), channel_id=1, source_target_pairs={{0,16},{16,32},{32,48},{48,64},{64,80},{80,96},{96,112},{112,128},... | collective-permute-start | bytes 245768 | tf_op jit(solution)/shard_map/ppermute | solution.py:24
  25.1 2.5 %collective-permute-start.5 = (bf16[8,16,256]{2,1,0:T(8,128)(2,1)S(1)}, bf16[8,16,256]{2,1,0:T(8,128)(2,1)S(1)}, u32[]{:S(2)}, u32[]{:S(2)}) collective-permute-start(bf16[8,16,256]{2,1,0:T(8,128)(2,1)S(1)} %get-tuple-element.35), channel_id=1, source_target_pairs={{32,0},{48,16},{64,32},{80,48},{96,64},{112,80},{128,96},{144,112}... | collective-permute-start | bytes 196616 | tf_op jit(solution)/shard_map/ppermute | solution.py:24
  27.6 2.6 %collective-permute-done.2.above_ref = bf16[10,16,256]{2,1,0:T(8,128)(2,1)S(1)} collective-permute-done((bf16[10,16,256]{2,1,0:T(8,128)(2,1)S(1)}, bf16[10,16,256]{2,1,0:T(8,128)(2,1)S(1)}, u32[]{:S(2)}, u32[]{:S(2)}) %collective-permute-start.2) | collective-permute-done | bytes 81952 | tf_op jit(solution)/shard_map/ppermute | solution.py:24
  30.2 0.7 copy-done.3
  30.9 0.7 copy-done.4
  31.6 0.7 copy-done.7
  32.2 1.7 %collective-permute-done.5.after_ref = bf16[8,16,256]{2,1,0:T(8,128)(2,1)S(1)} collective-permute-done((bf16[8,16,256]{2,1,0:T(8,128)(2,1)S(1)}, bf16[8,16,256]{2,1,0:T(8,128)(2,1)S(1)}, u32[]{:S(2)}, u32[]{:S(2)}) %collective-permute-start.5) | collective-permute-done | bytes 65568 | tf_op jit(solution)/shard_map/ppermute | solution.py:24
  33.9 9.9 %shard_map.108 = (bf16[32,32,256]{2,1,0:T(8,128)(2,1)}, bf16[8,200,256]{2,1,0:T(8,128)(2,1)S(1)}, bf16[8,200,256]{2,1,0:T(8,128)(2,1)S(1)}) custom-call(s32[4,16]{1,0:T(4,128)S(1)} %get-tuple-element.29.boxes_ref, s32[1,16]{1,0:T(1,128)S(1)} %get-tuple-element.30.owner_ref, bf16[32,32,256]{2,1,0:T(8,128)(2,1)S(1)} %get-tuple-element.31.own_ref, ...), custom_call_target="tpu_custom_call" | custom-call | flops 6000000000 | bytes 1000000 | tf_op jit(solution)/shard_map/pallas_call | solution.py:29
  43.8 0.0 copy-start
  43.8 0.0 copy-start.1
  43.8 0.0 copy-start.5
  43.9 0.0 copy-start.6
  43.9 2.2 %collective-permute-start.6 = (bf16[8,200,256]{2,1,0:T(8,128)(2,1)S(1)}, bf16[8,200,256]{2,1,0:T(8,128)(2,1)S(1)}, u32[]{:S(2)}, u32[]{:S(2)}) collective-permute-start(bf16[8,200,256]{2,1,0:T(8,128)(2,1)S(1)} %get-tuple-element.39), channel_id=1, source_target_pairs={{0,1},{1,0},{2,3},{3,2},{4,5},{5,4},{6,7},{7,6},{8,9},{9,8},{10,11... | collective-permute-start | bytes 2457608 | tf_op jit(solution)/shard_map/ppermute | solution.py:400
  46.1 2.2 %collective-permute-done.6.swapped_ref = bf16[8,200,256]{2,1,0:T(8,128)(2,1)S(1)} collective-permute-done((bf16[8,200,256]{2,1,0:T(8,128)(2,1)S(1)}, bf16[8,200,256]{2,1,0:T(8,128)(2,1)S(1)}, u32[]{:S(2)}, u32[]{:S(2)}) %collective-permute-start.6) | collective-permute-done | bytes 819232 | tf_op jit(solution)/shard_map/ppermute | solution.py:400
  48.2 0.1 add_convert_fusion
  48.3 5.0 %collective-permute-start.7 = (bf16[3,200,256]{2,1,0:T(8,128)(2,1)S(1)}, bf16[3,200,256]{2,1,0:T(8,128)(2,1)S(1)}, u32[]{:S(2)}, u32[]{:S(2)}) collective-permute-start(bf16[3,200,256]{2,1,0:T(8,128)(2,1)S(1)} %add_convert_fusion), channel_id=1, source_target_pairs={{0,2},{1,15},{2,4},{3,1},{4,6},{5,3},{6,8},{7,5},{8,10},{9,7},{10,... | collective-permute-start | bytes 921608 | tf_op jit(solution)/shard_map/ppermute | solution.py:404
  53.3 0.1 add_convert_fusion.1
  53.4 2.9 %collective-permute-start.8 = (bf16[2,200,256]{2,1,0:T(8,128)(2,1)S(1)}, bf16[2,200,256]{2,1,0:T(8,128)(2,1)S(1)}, u32[]{:S(2)}, u32[]{:S(2)}) collective-permute-start(bf16[2,200,256]{2,1,0:T(8,128)(2,1)S(1)} %add_convert_fusion.1), channel_id=1, source_target_pairs={{0,14},{1,3},{2,0},{3,5},{4,2},{5,7},{6,4},{7,9},{8,6},{9,11},{10,... | collective-permute-start | bytes 614408 | tf_op jit(solution)/shard_map/ppermute | solution.py:404
  56.3 4.7 %collective-permute-done.8 = bf16[2,200,256]{2,1,0:T(8,128)(2,1)S(1)} collective-permute-done((bf16[2,200,256]{2,1,0:T(8,128)(2,1)S(1)}, bf16[2,200,256]{2,1,0:T(8,128)(2,1)S(1)}, u32[]{:S(2)}, u32[]{:S(2)}) %collective-permute-start.8) | collective-permute-done | bytes 204832 | tf_op jit(solution)/shard_map/ppermute | solution.py:404
  61.0 0.1 fusion.1
  61.2 7.7 %collective-permute-start.10 = (bf16[200,256]{1,0:T(8,128)(2,1)S(1)}, bf16[200,256]{1,0:T(8,128)(2,1)S(1)}, u32[]{:S(2)}, u32[]{:S(2)}) collective-permute-start(bf16[200,256]{1,0:T(8,128)(2,1)S(1)} %get-tuple-element.40), channel_id=1, source_target_pairs={{0,6},{1,11},{2,8},{3,13},{4,10},{5,15},{6,12},{7,1},{8,14},{9,3},... | collective-permute-start | bytes 307208 | tf_op jit(solution)/shard_map/ppermute | solution.py:404
  68.9 1.9 %collective-permute-start.9 = (bf16[200,256]{1,0:T(8,128)(2,1)S(1)}, bf16[200,256]{1,0:T(8,128)(2,1)S(1)}, u32[]{:S(2)}, u32[]{:S(2)}) collective-permute-start(bf16[200,256]{1,0:T(8,128)(2,1)S(1)} %get-tuple-element.41), channel_id=1, source_target_pairs={{0,12},{1,5},{2,14},{3,7},{4,0},{5,9},{6,2},{7,11},{8,4},{9,13},{1... | collective-permute-start | bytes 307208 | tf_op jit(solution)/shard_map/ppermute | solution.py:404
  70.8 3.0 %collective-permute-done.10.three_ref = bf16[200,256]{1,0:T(8,128)(2,1)S(1)} collective-permute-done((bf16[200,256]{1,0:T(8,128)(2,1)S(1)}, bf16[200,256]{1,0:T(8,128)(2,1)S(1)}, u32[]{:S(2)}, u32[]{:S(2)}) %collective-permute-start.10) | collective-permute-done | bytes 102432 | tf_op jit(solution)/shard_map/ppermute | solution.py:404
  73.8 3.6 %collective-permute-done.9.two_ref = bf16[200,256]{1,0:T(8,128)(2,1)S(1)} collective-permute-done((bf16[200,256]{1,0:T(8,128)(2,1)S(1)}, bf16[200,256]{1,0:T(8,128)(2,1)S(1)}, u32[]{:S(2)}, u32[]{:S(2)}) %collective-permute-start.9) | collective-permute-done | bytes 102432 | tf_op jit(solution)/shard_map/ppermute | solution.py:404
  77.4 1.7 %shard_map.109 = bf16[1,28,28,256]{3,2,1,0:T(8,128)(2,1)} custom-call(bf16[8,200,256]{2,1,0:T(8,128)(2,1)S(1)} %get-tuple-element.38.mine_ref, bf16[8,200,256]{2,1,0:T(8,128)(2,1)S(1)} %collective-permute-done.6.swapped_ref, bf16[3,200,256]{2,1,0:T(8,128)(2,1)S(1)} %collective-permute-done.7.ahead_ref, bf16[200,256]{1,0:T(8,128)(2,1)S(1)} %collective-permute-done.9.two_ref, ...), custom_call_target="tpu_custom_call" | custom-call | flops 1000000000 | bytes 1000000 | tf_op jit(solution)/shard_map/pallas_call | solution.py:29
  (15 shorter events, 0.0 us)
Async XLA Ops:
  0.6 1.0 %copy-start.2 = (bf16[32,32,256]{2,1,0:T(8,128)(2,1)S(1)}, bf16[32,32,256]{2,1,0:T(8,128)(2,1)}, u32[]{:S(2)}) copy-start(bf16[32,32,256]{2,1,0:T(8,128)(2,1)} %tile_ref.1) | copy-start | bytes 1572868
  1.8 32.1 %collective-permute-start.3 = (bf16[32,32,256]{2,1,0:T(8,128)(2,1)S(1)}, bf16[32,32,256]{2,1,0:T(8,128)(2,1)S(1)}, u32[]{:S(2)}, u32[]{:S(2)}) collective-permute-start(bf16[32,32,256]{2,1,0:T(8,128)(2,1)S(1)} %copy-done.2), channel_id=1, source_target_pairs={{16,0},{32,16},{48,32},{64,48},{80,64},{96,80},{112,96},{128,112},... | collective-permute-start | bytes 1572872 | tf_op jit(solution)/shard_map/ppermute | solution.py:24
  13.0 2.8 %collective-permute-start = (bf16[2,32,256]{2,1,0:T(8,128)(2,1)S(1)}, bf16[2,32,256]{2,1,0:T(8,128)(2,1)S(1)}, u32[]{:S(2)}, u32[]{:S(2)}) collective-permute-start(bf16[2,32,256]{2,1,0:T(8,128)(2,1)S(1)} %get-tuple-element.24.tail_ref), channel_id=1, source_target_pairs={{0,1},{1,2},{2,3},{3,4},{4,5},{5,6},{6,7},{7,8},{8,9},{9,10},{10,1... | collective-permute-start | bytes 98312 | tf_op jit(solution)/shard_map/ppermute | solution.py:24
  14.5 4.7 %collective-permute-start.1 = (bf16[2,32,256]{2,1,0:T(8,128)(2,1)S(1)}, bf16[2,32,256]{2,1,0:T(8,128)(2,1)S(1)}, u32[]{:S(2)}, u32[]{:S(2)}) collective-permute-start(bf16[2,32,256]{2,1,0:T(8,128)(2,1)S(1)} %get-tuple-element.25.lead_ref), channel_id=1, source_target_pairs={{1,0},{2,1},{3,2},{4,3},{5,4},{6,5},{7,6},{8,7},{9,8},{10,9},{11,1... | collective-permute-start | bytes 98312 | tf_op jit(solution)/shard_map/ppermute | solution.py:24
  19.3 14.6 %collective-permute-start.4 = (bf16[6,32,256]{2,1,0:T(8,128)(2,1)S(1)}, bf16[6,32,256]{2,1,0:T(8,128)(2,1)S(1)}, u32[]{:S(2)}, u32[]{:S(2)}) collective-permute-start(bf16[6,32,256]{2,1,0:T(8,128)(2,1)S(1)} %get-tuple-element.33.own_sides_ref), channel_id=1, source_target_pairs={{16,0},{32,16},{48,32},{64,48},{80,64},{96,80},{112,96},{128,112},... | collective-permute-start | bytes 294920 | tf_op jit(solution)/shard_map/ppermute | solution.py:24
  21.7 8.4 %collective-permute-start.2 = (bf16[10,16,256]{2,1,0:T(8,128)(2,1)S(1)}, bf16[10,16,256]{2,1,0:T(8,128)(2,1)S(1)}, u32[]{:S(2)}, u32[]{:S(2)}) collective-permute-start(bf16[10,16,256]{2,1,0:T(8,128)(2,1)S(1)} %shard_map.105), channel_id=1, source_target_pairs={{0,16},{16,32},{32,48},{48,64},{64,80},{80,96},{96,112},{112,128},... | collective-permute-start | bytes 245768 | tf_op jit(solution)/shard_map/ppermute | solution.py:24
  25.1 8.7 %collective-permute-start.5 = (bf16[8,16,256]{2,1,0:T(8,128)(2,1)S(1)}, bf16[8,16,256]{2,1,0:T(8,128)(2,1)S(1)}, u32[]{:S(2)}, u32[]{:S(2)}) collective-permute-start(bf16[8,16,256]{2,1,0:T(8,128)(2,1)S(1)} %get-tuple-element.35), channel_id=1, source_target_pairs={{32,0},{48,16},{64,32},{80,48},{96,64},{112,80},{128,96},{144,112}... | collective-permute-start | bytes 196616 | tf_op jit(solution)/shard_map/ppermute | solution.py:24
  30.2 0.7 copy-start.3
  30.9 0.7 copy-start.4
  31.5 0.7 copy-start.7
  43.8 33.6 %copy-start = (bf16[1,3,3,256,256]{4,3,2,1,0:T(8,128)(2,1)S(1)}, bf16[1,3,3,256,256]{4,3,2,1,0:T(8,128)(2,1)}, u32[]{:S(2)}) copy-start(bf16[1,3,3,256,256]{4,3,2,1,0:T(8,128)(2,1)} %param.14) | copy-start | bytes 3538948
  43.8 33.6 %copy-start.1 = (bf16[2,2,256,256]{3,2,1,0:T(8,128)(2,1)S(1)}, bf16[2,2,256,256]{3,2,1,0:T(8,128)(2,1)}, u32[]{:S(2)}) copy-start(bf16[2,2,256,256]{3,2,1,0:T(8,128)(2,1)} %param.16) | copy-start | bytes 1572868
  43.8 33.6 %copy-start.5 = (f32[1,256]{1,0:T(1,128)S(1)}, f32[1,256]{1,0:T(1,128)}, u32[]{:S(2)}) copy-start(f32[1,256]{1,0:T(1,128)} %bias_ref.1) | copy-start | bytes 3076
  43.9 33.6 %copy-start.6 = (f32[256]{0:T(256)S(1)}, f32[256]{0:T(256)}, u32[]{:S(2)}) copy-start(f32[256]{0:T(256)} %param.17) | copy-start | bytes 3076
  43.9 4.4 %collective-permute-start.6 = (bf16[8,200,256]{2,1,0:T(8,128)(2,1)S(1)}, bf16[8,200,256]{2,1,0:T(8,128)(2,1)S(1)}, u32[]{:S(2)}, u32[]{:S(2)}) collective-permute-start(bf16[8,200,256]{2,1,0:T(8,128)(2,1)S(1)} %get-tuple-element.39), channel_id=1, source_target_pairs={{0,1},{1,0},{2,3},{3,2},{4,5},{5,4},{6,7},{7,6},{8,9},{9,8},{10,11... | collective-permute-start | bytes 2457608 | tf_op jit(solution)/shard_map/ppermute | solution.py:400
  48.3 12.7 %collective-permute-start.7 = (bf16[3,200,256]{2,1,0:T(8,128)(2,1)S(1)}, bf16[3,200,256]{2,1,0:T(8,128)(2,1)S(1)}, u32[]{:S(2)}, u32[]{:S(2)}) collective-permute-start(bf16[3,200,256]{2,1,0:T(8,128)(2,1)S(1)} %add_convert_fusion), channel_id=1, source_target_pairs={{0,2},{1,15},{2,4},{3,1},{4,6},{5,3},{6,8},{7,5},{8,10},{9,7},{10,... | collective-permute-start | bytes 921608 | tf_op jit(solution)/shard_map/ppermute | solution.py:404
  53.4 7.7 %collective-permute-start.8 = (bf16[2,200,256]{2,1,0:T(8,128)(2,1)S(1)}, bf16[2,200,256]{2,1,0:T(8,128)(2,1)S(1)}, u32[]{:S(2)}, u32[]{:S(2)}) collective-permute-start(bf16[2,200,256]{2,1,0:T(8,128)(2,1)S(1)} %add_convert_fusion.1), channel_id=1, source_target_pairs={{0,14},{1,3},{2,0},{3,5},{4,2},{5,7},{6,4},{7,9},{8,6},{9,11},{10,... | collective-permute-start | bytes 614408 | tf_op jit(solution)/shard_map/ppermute | solution.py:404
  61.2 12.7 %collective-permute-start.10 = (bf16[200,256]{1,0:T(8,128)(2,1)S(1)}, bf16[200,256]{1,0:T(8,128)(2,1)S(1)}, u32[]{:S(2)}, u32[]{:S(2)}) collective-permute-start(bf16[200,256]{1,0:T(8,128)(2,1)S(1)} %get-tuple-element.40), channel_id=1, source_target_pairs={{0,6},{1,11},{2,8},{3,13},{4,10},{5,15},{6,12},{7,1},{8,14},{9,3},... | collective-permute-start | bytes 307208 | tf_op jit(solution)/shard_map/ppermute | solution.py:404
  68.9 8.5 %collective-permute-start.9 = (bf16[200,256]{1,0:T(8,128)(2,1)S(1)}, bf16[200,256]{1,0:T(8,128)(2,1)S(1)}, u32[]{:S(2)}, u32[]{:S(2)}) collective-permute-start(bf16[200,256]{1,0:T(8,128)(2,1)S(1)} %get-tuple-element.41), channel_id=1, source_target_pairs={{0,12},{1,5},{2,14},{3,7},{4,0},{5,9},{6,2},{7,11},{8,4},{9,13},{1... | collective-permute-start | bytes 307208 | tf_op jit(solution)/shard_map/ppermute | solution.py:404

commit v8 on v7

--- a/solution.py
+++ b/solution.py
@@ -99,9 +99,7 @@
         down_kernel, (jax.ShapeDtypeStruct((2 * whole + 6, TILE, channels), BF16),),
         [vmem] * 5, [], 4, 10**5, *strips,
     )
-    above, small = lax.optimization_barrier((shift(to_down, "row", 1), small))
-    shapes = tuple(jax.ShapeDtypeStruct(value.shape, value.dtype) for value in small)
-    small = call(hold_kernel, shapes, [vmem] * len(small), [], 4, 10**5, *small)
+    above = shift(to_down, "row", 1)
     sides_shape = jax.ShapeDtypeStruct((6, rows, channels), BF16)
     up_shape = jax.ShapeDtypeStruct((whole + 6, TILE, channels), BF16)
     own_sides, to_up = call(
@@ -109,6 +107,9 @@
     )
     sides = shift(own_sides, "row", -1)
     after = shift(to_up, "row", -2)
+    small, _ = lax.optimization_barrier((small, (to_down, to_up)))
+    shapes = tuple(jax.ShapeDtypeStruct(value.shape, value.dtype) for value in small)
+    small = call(hold_kernel, shapes, [vmem] * len(small), [], 4, 10**5, *small)
     return below, own_sides, sides, above, after, held, small
 
 

time: 79.3 us -> 78.9 us (level)
  transfers between devices with their start and end apart: 11 -> 11, of which waited for: 7 -> 6; matrix products, arithmetic and copies ran while one was open for 0% -> 0% of each run, Pallas kernels for 0% -> 0%
where the time goes in v8:
time: 78.9 us; the launch traced here: 78.3 us
  starting transfers between devices  41.6 us (53%)
  waiting for transfers between devices  21.1 us (27%)
  Pallas kernels  11.5 us (15%)
  local copies, waits for them, and re-layouts  3.07 us (4%)
  between operations  0.83 us (1%)
    ppermute x6, starting transfers between devices, shift(): lax.ppermute(value, axis, [(i, i + step) for i in devices if i + step in...  22.3 us
    ppermute x4, starting transfers between devices, send(): lax.ppermute(value, 'col', [(i, (i + steps[i]) % peers) for i in range(pe...  16.8 us
    pallas_call x6, Pallas kernels, call(): pl.pallas_call(kernel, out_shape=out_shape, in_specs=in_specs, out_specs=...  11.5 us
    ppermute x4, waiting for transfers between devices, send(): lax.ppermute(value, 'col', [(i, (i + steps[i]) % peers) for i in range(pe...  11.4 us
    ppermute x6, waiting for transfers between devices, shift(): lax.ppermute(value, axis, [(i, i + step) for i in devices if i + step in...  7.69 us
    unnamed x16, local copies, waits for them, and re-layouts  3.07 us
    ppermute x1, starting transfers between devices, per_device(): swapped = lax.ppermute(other, 'col', [(i, i ^ 1) for i in range(peers)])  2.49 us
    ppermute x1, waiting for transfers between devices, per_device(): swapped = lax.ppermute(other, 'col', [(i, i ^ 1) for i in range(peers)])  1.94 us
  transfers between devices with their start and end apart: 11, of which 6 were waited for; matrix products, arithmetic and copies ran while one was open for 0% of the time, Pallas kernels for 0%

profile of v8, /device:TPU:6, one launch (start us, length us, event | category | flops | bytes accessed | tf_op | source)
XLA Modules:
  0.0 78.3 jit_solution(7544400522333632364)
XLA Ops:
  0.6 1.0 %copy-done.2 = bf16[32,32,256]{2,1,0:T(8,128)(2,1)S(1)} copy-done((bf16[32,32,256]{2,1,0:T(8,128)(2,1)S(1)}, bf16[32,32,256]{2,1,0:T(8,128)(2,1)}, u32[]{:S(2)}) %copy-start.2) | copy-done | bytes 524312
  1.7 0.1 shard_map.104
  1.8 11.2 %collective-permute-start.2 = (bf16[32,32,256]{2,1,0:T(8,128)(2,1)S(1)}, bf16[32,32,256]{2,1,0:T(8,128)(2,1)S(1)}, u32[]{:S(2)}, u32[]{:S(2)}) collective-permute-start(bf16[32,32,256]{2,1,0:T(8,128)(2,1)S(1)} %copy-done.2), channel_id=1, source_target_pairs={{16,0},{32,16},{48,32},{64,48},{80,64},{96,80},{112,96},{128,112},... | collective-permute-start | bytes 1572872 | tf_op jit(solution)/shard_map/ppermute | solution.py:24
  13.0 1.5 %collective-permute-start = (bf16[2,32,256]{2,1,0:T(8,128)(2,1)S(1)}, bf16[2,32,256]{2,1,0:T(8,128)(2,1)S(1)}, u32[]{:S(2)}, u32[]{:S(2)}) collective-permute-start(bf16[2,32,256]{2,1,0:T(8,128)(2,1)S(1)} %get-tuple-element.23.tail_ref), channel_id=1, source_target_pairs={{0,1},{1,2},{2,3},{3,4},{4,5},{5,6},{6,7},{7,8},{8,9},{9,10},{10,1... | collective-permute-start | bytes 98312 | tf_op jit(solution)/shard_map/ppermute | solution.py:24
  14.5 1.3 %collective-permute-start.1 = (bf16[2,32,256]{2,1,0:T(8,128)(2,1)S(1)}, bf16[2,32,256]{2,1,0:T(8,128)(2,1)S(1)}, u32[]{:S(2)}, u32[]{:S(2)}) collective-permute-start(bf16[2,32,256]{2,1,0:T(8,128)(2,1)S(1)} %get-tuple-element.24.lead_ref), channel_id=1, source_target_pairs={{1,0},{2,1},{3,2},{4,3},{5,4},{6,5},{7,6},{8,7},{9,8},{10,9},{11,1... | collective-permute-start | bytes 98312 | tf_op jit(solution)/shard_map/ppermute | solution.py:24
  15.8 3.4 %collective-permute-done.1.right_ref = bf16[2,32,256]{2,1,0:T(8,128)(2,1)S(1)} collective-permute-done((bf16[2,32,256]{2,1,0:T(8,128)(2,1)S(1)}, bf16[2,32,256]{2,1,0:T(8,128)(2,1)S(1)}, u32[]{:S(2)}, u32[]{:S(2)}) %collective-permute-start.1) | collective-permute-done | bytes 32800 | tf_op jit(solution)/shard_map/ppermute | solution.py:24
  19.3 2.5 %collective-permute-start.3 = (bf16[6,32,256]{2,1,0:T(8,128)(2,1)S(1)}, bf16[6,32,256]{2,1,0:T(8,128)(2,1)S(1)}, u32[]{:S(2)}, u32[]{:S(2)}) collective-permute-start(bf16[6,32,256]{2,1,0:T(8,128)(2,1)S(1)} %get-tuple-element.33.own_sides_ref), channel_id=1, source_target_pairs={{16,0},{32,16},{48,32},{64,48},{80,64},{96,80},{112,96},{128,112},... | collective-permute-start | bytes 294920 | tf_op jit(solution)/shard_map/ppermute | solution.py:24
  21.7 3.4 %collective-permute-start.4 = (bf16[10,16,256]{2,1,0:T(8,128)(2,1)S(1)}, bf16[10,16,256]{2,1,0:T(8,128)(2,1)S(1)}, u32[]{:S(2)}, u32[]{:S(2)}) collective-permute-start(bf16[10,16,256]{2,1,0:T(8,128)(2,1)S(1)} %shard_map.105), channel_id=1, source_target_pairs={{0,16},{16,32},{32,48},{48,64},{64,80},{80,96},{96,112},{112,128},... | collective-permute-start | bytes 245768 | tf_op jit(solution)/shard_map/ppermute | solution.py:24
  25.1 2.5 %collective-permute-start.5 = (bf16[8,16,256]{2,1,0:T(8,128)(2,1)S(1)}, bf16[8,16,256]{2,1,0:T(8,128)(2,1)S(1)}, u32[]{:S(2)}, u32[]{:S(2)}) collective-permute-start(bf16[8,16,256]{2,1,0:T(8,128)(2,1)S(1)} %get-tuple-element.25), channel_id=1, source_target_pairs={{32,0},{48,16},{64,32},{80,48},{96,64},{112,80},{128,96},{144,112}... | collective-permute-start | bytes 196616 | tf_op jit(solution)/shard_map/ppermute | solution.py:24
  27.6 0.0 copy-start.3
  27.6 0.7 copy-done.3
  28.3 0.7 copy-done.4
  29.0 0.7 copy-done.7
  29.6 4.3 %collective-permute-done.5.after_ref = bf16[8,16,256]{2,1,0:T(8,128)(2,1)S(1)} collective-permute-done((bf16[8,16,256]{2,1,0:T(8,128)(2,1)S(1)}, bf16[8,16,256]{2,1,0:T(8,128)(2,1)S(1)}, u32[]{:S(2)}, u32[]{:S(2)}) %collective-permute-start.5) | collective-permute-done | bytes 65568 | tf_op jit(solution)/shard_map/ppermute | solution.py:24
  33.9 9.6 %shard_map.108 = (bf16[32,32,256]{2,1,0:T(8,128)(2,1)}, bf16[8,200,256]{2,1,0:T(8,128)(2,1)S(1)}, bf16[8,200,256]{2,1,0:T(8,128)(2,1)S(1)}) custom-call(s32[4,16]{1,0:T(4,128)S(1)} %get-tuple-element.29.boxes_ref, s32[1,16]{1,0:T(1,128)S(1)} %get-tuple-element.30.owner_ref, bf16[32,32,256]{2,1,0:T(8,128)(2,1)S(1)} %get-tuple-element.31.own_ref, ...), custom_call_target="tpu_custom_call" | custom-call | flops 6000000000 | bytes 1000000 | tf_op jit(solution)/shard_map/pallas_call | solution.py:29
  43.5 0.0 copy-start
  43.5 0.0 copy-start.1
  43.6 0.0 copy-start.5
  43.6 0.0 copy-start.6
  43.6 2.5 %collective-permute-start.6 = (bf16[8,200,256]{2,1,0:T(8,128)(2,1)S(1)}, bf16[8,200,256]{2,1,0:T(8,128)(2,1)S(1)}, u32[]{:S(2)}, u32[]{:S(2)}) collective-permute-start(bf16[8,200,256]{2,1,0:T(8,128)(2,1)S(1)} %get-tuple-element.37), channel_id=1, source_target_pairs={{0,1},{1,0},{2,3},{3,2},{4,5},{5,4},{6,7},{7,6},{8,9},{9,8},{10,11... | collective-permute-start | bytes 2457608 | tf_op jit(solution)/shard_map/ppermute | solution.py:401
  46.1 1.9 %collective-permute-done.6.swapped_ref = bf16[8,200,256]{2,1,0:T(8,128)(2,1)S(1)} collective-permute-done((bf16[8,200,256]{2,1,0:T(8,128)(2,1)S(1)}, bf16[8,200,256]{2,1,0:T(8,128)(2,1)S(1)}, u32[]{:S(2)}, u32[]{:S(2)}) %collective-permute-start.6) | collective-permute-done | bytes 819232 | tf_op jit(solution)/shard_map/ppermute | solution.py:401
  48.0 0.1 add_convert_fusion
  48.1 5.2 %collective-permute-start.7 = (bf16[3,200,256]{2,1,0:T(8,128)(2,1)S(1)}, bf16[3,200,256]{2,1,0:T(8,128)(2,1)S(1)}, u32[]{:S(2)}, u32[]{:S(2)}) collective-permute-start(bf16[3,200,256]{2,1,0:T(8,128)(2,1)S(1)} %add_convert_fusion), channel_id=1, source_target_pairs={{0,2},{1,15},{2,4},{3,1},{4,6},{5,3},{6,8},{7,5},{8,10},{9,7},{10,... | collective-permute-start | bytes 921608 | tf_op jit(solution)/shard_map/ppermute | solution.py:405
  53.3 0.1 add_convert_fusion.1
  53.4 1.9 %collective-permute-start.8 = (bf16[2,200,256]{2,1,0:T(8,128)(2,1)S(1)}, bf16[2,200,256]{2,1,0:T(8,128)(2,1)S(1)}, u32[]{:S(2)}, u32[]{:S(2)}) collective-permute-start(bf16[2,200,256]{2,1,0:T(8,128)(2,1)S(1)} %add_convert_fusion.1), channel_id=1, source_target_pairs={{0,14},{1,3},{2,0},{3,5},{4,2},{5,7},{6,4},{7,9},{8,6},{9,11},{10,... | collective-permute-start | bytes 614408 | tf_op jit(solution)/shard_map/ppermute | solution.py:405
  55.3 5.7 %collective-permute-done.8 = bf16[2,200,256]{2,1,0:T(8,128)(2,1)S(1)} collective-permute-done((bf16[2,200,256]{2,1,0:T(8,128)(2,1)S(1)}, bf16[2,200,256]{2,1,0:T(8,128)(2,1)S(1)}, u32[]{:S(2)}, u32[]{:S(2)}) %collective-permute-start.8) | collective-permute-done | bytes 204832 | tf_op jit(solution)/shard_map/ppermute | solution.py:405
  61.0 0.1 fusion.1
  61.2 7.7 %collective-permute-start.10 = (bf16[200,256]{1,0:T(8,128)(2,1)S(1)}, bf16[200,256]{1,0:T(8,128)(2,1)S(1)}, u32[]{:S(2)}, u32[]{:S(2)}) collective-permute-start(bf16[200,256]{1,0:T(8,128)(2,1)S(1)} %get-tuple-element.38), channel_id=1, source_target_pairs={{0,6},{1,11},{2,8},{3,13},{4,10},{5,15},{6,12},{7,1},{8,14},{9,3},... | collective-permute-start | bytes 307208 | tf_op jit(solution)/shard_map/ppermute | solution.py:405
  68.9 1.9 %collective-permute-start.9 = (bf16[200,256]{1,0:T(8,128)(2,1)S(1)}, bf16[200,256]{1,0:T(8,128)(2,1)S(1)}, u32[]{:S(2)}, u32[]{:S(2)}) collective-permute-start(bf16[200,256]{1,0:T(8,128)(2,1)S(1)} %get-tuple-element.39), channel_id=1, source_target_pairs={{0,12},{1,5},{2,14},{3,7},{4,0},{5,9},{6,2},{7,11},{8,4},{9,13},{1... | collective-permute-start | bytes 307208 | tf_op jit(solution)/shard_map/ppermute | solution.py:405
  70.8 2.6 %collective-permute-done.10.three_ref = bf16[200,256]{1,0:T(8,128)(2,1)S(1)} collective-permute-done((bf16[200,256]{1,0:T(8,128)(2,1)S(1)}, bf16[200,256]{1,0:T(8,128)(2,1)S(1)}, u32[]{:S(2)}, u32[]{:S(2)}) %collective-permute-start.10) | collective-permute-done | bytes 102432 | tf_op jit(solution)/shard_map/ppermute | solution.py:405
  73.4 3.1 %collective-permute-done.9.two_ref = bf16[200,256]{1,0:T(8,128)(2,1)S(1)} collective-permute-done((bf16[200,256]{1,0:T(8,128)(2,1)S(1)}, bf16[200,256]{1,0:T(8,128)(2,1)S(1)}, u32[]{:S(2)}, u32[]{:S(2)}) %collective-permute-start.9) | collective-permute-done | bytes 102432 | tf_op jit(solution)/shard_map/ppermute | solution.py:405
  76.6 1.7 %shard_map.109 = bf16[1,28,28,256]{3,2,1,0:T(8,128)(2,1)} custom-call(bf16[8,200,256]{2,1,0:T(8,128)(2,1)S(1)} %get-tuple-element.36.mine_ref, bf16[8,200,256]{2,1,0:T(8,128)(2,1)S(1)} %collective-permute-done.6.swapped_ref, bf16[3,200,256]{2,1,0:T(8,128)(2,1)S(1)} %collective-permute-done.7.ahead_ref, bf16[200,256]{1,0:T(8,128)(2,1)S(1)} %collective-permute-done.9.two_ref, ...), custom_call_target="tpu_custom_call" | custom-call | flops 1000000000 | bytes 1000000 | tf_op jit(solution)/shard_map/pallas_call | solution.py:29
  (15 shorter events, 0.0 us)
Async XLA Ops:
  0.6 1.0 %copy-start.2 = (bf16[32,32,256]{2,1,0:T(8,128)(2,1)S(1)}, bf16[32,32,256]{2,1,0:T(8,128)(2,1)}, u32[]{:S(2)}) copy-start(bf16[32,32,256]{2,1,0:T(8,128)(2,1)} %tile_ref.1) | copy-start | bytes 1572868
  1.8 32.1 %collective-permute-start.2 = (bf16[32,32,256]{2,1,0:T(8,128)(2,1)S(1)}, bf16[32,32,256]{2,1,0:T(8,128)(2,1)S(1)}, u32[]{:S(2)}, u32[]{:S(2)}) collective-permute-start(bf16[32,32,256]{2,1,0:T(8,128)(2,1)S(1)} %copy-done.2), channel_id=1, source_target_pairs={{16,0},{32,16},{48,32},{64,48},{80,64},{96,80},{112,96},{128,112},... | collective-permute-start | bytes 1572872 | tf_op jit(solution)/shard_map/ppermute | solution.py:24
  13.0 2.8 %collective-permute-start = (bf16[2,32,256]{2,1,0:T(8,128)(2,1)S(1)}, bf16[2,32,256]{2,1,0:T(8,128)(2,1)S(1)}, u32[]{:S(2)}, u32[]{:S(2)}) collective-permute-start(bf16[2,32,256]{2,1,0:T(8,128)(2,1)S(1)} %get-tuple-element.23.tail_ref), channel_id=1, source_target_pairs={{0,1},{1,2},{2,3},{3,4},{4,5},{5,6},{6,7},{7,8},{8,9},{9,10},{10,1... | collective-permute-start | bytes 98312 | tf_op jit(solution)/shard_map/ppermute | solution.py:24
  14.5 4.7 %collective-permute-start.1 = (bf16[2,32,256]{2,1,0:T(8,128)(2,1)S(1)}, bf16[2,32,256]{2,1,0:T(8,128)(2,1)S(1)}, u32[]{:S(2)}, u32[]{:S(2)}) collective-permute-start(bf16[2,32,256]{2,1,0:T(8,128)(2,1)S(1)} %get-tuple-element.24.lead_ref), channel_id=1, source_target_pairs={{1,0},{2,1},{3,2},{4,3},{5,4},{6,5},{7,6},{8,7},{9,8},{10,9},{11,1... | collective-permute-start | bytes 98312 | tf_op jit(solution)/shard_map/ppermute | solution.py:24
  19.3 14.6 %collective-permute-start.3 = (bf16[6,32,256]{2,1,0:T(8,128)(2,1)S(1)}, bf16[6,32,256]{2,1,0:T(8,128)(2,1)S(1)}, u32[]{:S(2)}, u32[]{:S(2)}) collective-permute-start(bf16[6,32,256]{2,1,0:T(8,128)(2,1)S(1)} %get-tuple-element.33.own_sides_ref), channel_id=1, source_target_pairs={{16,0},{32,16},{48,32},{64,48},{80,64},{96,80},{112,96},{128,112},... | collective-permute-start | bytes 294920 | tf_op jit(solution)/shard_map/ppermute | solution.py:24
  21.7 12.1 %collective-permute-start.4 = (bf16[10,16,256]{2,1,0:T(8,128)(2,1)S(1)}, bf16[10,16,256]{2,1,0:T(8,128)(2,1)S(1)}, u32[]{:S(2)}, u32[]{:S(2)}) collective-permute-start(bf16[10,16,256]{2,1,0:T(8,128)(2,1)S(1)} %shard_map.105), channel_id=1, source_target_pairs={{0,16},{16,32},{32,48},{48,64},{64,80},{80,96},{96,112},{112,128},... | collective-permute-start | bytes 245768 | tf_op jit(solution)/shard_map/ppermute | solution.py:24
  25.1 8.7 %collective-permute-start.5 = (bf16[8,16,256]{2,1,0:T(8,128)(2,1)S(1)}, bf16[8,16,256]{2,1,0:T(8,128)(2,1)S(1)}, u32[]{:S(2)}, u32[]{:S(2)}) collective-permute-start(bf16[8,16,256]{2,1,0:T(8,128)(2,1)S(1)} %get-tuple-element.25), channel_id=1, source_target_pairs={{32,0},{48,16},{64,32},{80,48},{96,64},{112,80},{128,96},{144,112}... | collective-permute-start | bytes 196616 | tf_op jit(solution)/shard_map/ppermute | solution.py:24
  27.6 0.7 copy-start.3
  28.3 0.7 copy-start.4
  29.0 0.7 copy-start.7
  43.5 33.0 %copy-start = (bf16[1,3,3,256,256]{4,3,2,1,0:T(8,128)(2,1)S(1)}, bf16[1,3,3,256,256]{4,3,2,1,0:T(8,128)(2,1)}, u32[]{:S(2)}) copy-start(bf16[1,3,3,256,256]{4,3,2,1,0:T(8,128)(2,1)} %param.14) | copy-start | bytes 3538948
  43.5 33.0 %copy-start.1 = (bf16[2,2,256,256]{3,2,1,0:T(8,128)(2,1)S(1)}, bf16[2,2,256,256]{3,2,1,0:T(8,128)(2,1)}, u32[]{:S(2)}) copy-start(bf16[2,2,256,256]{3,2,1,0:T(8,128)(2,1)} %param.16) | copy-start | bytes 1572868
  43.6 33.0 %copy-start.5 = (f32[1,256]{1,0:T(1,128)S(1)}, f32[1,256]{1,0:T(1,128)}, u32[]{:S(2)}) copy-start(f32[1,256]{1,0:T(1,128)} %bias_ref.1) | copy-start | bytes 3076
  43.6 33.0 %copy-start.6 = (f32[256]{0:T(256)S(1)}, f32[256]{0:T(256)}, u32[]{:S(2)}) copy-start(f32[256]{0:T(256)} %param.17) | copy-start | bytes 3076
  43.6 4.4 %collective-permute-start.6 = (bf16[8,200,256]{2,1,0:T(8,128)(2,1)S(1)}, bf16[8,200,256]{2,1,0:T(8,128)(2,1)S(1)}, u32[]{:S(2)}, u32[]{:S(2)}) collective-permute-start(bf16[8,200,256]{2,1,0:T(8,128)(2,1)S(1)} %get-tuple-element.37), channel_id=1, source_target_pairs={{0,1},{1,0},{2,3},{3,2},{4,5},{5,4},{6,7},{7,6},{8,9},{9,8},{10,11... | collective-permute-start | bytes 2457608 | tf_op jit(solution)/shard_map/ppermute | solution.py:401
  48.1 12.9 %collective-permute-start.7 = (bf16[3,200,256]{2,1,0:T(8,128)(2,1)S(1)}, bf16[3,200,256]{2,1,0:T(8,128)(2,1)S(1)}, u32[]{:S(2)}, u32[]{:S(2)}) collective-permute-start(bf16[3,200,256]{2,1,0:T(8,128)(2,1)S(1)} %add_convert_fusion), channel_id=1, source_target_pairs={{0,2},{1,15},{2,4},{3,1},{4,6},{5,3},{6,8},{7,5},{8,10},{9,7},{10,... | collective-permute-start | bytes 921608 | tf_op jit(solution)/shard_map/ppermute | solution.py:405
  53.4 7.7 %collective-permute-start.8 = (bf16[2,200,256]{2,1,0:T(8,128)(2,1)S(1)}, bf16[2,200,256]{2,1,0:T(8,128)(2,1)S(1)}, u32[]{:S(2)}, u32[]{:S(2)}) collective-permute-start(bf16[2,200,256]{2,1,0:T(8,128)(2,1)S(1)} %add_convert_fusion.1), channel_id=1, source_target_pairs={{0,14},{1,3},{2,0},{3,5},{4,2},{5,7},{6,4},{7,9},{8,6},{9,11},{10,... | collective-permute-start | bytes 614408 | tf_op jit(solution)/shard_map/ppermute | solution.py:405
  61.2 12.2 %collective-permute-start.10 = (bf16[200,256]{1,0:T(8,128)(2,1)S(1)}, bf16[200,256]{1,0:T(8,128)(2,1)S(1)}, u32[]{:S(2)}, u32[]{:S(2)}) collective-permute-start(bf16[200,256]{1,0:T(8,128)(2,1)S(1)} %get-tuple-element.38), channel_id=1, source_target_pairs={{0,6},{1,11},{2,8},{3,13},{4,10},{5,15},{6,12},{7,1},{8,14},{9,3},... | collective-permute-start | bytes 307208 | tf_op jit(solution)/shard_map/ppermute | solution.py:405
  68.9 7.6 %collective-permute-start.9 = (bf16[200,256]{1,0:T(8,128)(2,1)S(1)}, bf16[200,256]{1,0:T(8,128)(2,1)S(1)}, u32[]{:S(2)}, u32[]{:S(2)}) collective-permute-start(bf16[200,256]{1,0:T(8,128)(2,1)S(1)} %get-tuple-element.39), channel_id=1, source_target_pairs={{0,12},{1,5},{2,14},{3,7},{4,0},{5,9},{6,2},{7,11},{8,4},{9,13},{1... | collective-permute-start | bytes 307208 | tf_op jit(solution)/shard_map/ppermute | solution.py:405
